TPU v7x, 32 devices: a whole 2x2x4 slice. The times are simulated.
32 devices in a mesh: groups: 2 (over y), det: 4 (over z), wafer: 2 (over x), rep: 2 (over core).
Axes of the slice: x: 2, y: 2, z: 4, core: 2. Of those that a mesh axis runs over, the one named last changes fastest.
Arguments:
- tod: float32 [4, 32, 4096], P(('groups', 'wafer'), 'det', 'rep'), parts along dimension 0, may hold values from -6 to 6
- psi: float32 [4, 32, 4096], P(('groups', 'wafer'), 'det', 'rep'), parts along dimension 0, may hold values from -3.140625 to 3.140625
- point_row: int32 [4, 32, 32], P(('groups', 'wafer'), 'det', 'rep'), parts along dimension 0, may hold values from 0 to 24575
- hit_list: int32 [4, 4, 2, 8, 32], P(('groups', 'wafer'), 'det', 'rep'), parts along dimension 0, may hold values from 0 to 128, as said below
- group_id: int32 [4, 32], P(('groups', 'wafer'), 'det'), parts along dimension 0, may hold values from 0 to 3, as said below
- a_zero: float32 [4, 32], P(('groups', 'wafer'), 'det'), parts along dimension 0, may hold values from 2 to 8
- band_coef: float32 [4, 32, 4], P(('groups', 'wafer'), 'det'), parts along dimension 0, may hold values from -0.2 to 0.2
- band_lag: int32 [4, 32, 4], P(('groups', 'wafer'), 'det'), parts along dimension 0, may hold values from 1 to 16
Outputs:
- solution: float32 [393216, 192], P(('groups', 'det', 'wafer')), parts along dimension 0
- residual: float32 [393216, 192], P(('groups', 'det', 'wafer')), parts along dimension 0
There are 2 independent parts, one for each index of `groups`. A program takes and returns all parts, laid end to end along the dimension named above; each array names one. Nothing has to cross between parts.
Inputs may be any that keep to these rules, and one draw needn't show every extreme that they name: `hit_list`: every sample block of a device (numbers 0 to 127) stands exactly once in that device's table; unused entries hold 128. In every draw some owner receives 32 blocks from every device. `group_id`: in every draw one readout group of some wafer has no detector.
All inputs are finite; a program needn't handle non-finite values.
Results may differ from a plain program's by a relative error of at most 0.0003.
Values sent between devices are 32-bit elements; how exact they have to be, the bound alone decides.
No kernel may reach another device: no remote copies, remote signals or barrier semaphores. Data moves between devices by JAX's collectives and lax.ppermute only.
A program may use at most 448 MiB of HBM per device.

v0:
```python
import functools

import jax
import jax.numpy as jnp
from jax import lax
from jax.experimental import pallas as pl
from jax.experimental.pallas import tpu as pltpu
from jax.sharding import PartitionSpec as P

BLOCKS = 196608
PBLOCK = 64
SBLOCK = 128
NSUB = 4
LAG = 16
ITERS = 3


prior_weight = 1.0


def with_halo(block, sides, width):
    for axis, dim in sides:
        count = lax.axis_size(axis)
        forward = [(i, i + 1) for i in range(count - 1)]
        backward = [(target, source) for source, target in forward]
        low = lax.ppermute(
            lax.slice_in_dim(block, block.shape[dim] - width, None, axis=dim), axis, forward
        )
        high = lax.ppermute(lax.slice_in_dim(block, 0, width, axis=dim), axis, backward)
        block = jnp.concatenate([low, block, high], axis=dim)
    return block


def distributed(tod, psi, point_row, hit_list, group_id, a_zero, band_coef, band_lag):
    highest = lax.Precision.HIGHEST
    samples = tod[0]
    angles = psi[0]
    det_count, time_count = samples.shape
    time_blocks = time_count // SBLOCK
    block_count = det_count * time_blocks
    send_table = hit_list[0, 0, 0]
    owner_count, capacity = send_table.shape
    owner_rows = BLOCKS // owner_count
    block_width = 3 * PBLOCK
    detector = lax.axis_index("det") * det_count + jnp.arange(det_count, dtype=jnp.int32)
    within = (jnp.arange(SBLOCK, dtype=jnp.int32)[None, :] + 3 * detector[:, None]) % PBLOCK
    pixel_table = (within[:, :, None] == jnp.arange(PBLOCK, dtype=jnp.int32)[None, None, :]).astype(
        jnp.float32
    )
    cosine_two = jnp.cos(2.0 * angles).reshape(det_count, time_blocks, SBLOCK)
    sine_two = jnp.sin(2.0 * angles).reshape(det_count, time_blocks, SBLOCK)
    slot_ids = send_table.reshape(-1)
    row_source = jnp.concatenate([point_row[0].reshape(-1), jnp.zeros((1,), jnp.int32)])
    slot_rows = row_source[slot_ids].astype(jnp.float32).reshape(owner_count, capacity)
    member = (group_id[0][:, None] == jnp.arange(NSUB, dtype=jnp.int32)[None, :]).astype(
        jnp.float32
    )
    member_count = jnp.sum(member, axis=0)
    lag_table = (
        band_lag[0][:, :, None] == jnp.arange(1, LAG + 1, dtype=jnp.int32)[None, None, :]
    ).astype(jnp.float32)
    lag_weight = jnp.einsum("dj,djl->dl", band_coef[0], lag_table, precision=highest)
    base_weight = a_zero[0]

    def slot_payload(by_block):
        width = by_block.shape[1]
        extended = jnp.concatenate([by_block, jnp.zeros((1, width), by_block.dtype)])
        return extended[slot_ids].reshape(owner_count, capacity, width)

    def deliver(payload):
        width = payload.shape[-1]
        got_values, got_rows = (
            lax.all_to_all(payload, ("det", "wafer"), split_axis=0, concat_axis=0, tiled=True),
            lax.all_to_all(slot_rows, ("det", "wafer"), split_axis=0, concat_axis=0, tiled=True),
        )
        return (got_values, got_rows)

    def back_project(stream, squared):
        shaped = stream.reshape(det_count, time_blocks, SBLOCK)
        first = cosine_two * cosine_two if squared else cosine_two
        second = sine_two * sine_two if squared else sine_two
        stacked = jnp.stack([shaped, first * shaped, second * shaped], axis=2)
        stokes = jnp.einsum("dkcs,dsp->dkcp", stacked, pixel_table, precision=highest)
        return stokes.reshape(block_count, block_width)

    def to_owners(stream, squared):
        got_values, got_rows = deliver(slot_payload(back_project(stream, squared)))
        pair_values, pair_rows = (
            lax.all_gather(got_values, "rep", axis=0, tiled=True),
            lax.all_gather(got_rows, "rep", axis=0, tiled=True),
        )
        target_rows = pair_rows.reshape(-1).astype(jnp.int32)
        summed = (
            jnp.zeros((owner_rows, block_width), jnp.float32)
            .at[target_rows]
            .add(pair_values.reshape(-1, block_width))
        )
        return (summed, got_rows.astype(jnp.int32))

    def remove_common(stream):
        local_sums = jnp.einsum("dg,dt->gt", member, stream, precision=highest)
        group_sums, group_counts = lax.psum((local_sums, member_count), "det")
        group_means = group_sums / jnp.maximum(group_counts, 1.0)[:, None]
        return stream - jnp.einsum("dg,gt->dt", member, group_means, precision=highest)

    def band_filter(stream):
        padded = with_halo(stream, (("rep", 1),), LAG)
        result = base_weight[:, None] * stream
        for offset in range(1, LAG + 1):
            later = padded[:, LAG + offset : LAG + offset + time_count]
            earlier = padded[:, LAG - offset : LAG - offset + time_count]
            result = result + lag_weight[:, offset - 1 : offset] * (later + earlier)
        return result

    def weigh_stream(stream):
        return remove_common(band_filter(remove_common(stream)))

    weight_stream = jnp.broadcast_to(base_weight[:, None], (det_count, time_count))
    diag_sum, serve_rows = to_owners(weight_stream, True)
    inverse_diag = 1.0 / (diag_sum + prior_weight)
    right_side = to_owners(weigh_stream(samples), False)[0]
    solution = jnp.zeros_like(right_side)
    residual = right_side

    def inner(left_map, right_map):
        return lax.psum(jnp.sum(left_map * right_map), ("det", "wafer"))

    precond = inverse_diag * residual
    direction = precond
    energy = inner(residual, precond)
    for iteration in range(ITERS):
        from_blocks = direction[serve_rows.reshape(-1)].reshape(owner_count, capacity, block_width)
        return_width = from_blocks.shape[-1]
        returned = lax.all_to_all(
            from_blocks, ("det", "wafer"), split_axis=0, concat_axis=0, tiled=True
        )
        return_placed = jnp.zeros((block_count + 1, return_width), jnp.float32)
        return_placed = return_placed.at[slot_ids].set(returned.reshape(-1, return_width))
        blocks = return_placed[:block_count].reshape(det_count, time_blocks, 3, PBLOCK)
        project_stokes = jnp.einsum("dkcp,dsp->dkcs", blocks, pixel_table, precision=highest)
        project_stream = (
            project_stokes[:, :, 0]
            + cosine_two * project_stokes[:, :, 1]
            + sine_two * project_stokes[:, :, 2]
        )
        seen_stream = project_stream.reshape(det_count, time_count)
        image_map = to_owners(weigh_stream(seen_stream), False)[0] + prior_weight * direction
        step_size = energy / inner(direction, image_map)
        solution = solution + step_size * direction
        residual = residual - step_size * image_map
        precond = inverse_diag * residual
        energy_next = inner(residual, precond)
        direction = precond + energy_next / energy * direction
        energy = energy_next
    return (solution, residual)


LANES = 128
ROWS = 8
OUT_TILES = 8
PAIR_BATCH = 4
BIG = float(1 << 24)
VMEM_BYTES = 60 << 20


def wide(values):
    return jnp.broadcast_to(values, (ROWS, LANES))


def tile_iotas():
    lane = lax.broadcasted_iota(jnp.int32, (ROWS, LANES), 1)
    sub = lax.broadcasted_iota(jnp.int32, (ROWS, LANES), 0)
    return lane, sub


def cosine_sine_double(angle):
    turns = jnp.floor(angle * 1.2732395447351628 + 0.5)
    reduced = 2.0 * angle - turns * 1.5703125
    reduced = reduced - turns * 4.837512969970703125e-4
    reduced = reduced - turns * 7.54978995489188216e-8
    square = reduced * reduced
    sine = (-1.9515295891e-4 * square + 8.3321608736e-3) * square - 1.6666654611e-1
    sine = sine * square * reduced + reduced
    cosine = (2.443315711809948e-5 * square - 1.388731625493765e-3) * square
    cosine = (cosine + 4.166664568298827e-2) * square * square - 0.5 * square + 1.0
    quarter = turns.astype(jnp.int32)
    odd = (quarter & 1) == 1
    first = jnp.where(odd, sine, cosine)
    second = jnp.where(odd, cosine, sine)
    first = jnp.where(((quarter + 1) & 2) == 2, -first, first)
    second = jnp.where((quarter & 2) == 2, -second, second)
    return first, second


def pack_kernel(
    shape, angle_ref, tod_ref, row_ref, hit_ref, group_ref, base_ref, coef_ref, lag_ref,
    table_ref, angle_rows_ref, tod_rows_ref,
):
    wafers, dets, reps, tiles, owners, capacity, owner_rows, lag_count = shape
    lane, sub = tile_iotas()
    lists = hit_ref[...]
    owner_hits = jnp.zeros((ROWS, LANES), jnp.float32)
    for c in range(capacity):
        owner_hits = owner_hits + jnp.where(wide(lists[:, c : c + 1]) == lane, 1.0, 0.0)
    owner_of = jnp.sum(owner_hits * sub.astype(jnp.float32), axis=0, keepdims=True)

    def spread(values, width):
        return jnp.concatenate(
            [values, jnp.zeros((values.shape[0], LANES - width), values.dtype)], axis=1
        )

    rows = spread(row_ref[...].astype(jnp.float32), tiles)
    ids = owner_of * float(owner_rows) + rows[0:1]
    for k in range(1, ROWS):
        ids = ids + pltpu.roll(rows[k : k + 1], k * tiles, 1)
    floats = spread(base_ref[...], ROWS)
    whole = spread(group_ref[...].astype(jnp.float32), ROWS)
    for j in range(lag_count):
        at = (j + 1) * ROWS
        floats = floats + pltpu.roll(spread(coef_ref[j : j + 1, :], ROWS), at, 1)
        lag = lag_ref[j : j + 1, :].astype(jnp.float32)
        whole = whole + pltpu.roll(spread(lag, ROWS), at, 1)
    table = jnp.where(sub == 0, wide(ids), jnp.where(sub == 1, wide(floats), wide(whole)))
    table_ref[:, 0:LANES] = table
    table_ref[:, LANES : 2 * LANES] = spread(lists.astype(jnp.float32), capacity)
    for b in range(tiles):
        angle_rows_ref[:, b, :] = angle_ref[:, b * LANES : (b + 1) * LANES]
        tod_rows_ref[:, b, :] = tod_ref[:, b * LANES : (b + 1) * LANES]


def part_copies(shape, self_ref, refs, target, sem):
    wafers, dets, reps = shape[:3]
    here_ref, across_ref, other_ref = refs
    copies = []
    for swap_rep in range(reps):
        for swap_wafer in range(wafers):
            for shift in range(dets):
                if swap_rep:
                    source = other_ref.at[swap_wafer, shift]
                else:
                    source = (across_ref if swap_wafer else here_ref).at[shift]
                wafer = self_ref[0] ^ swap_wafer
                det = self_ref[1] - shift
                det = jnp.where(det < 0, det + dets, det)
                device = (wafer * dets + det) * reps + (self_ref[2] ^ swap_rep)
                copies.append(
                    pltpu.make_async_copy(source, target(device), sem.at[len(copies)])
                )
    return copies


def table_copies(shape, self_ref, refs, part_ref, sem):
    wafers, dets, reps = shape[:3]
    chips = wafers * dets
    here = self_ref[1] * wafers + self_ref[0]
    copies = []
    for shift, ref in enumerate(refs):
        chip = here - shift
        chip = jnp.where(chip < 0, chip + chips, chip)
        team = lax.rem(chip, wafers) * dets + lax.div(chip, wafers)
        to = part_ref.at[pl.ds(team * reps, reps)]
        copies.append(pltpu.make_async_copy(ref, to, sem.at[shift]))
    for copy in copies:
        copy.start()
    for copy in copies:
        copy.wait()


def exact_dot(left, right, dims=((1,), (0,))):
    return lax.dot_general(
        left.astype(jnp.bfloat16), right.astype(jnp.bfloat16), (dims, ((), ())),
        preferred_element_type=jnp.float32,
    )


def twin_kernel(shape, self_ref, *refs):
    wafers, dets, reps, tiles, owners, capacity, owner_rows, lag_count = shape
    devices = wafers * dets * reps
    total = devices * LANES
    table_refs, refs = refs[: wafers * dets], refs[wafers * dets :]
    weight_ref, float_ref, whole_ref, size_ref, pair_ref, group_ref = refs[:6]
    part_ref, code_ref, lead_ref, part_sem = refs[6:]
    lane, sub = tile_iotas()
    lane_f = lane.astype(jnp.float32)
    table_copies(shape, self_ref, table_refs, part_ref, part_sem)

    def survey(device, carry):
        float_ref[pl.ds(device, 1), :] = part_ref[device, 1:2, 0:LANES]
        whole_ref[pl.ds(device, 1), :] = part_ref[device, 2:3, 0:LANES].astype(jnp.int32)
        ids = jnp.broadcast_to(part_ref[device, 0:1, 0:LANES], (LANES, LANES)).T
        ids = [ids[j * ROWS : (j + 1) * ROWS] for j in range(tiles)]

        def compare(other, state):
            key, least = state
            row = wide(part_ref[other, 0:1, 0:LANES])
            least = [
                jnp.minimum(least[j], jnp.where(ids[j] == row, key, BIG)) for j in range(tiles)
            ]
            return key + LANES, least

        none = jnp.full((ROWS, LANES), BIG, jnp.float32)
        _, least = lax.fori_loop(0, device + 1, compare, (lane_f, [none] * tiles))
        codes, leads = none, none
        for j in range(tiles):
            lead = jnp.min(least[j], axis=1, keepdims=True)
            mine = (device * LANES + j * ROWS + sub[:, 0:1]).astype(jnp.float32)
            weight_ref[device * tiles + j] = wide(jnp.where(lead == mine, 0.5, 0.0))
            later = lead < mine
            leads = jnp.where(lane == j, jnp.where(later, lead, BIG), leads)
            codes = jnp.where(lane == j, jnp.where(later, mine * float(total) + lead, BIG), codes)
        code_ref[device] = codes
        lead_ref[device] = leads
        return carry

    lax.fori_loop(0, devices, survey, 0)

    def next_code(last):
        found = jnp.full((ROWS, LANES), BIG, jnp.float32)
        for device in range(devices):
            codes = code_ref[device]
            found = jnp.minimum(found, jnp.where(codes > last, codes, BIG))
        return jnp.min(found)

    def detector(key):
        team = lax.rem(lax.div(key, reps * LANES), dets)
        return team * ROWS + lax.rem(lax.div(key, tiles), ROWS)

    def take(state):
        pairs, grouped, code = state
        number = code.astype(jnp.int32)
        key = lax.div(number, total)
        lead = lax.rem(number, total)
        shift = (3 * (detector(key) - detector(lead))) & (PBLOCK - 1)
        wanted = lead.astype(jnp.float32)
        same = jnp.zeros((ROWS, LANES), jnp.float32)
        for device in range(devices):
            same = same + jnp.where(lead_ref[device] == wanted, 1.0, 0.0)
        alone = jnp.sum(same) < 1.5
        entry = twin_entry(key, lead, shift)
        pair_ref[pairs] = entry
        group_ref[grouped] = entry
        return (
            pairs + jnp.where(alone, 1, 0), grouped + jnp.where(alone, 0, 1), next_code(code)
        )

    pairs, grouped, _ = lax.while_loop(
        lambda state: state[2] < BIG, take,
        (jnp.int32(0), jnp.int32(0), next_code(jnp.float32(-1.0))),
    )
    batches = lax.div(pairs + PAIR_BATCH - 1, PAIR_BATCH)

    def fill(n, carry):
        pair_ref[n] = twin_entry(total, total + 1, 0)
        return carry

    lax.fori_loop(pairs, batches * PAIR_BATCH, fill, 0)
    size_ref[0] = batches
    size_ref[1] = grouped


def twin_entry(key, lead, shift):
    return key * (1 << 19) + lead * (1 << 6) + shift


def twin_of(entry):
    return entry >> 19, (entry >> 6) & ((1 << 13) - 1), entry & (PBLOCK - 1)


def place_kernel(shape, self_ref, *refs):
    wafers, dets, reps, tiles, owners, capacity, owner_rows, lag_count = shape
    devices = wafers * dets * reps
    slots = devices * capacity
    table_refs, refs = refs[: wafers * dets], refs[wafers * dets :]
    place_ref, start_ref, move_ref = refs[:3]
    part_ref, rank_ref, hits_ref, rank_smem, hits_smem, part_sem, table_sem = refs[3:]
    lane, sub = tile_iotas()
    own = self_ref[1] * wafers + self_ref[0]
    first_row = (own * owner_rows).astype(jnp.float32)
    table_copies(shape, self_ref, table_refs, part_ref, part_sem)
    depth = 2 * LANES
    tall = lax.broadcasted_iota(jnp.int32, (depth, LANES), 0).astype(jnp.float32)

    def one_hots(device):
        local_row = part_ref[device, 0:1, 0:LANES] - first_row
        high = jnp.floor(local_row * (1.0 / LANES))
        low = local_row - high * LANES
        high = (jnp.broadcast_to(high, (depth, LANES)) == tall).astype(jnp.float32)
        low = (jnp.broadcast_to(low, (LANES, LANES)) == tall[0:LANES]).astype(jnp.float32)
        return high, low

    def survey(pair, hits):
        for k in range(2):
            device = 2 * pair + k
            own_hits = jnp.where(sub == own, part_ref[device, :, LANES : 2 * LANES], 0.0)
            own_hits = jnp.sum(own_hits, axis=0, keepdims=True)
            hits_ref[pl.ds(device, 1), :] = own_hits.astype(jnp.int32)
            high, low = one_hots(device)
            hits = hits + exact_dot(high, low, ((1,), (1,)))
        return hits

    hits = lax.fori_loop(0, devices // 2, survey, jnp.zeros((depth, LANES), jnp.float32))
    full = jnp.minimum(hits, 1.0)

    def ordered(size, axis):
        first = lax.broadcasted_iota(jnp.int32, (size, size), axis)
        second = lax.broadcasted_iota(jnp.int32, (size, size), 1 - axis)
        return (first < second).astype(jnp.float32)

    counts = exact_dot(jnp.ones((ROWS, LANES), jnp.float32), full, ((1,), (1,)))
    start_ref[...] = exact_dot(counts, ordered(depth, 0)).astype(jnp.int32)
    sums = exact_dot(full, jnp.ones((LANES, LANES), jnp.float32))
    place = exact_dot(full, ordered(LANES, 0)) + exact_dot(ordered(depth, 1), sums)
    place_ref[...] = jnp.where(full > 0.0, place, -1.0).astype(jnp.int32)
    place_high = jnp.floor(place * (1.0 / LANES))
    place_parts = jnp.concatenate([place_high, place - place_high * LANES], axis=0)

    def rank_of(pair, carry):
        for k in range(2):
            device = 2 * pair + k
            high, low = one_hots(device)
            parts = exact_dot(place_parts, low)
            rank = high * (parts[0:depth] * LANES + parts[depth : 2 * depth])
            rank = jnp.sum(rank, axis=0, keepdims=True)
            rank_ref[pl.ds(device, 1), :] = rank.astype(jnp.int32)
        return carry

    lax.fori_loop(0, devices // 2, rank_of, 0)
    copies = (
        pltpu.make_async_copy(rank_ref, rank_smem, table_sem.at[0]),
        pltpu.make_async_copy(hits_ref, hits_smem, table_sem.at[1]),
    )
    for copy in copies:
        copy.start()
    for copy in copies:
        copy.wait()

    def pick(device, carry):
        for c in range(capacity):
            number = hits_smem[device, c]
            valid = number < LANES
            number = number & (LANES - 1)
            target = jnp.where(valid, rank_smem[device, number], slots + LANES)
            move_ref[device * capacity + c] = target * (1 << 16) + device * LANES + number
        return carry

    lax.fori_loop(0, devices, pick, 0)


def map_kernel(
    shape, self_ref, size_ref, pair_ref, group_ref, move_ref, float_smem, whole_smem,
    angle_here_ref, angle_across_ref, angle_other_ref, tod_here_ref, tod_across_ref, tod_other_ref,
    weight_ref, column_ref,
    angle_ref, tod_ref, cos_ref, sin_ref, clean_ref, noise_ref,
    inverse_ref, r_map, image_map, share_ref, rows_ref, sorted_ref, angle_sem, tod_sem, *more_refs,
):
    wafers, dets, reps, tiles, owners, capacity, owner_rows, lag_count = shape
    devices = wafers * dets * reps
    halves = tiles // ROWS
    octets = reps * halves
    wafer_dets = dets * ROWS
    count = devices * tiles
    lane, sub = tile_iotas()
    zero = jnp.zeros((ROWS, LANES), jnp.float32)
    d_maps, sum_refs = more_refs[:ITERS], more_refs[ITERS:]
    first_sums, second_sums = sum_refs[:wafers], sum_refs[wafers:]

    def copies_of(refs, to_ref, sem):
        return part_copies(
            shape, self_ref, refs, lambda d: to_ref.at[pl.ds(d * tiles, tiles)], sem
        )

    angle_moves = copies_of((angle_here_ref, angle_across_ref, angle_other_ref), angle_ref, angle_sem)
    tod_moves = copies_of((tod_here_ref, tod_across_ref, tod_other_ref), tod_ref, tod_sem)
    for copy in angle_moves + tod_moves:
        copy.start()

    def fold(block):
        return block + pltpu.roll(block, LANES // 2, 1)

    def whole_sum(values):
        values = jnp.sum(values, axis=0, keepdims=True)
        return wide(jnp.sum(values, axis=1, keepdims=True))

    def loop(times, body, carry, unroll):
        def several(n, carry):
            for k in range(unroll):
                carry = body(n * unroll + k, carry)
            return carry

        return lax.fori_loop(0, times // unroll, several, carry)

    def device_of(wafer, n):
        return (wafer * dets + lax.shift_right_logical(n, 3)) * reps

    def register_of(wafer, n, octet):
        device = device_of(wafer, n) + octet // halves
        return device * tiles + (n & (ROWS - 1)) * halves + octet % halves

    def group_of(wafer, n):
        return whole_smem[device_of(wafer, n), n & (ROWS - 1)]

    def rows_of(octet):
        return pl.ds(octet * ROWS, ROWS)

    def count_members(n, counts):
        result = []
        for wafer in range(wafers):
            group = group_of(wafer, n)
            result += [
                counts[wafer * NSUB + g] + jnp.where(group == g, 1, 0) for g in range(NSUB)
            ]
        return tuple(result)

    members = lax.fori_loop(0, wafer_dets, count_members, (jnp.int32(0),) * (wafers * NSUB))
    for k, member in enumerate(members):
        share_ref[k] = 1.0 / jnp.maximum(zero + member.astype(jnp.float32), 1.0)
    for c in range(3):
        image_map[count, c] = zero
        r_map[count, c] = zero

    def clear_sorted(n, carry):
        at = pl.ds(pl.multiple_of(n * ROWS, ROWS), ROWS)
        sorted_ref[at, :] = jnp.zeros((ROWS, 6 * PBLOCK), jnp.float32)
        return carry

    lax.fori_loop(0, sorted_ref.shape[0] // ROWS, clear_sorted, 0)
    for copy in angle_moves:
        copy.wait()

    def survey(at, carry):
        first, second = cosine_sine_double(angle_ref[at])
        inside = lax.shift_right_logical(at, halves.bit_length() - 1) & (ROWS - 1)
        base = float_smem[lax.div(at, tiles), inside]
        cos_ref[at] = first
        sin_ref[at] = second
        image_map[at, 0] = zero + (base + base)
        image_map[at, 1] = fold(base * (first * first))
        image_map[at, 2] = fold(base * (second * second))
        return carry

    loop(count, survey, 0, 8)

    def merge_twins(target):
        def pair_batch(n, carry):
            found = []
            for k in range(PAIR_BATCH):
                key, lead, shift = twin_of(pair_ref[n * PAIR_BATCH + k])
                spots = [
                    (lax.shift_right_logical(spot, 3), pl.ds(spot & (ROWS - 1), 1))
                    for spot in (key, lead)
                ]
                values = [[target[at, c, row, :] for c in range(3)] for at, row in spots]
                found.append((spots, shift, values))
            for spots, shift, values in found:
                turns = (shift, (LANES - shift) & (LANES - 1))
                for (at, row), own, other, turn in zip(
                    spots, values, values[::-1], turns[::-1]
                ):
                    for c in range(3):
                        target[at, c, row, :] = own[c] + pltpu.roll(wide(other[c]), turn, 1)[0:1]
            return carry

        def gather_one(n, carry):
            key, lead, shift = twin_of(group_ref[n])
            at, row = lax.shift_right_logical(key, 3), key & (ROWS - 1)
            lead_at, lead_row = lax.shift_right_logical(lead, 3), lead & (ROWS - 1)
            for c in range(3):
                moved = pltpu.roll(wide(target[at, c, pl.ds(row, 1), :]), shift, 1)
                target[lead_at, c, pl.ds(lead_row, 1), :] += moved[0:1]
            return carry

        def spread_one(n, carry):
            key, lead, shift = twin_of(group_ref[n])
            at, row = lax.shift_right_logical(key, 3), key & (ROWS - 1)
            lead_at, lead_row = lax.shift_right_logical(lead, 3), lead & (ROWS - 1)
            turn = (LANES - shift) & (LANES - 1)
            for c in range(3):
                moved = pltpu.roll(wide(target[lead_at, c, pl.ds(lead_row, 1), :]), turn, 1)
                target[at, c, pl.ds(row, 1), :] = moved[0:1]
            return carry

        lax.fori_loop(0, size_ref[0], pair_batch, 0)
        lax.fori_loop(0, size_ref[1], gather_one, 0)
        lax.fori_loop(0, size_ref[1], spread_one, 0)

    def clear_sums(refs):
        for ref in refs:
            for group in range(NSUB):
                for octet in range(octets):
                    ref[group, rows_of(octet), :] = zero

    def average(refs):
        for wafer, ref in enumerate(refs):
            for group in range(NSUB):
                for octet in range(octets):
                    ref[group, rows_of(octet), :] *= share_ref[wafer * NSUB + group]

    def sum_streams(stream_of, carry):
        clear_sums(first_sums)

        def one_detector(n, carry):
            for wafer in range(wafers):
                group = group_of(wafer, n)
                for octet in range(octets):
                    stream, carry = stream_of(register_of(wafer, n, octet), carry)
                    clean_ref[wafer * wafer_dets + n, rows_of(octet), :] = stream
                    first_sums[wafer][group, rows_of(octet), :] += stream
            return carry

        carry = loop(wafer_dets, one_detector, carry, 2)
        average(first_sums)
        return carry

    def filter_streams():
        clear_sums(second_sums)

        def one_filter(n, carry):
            for wafer in range(wafers):
                device, inside = device_of(wafer, n), n & (ROWS - 1)
                detector = wafer * wafer_dets + n
                group = group_of(wafer, n)
                base = float_smem[device, inside]
                coefs = [float_smem[device, (j + 1) * ROWS + inside] for j in range(lag_count)]
                lags = [whole_smem[device, (j + 1) * ROWS + inside] for j in range(lag_count)]
                clean = [
                    clean_ref[detector, rows_of(octet), :] - first_sums[wafer][group, rows_of(octet), :]
                    for octet in range(octets)
                ]
                up = [pltpu.roll(here, ROWS - 1, 0) for here in clean] + [zero]
                down = [zero] + [pltpu.roll(here, 1, 0) for here in clean]
                for octet, here in enumerate(clean):
                    after = jnp.where(sub == ROWS - 1, up[octet + 1], up[octet])
                    ahead = jnp.where(sub == 0, down[octet], down[octet + 1])
                    result = base * here
                    for coef, lag in zip(coefs, lags):
                        later = pltpu.roll(jnp.where(lane < lag, after, here), LANES - lag, 1)
                        earlier = pltpu.roll(jnp.where(lane >= LANES - lag, ahead, here), lag, 1)
                        result = result + coef * (later + earlier)
                    noise_ref[detector, rows_of(octet), :] = result
                    second_sums[wafer][group, rows_of(octet), :] += result
                    carry = carry + here * result
            return carry

        product = loop(wafer_dets, one_filter, zero, 1)
        average(second_sums)
        return product

    def return_streams(target):
        def one_return(n, carry):
            for wafer in range(wafers):
                group = group_of(wafer, n)
                for octet in range(octets):
                    at = register_of(wafer, n, octet)
                    stream = noise_ref[wafer * wafer_dets + n, rows_of(octet), :]
                    stream = stream - second_sums[wafer][group, rows_of(octet), :]
                    target[at, 0] = fold(stream)
                    target[at, 1] = fold(cos_ref[at] * stream)
                    target[at, 2] = fold(sin_ref[at] * stream)
            return carry

        loop(wafer_dets, one_return, 0, 2)
        merge_twins(target)

    merge_twins(image_map)
    for copy in tod_moves:
        copy.wait()
    sum_streams(lambda at, carry: (tod_ref[at], carry), 0)
    filter_streams()
    return_streams(r_map)

    def begin(at, carry):
        parts = zero
        for c in range(3):
            inverse = 1.0 / (image_map[at, c] + prior_weight)
            inverse_ref[at, c] = inverse
            residual = r_map[at, c]
            parts = parts + residual * (inverse * residual)
        return carry + weight_ref[at] * parts

    energy = whole_sum(loop(count, begin, zero, 8))
    factor = zero
    steps = []
    for iteration, d_map in enumerate(d_maps):
        last = iteration == ITERS - 1

        def seen_stream(at, carry):
            parts = []
            for c in range(3):
                part = inverse_ref[at, c] * r_map[at, c]
                if iteration:
                    part = part + factor * d_maps[iteration - 1][at, c]
                d_map[at, c] = part
                parts.append(part)
            squares = parts[0] * parts[0] + parts[1] * parts[1] + parts[2] * parts[2]
            stream = parts[0] + cos_ref[at] * parts[1] + sin_ref[at] * parts[2]
            return stream, carry + weight_ref[at] * squares

        prior = sum_streams(seen_stream, zero)
        product = filter_streams()
        return_streams(image_map)
        step = energy / whole_sum(product + prior_weight * prior)
        steps.append(step)

        def new_residual(at, c):
            return r_map[at, c] - step * (image_map[at, c] + prior_weight * d_map[at, c])

        if not last:

            def update(at, carry):
                parts = zero
                for c in range(3):
                    residual = new_residual(at, c)
                    r_map[at, c] = residual
                    parts = parts + residual * (inverse_ref[at, c] * residual)
                return carry + weight_ref[at] * parts

            next_energy = whole_sum(loop(count, update, zero, 8))
            factor = next_energy / energy
            energy = next_energy
        else:

            def place_pixels(at, carry):
                team = lax.rem(lax.div(at, reps * tiles), dets)
                inside = lax.shift_right_logical(at, halves.bit_length() - 1) & (ROWS - 1)
                turn = (3 * (team * ROWS + inside)) & (PBLOCK - 1)
                values = []
                for c in range(3):
                    value = steps[0] * d_maps[0][at, c]
                    for k in range(1, ITERS):
                        value = value + steps[k] * d_maps[k][at, c]
                    values.append(value)
                values += [new_residual(at, c) for c in range(3)]
                values = [pltpu.roll(value, turn, 1) for value in values]
                rows = pl.ds(pl.multiple_of(at * ROWS, ROWS), ROWS)
                for c in range(3):
                    rows_ref[rows, c * LANES : (c + 1) * LANES] = jnp.where(
                        lane < PBLOCK, values[2 * c], values[2 * c + 1]
                    )
                return carry

            loop(count, place_pixels, 0, 8)

    def pick(device, carry):
        for c in range(capacity):
            move = move_ref[device * capacity + c]
            source, target = move & ((1 << 16) - 1), move >> 16
            sorted_ref[pl.ds(target, 1), :] = rows_ref[pl.ds(source, 1), :]
        return carry

    lax.fori_loop(0, devices, pick, 0)

    def turn_tile(tile, carry):
        columns = sorted_ref[pl.ds(pl.multiple_of(tile * LANES, LANES), LANES), :].T
        high = columns.astype(jnp.bfloat16)
        column_ref[tile, :, 0:LANES] = high
        column_ref[tile, :, LANES : 2 * LANES] = (columns - high.astype(jnp.float32)).astype(
            jnp.bfloat16
        )
        return carry

    lax.fori_loop(0, column_ref.shape[0], turn_tile, 0)


def write_kernel(start_ref, column_ref, place_ref, x_ref, r_ref):
    height = 3 * PBLOCK
    depth = lax.broadcasted_iota(jnp.int32, (LANES, LANES), 0)
    step = pl.program_id(0) * OUT_TILES

    def spread(group, tile):
        chosen = []
        for k in range(2):
            place = jnp.broadcast_to(place_ref[pl.ds(group + k, 1), :], (LANES, LANES))
            chosen.append(jnp.where(place == depth + tile * LANES, 1.0, 0.0).astype(jnp.bfloat16))
        chosen = jnp.concatenate(chosen, axis=1)
        chosen = jnp.concatenate([chosen, chosen], axis=0)
        return jnp.dot(column_ref[tile], chosen, preferred_element_type=jnp.float32)

    def tiles_of(group):
        start, end = start_ref[0, group], start_ref[0, group + 2]
        first = lax.shift_right_logical(start, 7)
        return first, lax.shift_right_logical(jnp.maximum(end - 1, start), 7)

    further = 0
    for pair in range(OUT_TILES // 2):
        first, last = tiles_of(step + 2 * pair)
        further = further + (last - first)
        values = spread(step + 2 * pair, first)
        columns = slice(pair * 2 * LANES, (pair + 1) * 2 * LANES)
        x_ref[:, columns] = values[:height]
        r_ref[:, columns] = values[height:]

    @pl.when(further > 0)
    def _():
        for pair in range(OUT_TILES // 2):
            first, last = tiles_of(step + 2 * pair)
            columns = slice(pair * 2 * LANES, (pair + 1) * 2 * LANES)

            def add_tile(tile, carry):
                values = spread(step + 2 * pair, tile)
                x_ref[:, columns] += values[:height]
                r_ref[:, columns] += values[height:]
                return carry

            lax.fori_loop(first + 1, last + 1, add_tile, 0)


def part_shape(sizes, tod, hit_list, band_lag):
    det_count, time_count = tod.shape[1:]
    owners, capacity = hit_list.shape[3:]
    return (
        sizes["wafer"], sizes["det"], sizes["rep"], time_count // SBLOCK,
        owners, capacity, BLOCKS // owners, band_lag.shape[2],
    ), det_count


def fits_one_device(shape, det_count):
    wafers, dets, reps, tiles, owners, capacity, owner_rows, lag_count = shape
    devices = wafers * dets * reps
    total = devices * tiles * det_count
    groups = owner_rows // LANES
    return (
        det_count == ROWS
        and owners == ROWS
        and tiles * ROWS == LANES
        and tiles % ROWS == 0
        and (wafers, reps) == (2, 2)
        and (1 + lag_count) * ROWS <= LANES
        and capacity <= LANES
        and devices * capacity % LANES == 0
        and owner_rows % (LANES * OUT_TILES) == 0
        and groups + 2 <= 2 * LANES
        and total * total < BIG
    )


def whole_part(shape, tod, psi, point_row, hit_list, group_id, a_zero, band_coef, band_lag):
    wafers, dets, reps, tiles, owners, capacity, owner_rows, lag_count = shape
    devices = wafers * dets * reps
    octets = reps * tiles // ROWS
    detectors = wafers * dets * ROWS
    count = devices * tiles
    total = count * ROWS
    slots = devices * capacity
    height = 3 * PBLOCK
    f32, i32 = jnp.float32, jnp.int32
    vmem, smem = pl.BlockSpec(memory_space=pltpu.VMEM), pl.BlockSpec(memory_space=pltpu.SMEM)
    anywhere = pl.BlockSpec(memory_space=pl.ANY)
    params = pltpu.CompilerParams(vmem_limit_bytes=VMEM_BYTES)
    swap = [(0, 1), (1, 0)]

    def along_det(block):
        moved = [
            lax.ppermute(block, "det", [(i, (i + shift) % dets) for i in range(dets)])
            for shift in range(1, dets)
        ]
        return [block] + moved

    def other_wafer(here):
        return lax.ppermute(here, "wafer", swap)

    def other_rep(here, across):
        return here, across, lax.ppermute(jnp.stack([here, across]), "rep", swap)

    tables, angles, samples = pl.pallas_call(
        functools.partial(pack_kernel, shape),
        out_shape=[
            jax.ShapeDtypeStruct((ROWS, 2 * LANES), f32),
            jax.ShapeDtypeStruct((ROWS, tiles, LANES), f32),
            jax.ShapeDtypeStruct((ROWS, tiles, LANES), f32),
        ],
        in_specs=[vmem] * 8,
        out_specs=[vmem] * 3,
        compiler_params=params,
        name="pack",
    )(
        psi[0], tod[0], point_row[0], hit_list[0, 0, 0], group_id, a_zero, band_coef[0].T,
        band_lag[0].T,
    )
    angles, samples = (stream.reshape(tiles, ROWS, LANES) for stream in (angles, samples))
    place_here = jnp.stack([lax.axis_index(axis) for axis in ("wafer", "det", "rep")]).astype(i32)
    chips = wafers * dets
    tables = lax.all_gather(tables, "rep", axis=0, tiled=False)
    angles, tables = lax.optimization_barrier((angles, tables))
    tables = [tables] + [
        lax.ppermute(tables, ("det", "wafer"), [(i, (i + shift) % chips) for i in range(chips)])
        for shift in range(1, chips)
    ]
    samples, angles, *tables = lax.optimization_barrier(
        (samples, jnp.stack(along_det(angles)), *tables)
    )
    angles_across = other_wafer(angles)
    samples = jnp.stack(along_det(samples))
    table_scratch = pltpu.VMEM((devices, ROWS, 2 * LANES), f32)
    table_sem = pltpu.SemaphoreType.DMA((chips,))
    twins = pl.pallas_call(
        functools.partial(twin_kernel, shape),
        out_shape=[
            jax.ShapeDtypeStruct((count, ROWS, LANES), f32),
            jax.ShapeDtypeStruct((devices, LANES), f32),
            jax.ShapeDtypeStruct((devices, LANES), i32),
            jax.ShapeDtypeStruct((2,), i32),
            jax.ShapeDtypeStruct((total,), i32),
            jax.ShapeDtypeStruct((total,), i32),
        ],
        in_specs=[smem] + [anywhere] * chips,
        out_specs=[vmem] * 3 + [smem] * 3,
        scratch_shapes=[
            table_scratch,
            pltpu.VMEM((devices, ROWS, LANES), f32),
            pltpu.VMEM((devices, ROWS, LANES), f32),
            table_sem,
        ],
        compiler_params=params,
        cost_estimate=pl.CostEstimate(flops=10**9, bytes_accessed=3 * 10**7, transcendentals=0),
        name="twins",
    )(place_here, *tables)
    angles, angles_across, samples, tables, twins = lax.optimization_barrier(
        (angles, angles_across, samples, tables, twins)
    )
    weight, floats, whole, size, pair, group = twins
    samples_across = other_wafer(samples)
    place, start, moves = pl.pallas_call(
        functools.partial(place_kernel, shape),
        out_shape=[
            jax.ShapeDtypeStruct((2 * LANES, LANES), i32),
            jax.ShapeDtypeStruct((ROWS, 2 * LANES), i32),
            jax.ShapeDtypeStruct((slots,), i32),
        ],
        in_specs=[smem] + [anywhere] * chips,
        out_specs=[vmem, vmem, smem],
        scratch_shapes=[
            table_scratch,
            pltpu.VMEM((devices, LANES), i32),
            pltpu.VMEM((devices, LANES), i32),
            pltpu.SMEM((devices, LANES), i32),
            pltpu.SMEM((devices, LANES), i32),
            table_sem,
            pltpu.SemaphoreType.DMA((2,)),
        ],
        compiler_params=params,
        cost_estimate=pl.CostEstimate(flops=10**9, bytes_accessed=2 * 10**7, transcendentals=0),
        name="places",
    )(place_here, *tables)
    angle_blocks = other_rep(angles, angles_across)
    samples, samples_across, place, start, moves = lax.optimization_barrier(
        (samples, samples_across, place, start, moves)
    )
    sample_blocks = other_rep(samples, samples_across)
    stream = pltpu.VMEM((count, ROWS, LANES), f32)
    sky = pltpu.VMEM((count, 3, ROWS, LANES), f32)
    sky_and_spare = pltpu.VMEM((count + 1, 3, ROWS, LANES), f32)
    group_sums = pltpu.VMEM((NSUB, octets * ROWS, LANES), f32)
    columns = pl.pallas_call(
        functools.partial(map_kernel, shape),
        out_shape=jax.ShapeDtypeStruct((slots // LANES + 1, 2 * height, 2 * LANES), jnp.bfloat16),
        in_specs=[smem] * 7 + [anywhere] * 6 + [vmem],
        out_specs=vmem,
        scratch_shapes=[
            stream, stream, stream, stream,
            pltpu.VMEM((detectors, octets * ROWS, LANES), f32),
            pltpu.VMEM((detectors, octets * ROWS, LANES), f32),
            sky, sky_and_spare, sky_and_spare,
            pltpu.VMEM((wafers * NSUB, ROWS, LANES), f32),
            pltpu.VMEM((total, 2 * height), f32),
            pltpu.VMEM((slots + LANES + ROWS, 2 * height), f32),
            pltpu.SemaphoreType.DMA((devices,)),
            pltpu.SemaphoreType.DMA((devices,)),
        ] + [sky] * ITERS + [group_sums] * (2 * wafers),
        compiler_params=params,
        name="map_maker",
    )(
        place_here, size, pair, group, moves, floats, whole, *angle_blocks,
        *sample_blocks, weight,
    )
    out_block = pl.BlockSpec((height, OUT_TILES * LANES), lambda n: (0, n))
    x_turned, r_turned = pl.pallas_call(
        write_kernel,
        grid=(owner_rows // (OUT_TILES * LANES),),
        out_shape=[jax.ShapeDtypeStruct((height, owner_rows), f32)] * 2,
        in_specs=[smem, vmem, vmem],
        out_specs=[out_block, out_block],
        compiler_params=params,
        name="write",
    )(start, columns, place)
    return x_turned.T, r_turned.T


def local(sizes, *arguments):
    tod, hit_list, band_lag = arguments[0], arguments[3], arguments[7]
    shape, det_count = part_shape(sizes, tod, hit_list, band_lag)
    if fits_one_device(shape, det_count):
        return whole_part(shape, *arguments)
    return distributed(*arguments)


def solution(mesh):
    placed = (
        P(("groups", "wafer"), "det", "rep"),
        P(("groups", "wafer"), "det", "rep"),
        P(("groups", "wafer"), "det", "rep"),
        P(("groups", "wafer"), "det", "rep", None, None),
        P(("groups", "wafer"), "det"),
        P(("groups", "wafer"), "det"),
        P(("groups", "wafer"), "det", None),
        P(("groups", "wafer"), "det", None),
    )
    return jax.shard_map(
        functools.partial(local, mesh.shape),
        mesh=mesh,
        in_specs=placed,
        out_specs=(P(("groups", "det", "wafer"), None), P(("groups", "det", "wafer"), None)),
        check_vma=False,
    )
```

profile of v0, /device:TPU:0, one launch (start us, length us, event | category | flops | bytes accessed | tf_op | source)
XLA Modules:
  0.0 126.6 jit_solution(14059678813266858553)
XLA Ops:
  0.6 1.7 %pack.1 = (f32[8,256]{1,0:T(8,128)}, f32[8,16,128]{2,1,0:T(8,128)}, f32[8,16,128]{2,1,0:T(8,128)}) custom-call(f32[8,2048]{1,0:T(8,128)} %bitcast.34, f32[8,2048]{1,0:T(8,128)} %bitcast.35, s32[8,16]{1,0:T(8,128)} %bitcast.59, s32[8,32]{1,0:T(8,128)} %bitcast.60, s32[1,8]{1,0:T(1,128)} %group_ref.1, f32[1,8]{1,0:T(1,128)} %base_ref.1, f32[4,8]{1,0:T(4,128)} %bitcast.61, ...), custom_call_target="tpu_custom_call" | custom-call | tf_op jit(solution)/shard_map/pack/pallas_call | solution.py:864
  2.3 2.1 %all-gather = f32[16,256]{1,0:T(8,128)S(1)} all-gather(f32[8,256]{1,0:T(8,128)} %get-tuple-element.52), channel_id=2, replica_groups=mesh['groups'=2,'det'=4,'wafer'=2,'rep'=2] {'rep'}, dimensions={0}, use_global_device_ids=true | all-gather | bytes 24576 | tf_op jit(solution)/shard_map/all_gather | solution.py:882
  4.5 5.0 %collective-permute-start.2 = (f32[16,8,128]{2,1,0:T(8,128)}, f32[16,8,128]{2,1,0:T(8,128)S(1)}, u32[]{:S(2)}, u32[]{:S(2)}) collective-permute-start(f32[16,8,128]{2,1,0:T(8,128)} %bitcast.40), channel_id=1, source_target_pairs={{0,12},{4,0},{8,4},{12,8},{1,13},{5,1},{9,5},{13,9},{2,14},{6,2},{... | collective-permute-start | bytes 196616 | tf_op jit(solution)/shard_map/ppermute | solution.py:853
  9.4 1.0 collective-permute-start
  10.4 3.7 %collective-permute-start.9 = (f32[2,8,256]{2,1,0:T(8,128)S(1)}, f32[2,8,256]{2,1,0:T(8,128)S(1)}, u32[]{:S(2)}, u32[]{:S(2)}) collective-permute-start(f32[2,8,256]{2,1,0:T(8,128)S(1)} %bitcast.50), channel_id=1, source_target_pairs={{0,14},{2,0},{4,2},{6,4},{8,6},{10,8},{12,10},{14,12},{1,15},{3,1}... | collective-permute-start | bytes 49160 | tf_op jit(solution)/shard_map/ppermute | solution.py:885
  14.7 0.9 collective-permute-done.9.refs_7_
  15.6 2.4 %collective-permute-start.7 = (f32[2,8,256]{2,1,0:T(8,128)S(1)}, f32[2,8,256]{2,1,0:T(8,128)S(1)}, u32[]{:S(2)}, u32[]{:S(2)}) collective-permute-start(f32[2,8,256]{2,1,0:T(8,128)S(1)} %bitcast.52), channel_id=1, source_target_pairs={{0,10},{2,12},{4,14},{6,0},{8,2},{10,4},{12,6},{14,8},{1,11},{3,13... | collective-permute-start | bytes 49160 | tf_op jit(solution)/shard_map/ppermute | solution.py:885
  18.0 2.4 %collective-permute-start.6 = (f32[2,8,256]{2,1,0:T(8,128)S(1)}, f32[2,8,256]{2,1,0:T(8,128)S(1)}, u32[]{:S(2)}, u32[]{:S(2)}) collective-permute-start(f32[2,8,256]{2,1,0:T(8,128)S(1)} %bitcast.53), channel_id=1, source_target_pairs={{0,8},{2,10},{4,12},{6,14},{8,0},{10,2},{12,4},{14,6},{1,9},{3,11}... | collective-permute-start | bytes 49160 | tf_op jit(solution)/shard_map/ppermute | solution.py:885
  20.5 0.8 collective-permute-start.5
  21.5 4.1 %collective-permute-start.3 = (f32[2,8,256]{2,1,0:T(8,128)S(1)}, f32[2,8,256]{2,1,0:T(8,128)S(1)}, u32[]{:S(2)}, u32[]{:S(2)}) collective-permute-start(f32[2,8,256]{2,1,0:T(8,128)S(1)} %bitcast.56), channel_id=1, source_target_pairs={{0,2},{2,4},{4,6},{6,8},{8,10},{10,12},{12,14},{14,0},{1,3},{3,5},... | collective-permute-start | bytes 49160 | tf_op jit(solution)/shard_map/ppermute | solution.py:885
  25.6 0.9 pad_maximum_fusion.2.angle_here_ref
  26.8 1.1 collective-permute-done.3.refs_1_
  27.9 1.5 %collective-permute-start.10 = (f32[4,16,8,128]{3,2,1,0:T(8,128)S(1)}, f32[4,16,8,128]{3,2,1,0:T(8,128)S(1)}, u32[]{:S(2)}, u32[]{:S(2)}) collective-permute-start(f32[4,16,8,128]{3,2,1,0:T(8,128)S(1)} %pad_maximum_fusion.2.angle_here_ref), channel_id=1, source_target_pairs={{0,2},{2,0},{1,3},{3,1},{4,6},{6,4},{5,7},{7,5},{8,10},{10,8},{9,1... | collective-permute-start | bytes 786440 | tf_op jit(solution)/shard_map/ppermute | solution.py:859
  30.1 0.6 collective-permute-start.13
  30.7 0.9 collective-permute-start.12
  31.6 0.7 collective-permute-start.11
  32.4 9.2 %twins.1 = (f32[256,8,128]{2,1,0:T(8,128)}, f32[16,128]{1,0:T(8,128)}, s32[16,128]{1,0:T(8,128)}, s32[2]{0:T(128)}, s32[2048]{0:T(1024)}, /*index=5*/s32[2048]{0:T(1024)}) custom-call(s32[3]{0:T(128)} %pad_add_fusion.self_ref, f32[2,8,256]{2,1,0:T(8,128)} %bitcast.57, f32[2,8,256]{2,1,0:T(8,128)} %copy-done.13, f32[2,8,256]{2,1,0:T(8,128)} %copy-done.12, ...), custom_call_target="tpu_custom_call" | custom-call | flops 1000000000 | bytes 30000000 | tf_op jit(solution)/shard_map/twins/pallas_call | solution.py:895
  41.7 0.9 pad_maximum_fusion.3.tod_here_ref
  42.6 1.3 %collective-permute-start.14 = (f32[4,16,8,128]{3,2,1,0:T(8,128)S(1)}, f32[4,16,8,128]{3,2,1,0:T(8,128)S(1)}, u32[]{:S(2)}, u32[]{:S(2)}) collective-permute-start(f32[4,16,8,128]{3,2,1,0:T(8,128)S(1)} %pad_maximum_fusion.3.tod_here_ref), channel_id=1, source_target_pairs={{0,2},{2,0},{1,3},{3,1},{4,6},{6,4},{5,7},{7,5},{8,10},{10,8},{9,1... | collective-permute-start | bytes 786440 | tf_op jit(solution)/shard_map/ppermute | solution.py:859
  44.0 9.1 %places.1 = (s32[256,128]{1,0:T(8,128)}, s32[8,256]{1,0:T(8,128)}, s32[512]{0:T(512)}) custom-call(s32[3]{0:T(128)} %pad_add_fusion.self_ref, f32[2,8,256]{2,1,0:T(8,128)} %bitcast.58, f32[2,8,256]{2,1,0:T(8,128)} %copy-done.13, f32[2,8,256]{2,1,0:T(8,128)} %copy-done.12, f32[2,8,256]{2,1,0:T(8,128)} %copy-done.11, f32[2,8,256]{2,1,0:T(8,128)} %copy-done.10, ...), custom_call_target="tpu_custom_call" | custom-call | flops 1000000000 | bytes 20000000 | tf_op jit(solution)/shard_map/places/pallas_call | solution.py:922
  53.7 1.5 %collective-permute-done.16.tod_other_ref = f32[2,4,16,8,128]{4,3,2,1,0:T(8,128)S(1)} collective-permute-done((f32[2,4,16,8,128]{4,3,2,1,0:T(8,128)S(1)}, f32[2,4,16,8,128]{4,3,2,1,0:T(8,128)S(1)}, u32[]{:S(2)}, u32[]{:S(2)}) %collective-permute-start.16) | collective-permute-done | bytes 524320 | tf_op jit(solution)/shard_map/ppermute | solution.py:862
  55.2 0.8 copy-done.5
  56.0 50.7 %map_maker.1.column_ref = bf16[5,384,256]{2,1,0:T(8,128)(2,1)} custom-call(s32[3]{0:T(128)} %pad_add_fusion.self_ref, s32[2]{0:T(128)} %get-tuple-element.84.size_ref, s32[2048]{0:T(1024)} %get-tuple-element.85.pair_ref, s32[2048]{0:T(1024)} %get-tuple-element.86.group_ref, s32[512]{0:T(512)} %get-tuple-element.87.move_ref, ...), custom_call_target="tpu_custom_call" | custom-call | tf_op jit(solution)/shard_map/map_maker/pallas_call | solution.py:953
  106.7 19.9 %write.1 = (f32[192,24576]{1,0:T(8,128)}, f32[192,24576]{1,0:T(8,128)}) custom-call(s32[8,256]{1,0:T(8,128)} %get-tuple-element.83.start_ref, bf16[5,384,256]{2,1,0:T(8,128)(2,1)} %map_maker.1.column_ref, s32[256,128]{1,0:T(8,128)} %get-tuple-element.95.place_ref), custom_call_target="tpu_custom_call" | custom-call | tf_op jit(solution)/shard_map/write/pallas_call | solution.py:976
  (49 shorter events, 2.5 us)
Async XLA Ops:
  4.5 27.9 %copy-start.6 = (f32[16,256]{1,0:T(8,128)}, f32[16,256]{1,0:T(8,128)S(1)}, u32[]{:S(2)}) copy-start(f32[16,256]{1,0:T(8,128)S(1)} %all-gather) | copy-start | bytes 49156
  4.5 16.0 %collective-permute-start.2 = (f32[16,8,128]{2,1,0:T(8,128)}, f32[16,8,128]{2,1,0:T(8,128)S(1)}, u32[]{:S(2)}, u32[]{:S(2)}) collective-permute-start(f32[16,8,128]{2,1,0:T(8,128)} %bitcast.40), channel_id=1, source_target_pairs={{0,12},{4,0},{8,4},{12,8},{1,13},{5,1},{9,5},{13,9},{2,14},{6,2},{... | collective-permute-start | bytes 196616 | tf_op jit(solution)/shard_map/ppermute | solution.py:853
  9.4 11.8 %collective-permute-start.1 = (f32[16,8,128]{2,1,0:T(8,128)}, f32[16,8,128]{2,1,0:T(8,128)S(1)}, u32[]{:S(2)}, u32[]{:S(2)}) collective-permute-start(f32[16,8,128]{2,1,0:T(8,128)} %bitcast.41), channel_id=1, source_target_pairs={{0,8},{4,12},{8,0},{12,4},{1,9},{5,13},{9,1},{13,5},{2,10},{6,14},... | collective-permute-start | bytes 196616 | tf_op jit(solution)/shard_map/ppermute | solution.py:853
  9.4 12.1 %collective-permute-start = (f32[16,8,128]{2,1,0:T(8,128)}, f32[16,8,128]{2,1,0:T(8,128)S(1)}, u32[]{:S(2)}, u32[]{:S(2)}) collective-permute-start(f32[16,8,128]{2,1,0:T(8,128)} %bitcast.42), channel_id=1, source_target_pairs={{0,4},{4,8},{8,12},{12,0},{1,5},{5,9},{9,13},{13,1},{2,6},{6,10},{... | collective-permute-start | bytes 196616 | tf_op jit(solution)/shard_map/ppermute | solution.py:853
  10.4 5.2 %collective-permute-start.9 = (f32[2,8,256]{2,1,0:T(8,128)S(1)}, f32[2,8,256]{2,1,0:T(8,128)S(1)}, u32[]{:S(2)}, u32[]{:S(2)}) collective-permute-start(f32[2,8,256]{2,1,0:T(8,128)S(1)} %bitcast.50), channel_id=1, source_target_pairs={{0,14},{2,0},{4,2},{6,4},{8,6},{10,8},{12,10},{14,12},{1,15},{3,1}... | collective-permute-start | bytes 49160 | tf_op jit(solution)/shard_map/ppermute | solution.py:885
  14.2 3.8 %collective-permute-start.8 = (f32[2,8,256]{2,1,0:T(8,128)S(1)}, f32[2,8,256]{2,1,0:T(8,128)S(1)}, u32[]{:S(2)}, u32[]{:S(2)}) collective-permute-start(f32[2,8,256]{2,1,0:T(8,128)S(1)} %bitcast.51), channel_id=1, source_target_pairs={{0,12},{2,14},{4,0},{6,2},{8,4},{10,6},{12,8},{14,10},{1,13},{3,15... | collective-permute-start | bytes 49160 | tf_op jit(solution)/shard_map/ppermute | solution.py:885
  15.6 16.8 %copy-start.7 = (f32[2,8,256]{2,1,0:T(8,128)}, f32[2,8,256]{2,1,0:T(8,128)S(1)}, u32[]{:S(2)}) copy-start(f32[2,8,256]{2,1,0:T(8,128)S(1)} %collective-permute-done.9.refs_7_) | copy-start | bytes 49156
  15.6 10.8 %collective-permute-start.7 = (f32[2,8,256]{2,1,0:T(8,128)S(1)}, f32[2,8,256]{2,1,0:T(8,128)S(1)}, u32[]{:S(2)}, u32[]{:S(2)}) collective-permute-start(f32[2,8,256]{2,1,0:T(8,128)S(1)} %bitcast.52), channel_id=1, source_target_pairs={{0,10},{2,12},{4,14},{6,0},{8,2},{10,4},{12,6},{14,8},{1,11},{3,13... | collective-permute-start | bytes 49160 | tf_op jit(solution)/shard_map/ppermute | solution.py:885
  18.0 14.4 %copy-start.8 = (f32[2,8,256]{2,1,0:T(8,128)}, f32[2,8,256]{2,1,0:T(8,128)S(1)}, u32[]{:S(2)}) copy-start(f32[2,8,256]{2,1,0:T(8,128)S(1)} %collective-permute-done.8.refs_6_) | copy-start | bytes 49156
  18.0 8.5 %collective-permute-start.6 = (f32[2,8,256]{2,1,0:T(8,128)S(1)}, f32[2,8,256]{2,1,0:T(8,128)S(1)}, u32[]{:S(2)}, u32[]{:S(2)}) collective-permute-start(f32[2,8,256]{2,1,0:T(8,128)S(1)} %bitcast.53), channel_id=1, source_target_pairs={{0,8},{2,10},{4,12},{6,14},{8,0},{10,2},{12,4},{14,6},{1,9},{3,11}... | collective-permute-start | bytes 49160 | tf_op jit(solution)/shard_map/ppermute | solution.py:885
  20.5 6.0 %collective-permute-start.5 = (f32[2,8,256]{2,1,0:T(8,128)S(1)}, f32[2,8,256]{2,1,0:T(8,128)S(1)}, u32[]{:S(2)}, u32[]{:S(2)}) collective-permute-start(f32[2,8,256]{2,1,0:T(8,128)S(1)} %bitcast.54), channel_id=1, source_target_pairs={{0,6},{2,8},{4,10},{6,12},{8,14},{10,0},{12,2},{14,4},{1,7},{3,9},... | collective-permute-start | bytes 49160 | tf_op jit(solution)/shard_map/ppermute | solution.py:885
  21.3 5.5 %collective-permute-start.4 = (f32[2,8,256]{2,1,0:T(8,128)S(1)}, f32[2,8,256]{2,1,0:T(8,128)S(1)}, u32[]{:S(2)}, u32[]{:S(2)}) collective-permute-start(f32[2,8,256]{2,1,0:T(8,128)S(1)} %bitcast.55), channel_id=1, source_target_pairs={{0,4},{2,6},{4,8},{6,10},{8,12},{10,14},{12,0},{14,2},{1,5},{3,7},... | collective-permute-start | bytes 49160 | tf_op jit(solution)/shard_map/ppermute | solution.py:885
  21.5 6.4 %collective-permute-start.3 = (f32[2,8,256]{2,1,0:T(8,128)S(1)}, f32[2,8,256]{2,1,0:T(8,128)S(1)}, u32[]{:S(2)}, u32[]{:S(2)}) collective-permute-start(f32[2,8,256]{2,1,0:T(8,128)S(1)} %bitcast.56), channel_id=1, source_target_pairs={{0,2},{2,4},{4,6},{6,8},{8,10},{10,12},{12,14},{14,0},{1,3},{3,5},... | collective-permute-start | bytes 49160 | tf_op jit(solution)/shard_map/ppermute | solution.py:885
  26.5 28.7 %copy-start = (f32[4,16,8,128]{3,2,1,0:T(8,128)}, f32[4,16,8,128]{3,2,1,0:T(8,128)S(1)}, u32[]{:S(2)}) copy-start(f32[4,16,8,128]{3,2,1,0:T(8,128)S(1)} %pad_maximum_fusion.2.angle_here_ref) | copy-start | bytes 786436
  26.5 5.9 %copy-start.9 = (f32[2,8,256]{2,1,0:T(8,128)}, f32[2,8,256]{2,1,0:T(8,128)S(1)}, u32[]{:S(2)}) copy-start(f32[2,8,256]{2,1,0:T(8,128)S(1)} %collective-permute-done.7.refs_5_) | copy-start | bytes 49156
  27.9 14.6 %collective-permute-start.10 = (f32[4,16,8,128]{3,2,1,0:T(8,128)S(1)}, f32[4,16,8,128]{3,2,1,0:T(8,128)S(1)}, u32[]{:S(2)}, u32[]{:S(2)}) collective-permute-start(f32[4,16,8,128]{3,2,1,0:T(8,128)S(1)} %pad_maximum_fusion.2.angle_here_ref), channel_id=1, source_target_pairs={{0,2},{2,0},{1,3},{3,1},{4,6},{6,4},{5,7},{7,5},{8,10},{10,8},{9,1... | collective-permute-start | bytes 786440 | tf_op jit(solution)/shard_map/ppermute | solution.py:859
  30.1 11.6 %collective-permute-start.13 = (f32[16,8,128]{2,1,0:T(8,128)}, f32[16,8,128]{2,1,0:T(8,128)S(1)}, u32[]{:S(2)}, u32[]{:S(2)}) collective-permute-start(f32[16,8,128]{2,1,0:T(8,128)} %bitcast.36), channel_id=1, source_target_pairs={{0,12},{4,0},{8,4},{12,8},{1,13},{5,1},{9,5},{13,9},{2,14},{6,2},{... | collective-permute-start | bytes 196616 | tf_op jit(solution)/shard_map/ppermute | solution.py:853
  30.7 10.9 %collective-permute-start.12 = (f32[16,8,128]{2,1,0:T(8,128)}, f32[16,8,128]{2,1,0:T(8,128)S(1)}, u32[]{:S(2)}, u32[]{:S(2)}) collective-permute-start(f32[16,8,128]{2,1,0:T(8,128)} %bitcast.37), channel_id=1, source_target_pairs={{0,8},{4,12},{8,0},{12,4},{1,9},{5,13},{9,1},{13,5},{2,10},{6,14},... | collective-permute-start | bytes 196616 | tf_op jit(solution)/shard_map/ppermute | solution.py:853
  31.6 10.0 %collective-permute-start.11 = (f32[16,8,128]{2,1,0:T(8,128)}, f32[16,8,128]{2,1,0:T(8,128)S(1)}, u32[]{:S(2)}, u32[]{:S(2)}) collective-permute-start(f32[16,8,128]{2,1,0:T(8,128)} %bitcast.38), channel_id=1, source_target_pairs={{0,4},{4,8},{8,12},{12,0},{1,5},{5,9},{9,13},{13,1},{2,6},{6,10},{... | collective-permute-start | bytes 196616 | tf_op jit(solution)/shard_map/ppermute | solution.py:853
  42.5 12.7 %copy-start.1 = (f32[4,16,8,128]{3,2,1,0:T(8,128)}, f32[4,16,8,128]{3,2,1,0:T(8,128)S(1)}, u32[]{:S(2)}) copy-start(f32[4,16,8,128]{3,2,1,0:T(8,128)S(1)} %pad_maximum_fusion.3.tod_here_ref) | copy-start | bytes 786436
  42.5 12.6 %copy-start.2 = (f32[4,16,8,128]{3,2,1,0:T(8,128)}, f32[4,16,8,128]{3,2,1,0:T(8,128)S(1)}, u32[]{:S(2)}) copy-start(f32[4,16,8,128]{3,2,1,0:T(8,128)S(1)} %collective-permute-done.10.angle_across_ref) | copy-start | bytes 786436
  42.6 10.5 %collective-permute-start.14 = (f32[4,16,8,128]{3,2,1,0:T(8,128)S(1)}, f32[4,16,8,128]{3,2,1,0:T(8,128)S(1)}, u32[]{:S(2)}, u32[]{:S(2)}) collective-permute-start(f32[4,16,8,128]{3,2,1,0:T(8,128)S(1)} %pad_maximum_fusion.3.tod_here_ref), channel_id=1, source_target_pairs={{0,2},{2,0},{1,3},{3,1},{4,6},{6,4},{5,7},{7,5},{8,10},{10,8},{9,1... | collective-permute-start | bytes 786440 | tf_op jit(solution)/shard_map/ppermute | solution.py:859
  43.9 9.8 %collective-permute-start.15 = (f32[2,4,16,8,128]{4,3,2,1,0:T(8,128)S(1)}, f32[2,4,16,8,128]{4,3,2,1,0:T(8,128)S(1)}, u32[]{:S(2)}, u32[]{:S(2)}) collective-permute-start(f32[2,4,16,8,128]{4,3,2,1,0:T(8,128)S(1)} %pad_maximum_fusion), channel_id=1, source_target_pairs={{0,1},{1,0},{2,3},{3,2},{4,5},{5,4},{6,7},{7,6},{8,9},{9,8},{10,11... | collective-permute-start | bytes 1572872 | tf_op jit(solution)/shard_map/ppermute | solution.py:862
  53.1 2.1 %collective-permute-start.16 = (f32[2,4,16,8,128]{4,3,2,1,0:T(8,128)S(1)}, f32[2,4,16,8,128]{4,3,2,1,0:T(8,128)S(1)}, u32[]{:S(2)}, u32[]{:S(2)}) collective-permute-start(f32[2,4,16,8,128]{4,3,2,1,0:T(8,128)S(1)} %pad_maximum_fusion.1), channel_id=1, source_target_pairs={{0,1},{1,0},{2,3},{3,2},{4,5},{5,4},{6,7},{7,6},{8,9},{9,8},{10,11... | collective-permute-start | bytes 1572872 | tf_op jit(solution)/shard_map/ppermute | solution.py:862
  (7 other events, 26.4 us)
where the time goes:
time: 128 us; the launch traced here: 127 us
  Pallas kernels  90.5 us (71%)
  starting transfers between devices  26 us (20%)
  waiting for transfers between devices  3.86 us (3%)
  other arithmetic  2.4 us (2%)
  blocking collectives  2.14 us (2%)
    pallas_call x1, Pallas kernels, whole_part(): pl.pallas_call(functools.partial(map_kernel, shape), out_shape=jax.ShapeD...  50.7 us
    pallas_call x1, Pallas kernels, whole_part(): pl.pallas_call(write_kernel, grid=(owner_rows // (OUT_TILES * LANES),), o...  19.9 us
    ppermute x7, starting transfers between devices, whole_part(): lax.ppermute(tables, ('det', 'wafer'), [(i, (i + shift) % chips) for i in...  14.2 us
    pallas_call x1, Pallas kernels, whole_part(): pl.pallas_call(functools.partial(twin_kernel, shape), out_shape=[jax.Shap...  9.19 us
    pallas_call x1, Pallas kernels, whole_part(): pl.pallas_call(functools.partial(place_kernel, shape), out_shape=[jax.Sha...  9.05 us
    ppermute x6, starting transfers between devices, along_det(): lax.ppermute(block, 'det', [(i, (i + shift) % dets) for i in range(dets)])  8.29 us
    ppermute x2, starting transfers between devices, other_wafer(): return lax.ppermute(here, 'wafer', swap)  2.79 us
  transfers between devices with their start and end apart: 17, of which 4 were waited for; matrix products, arithmetic and copies ran while one was open for 2% of the time, Pallas kernels for 14%

commit v1 on v0

--- a/solution.py
+++ b/solution.py
@@ -194,7 +194,7 @@
 
 def pack_kernel(
     shape, angle_ref, tod_ref, row_ref, hit_ref, group_ref, base_ref, coef_ref, lag_ref,
-    table_ref, angle_rows_ref, tod_rows_ref,
+    angle_rows_ref, tod_rows_ref,
 ):
     wafers, dets, reps, tiles, owners, capacity, owner_rows, lag_count = shape
     lane, sub = tile_iotas()
@@ -221,10 +221,10 @@
         lag = lag_ref[j : j + 1, :].astype(jnp.float32)
         whole = whole + pltpu.roll(spread(lag, ROWS), at, 1)
     table = jnp.where(sub == 0, wide(ids), jnp.where(sub == 1, wide(floats), wide(whole)))
-    table_ref[:, 0:LANES] = table
-    table_ref[:, LANES : 2 * LANES] = spread(lists.astype(jnp.float32), capacity)
+    angle_rows_ref[ROWS, 0:ROWS, :] = table
+    angle_rows_ref[ROWS, ROWS : 2 * ROWS, :] = spread(lists.astype(jnp.float32), capacity)
     for b in range(tiles):
-        angle_rows_ref[:, b, :] = angle_ref[:, b * LANES : (b + 1) * LANES]
+        angle_rows_ref[0:ROWS, b, :] = angle_ref[:, b * LANES : (b + 1) * LANES]
         tod_rows_ref[:, b, :] = tod_ref[:, b * LANES : (b + 1) * LANES]
 
 
@@ -249,17 +249,21 @@
     return copies
 
 
-def table_copies(shape, self_ref, refs, part_ref, sem):
+def table_copies(shape, self_ref, source_ref, part_ref, sem):
     wafers, dets, reps = shape[:3]
-    chips = wafers * dets
-    here = self_ref[1] * wafers + self_ref[0]
     copies = []
-    for shift, ref in enumerate(refs):
-        chip = here - shift
-        chip = jnp.where(chip < 0, chip + chips, chip)
-        team = lax.rem(chip, wafers) * dets + lax.div(chip, wafers)
-        to = part_ref.at[pl.ds(team * reps, reps)]
-        copies.append(pltpu.make_async_copy(ref, to, sem.at[shift]))
+    for rep in range(reps):
+        for swap_wafer in range(wafers):
+            for shift in range(dets):
+                det = self_ref[1] - shift
+                det = jnp.where(det < 0, det + dets, det)
+                device = ((self_ref[0] ^ swap_wafer) * dets + det) * reps + rep
+                copies.append(
+                    pltpu.make_async_copy(
+                        source_ref.at[rep, swap_wafer, shift], part_ref.at[device],
+                        sem.at[len(copies)],
+                    )
+                )
     for copy in copies:
         copy.start()
     for copy in copies:
@@ -273,33 +277,40 @@
     )
 
 
-def twin_kernel(shape, self_ref, *refs):
+def twin_kernel(
+    shape, self_ref, table_ref, weight_ref, float_ref, whole_ref, size_ref, pair_ref, group_ref,
+    part_ref, code_ref, lead_ref, part_sem,
+):
     wafers, dets, reps, tiles, owners, capacity, owner_rows, lag_count = shape
     devices = wafers * dets * reps
     total = devices * LANES
-    table_refs, refs = refs[: wafers * dets], refs[wafers * dets :]
-    weight_ref, float_ref, whole_ref, size_ref, pair_ref, group_ref = refs[:6]
-    part_ref, code_ref, lead_ref, part_sem = refs[6:]
+    per_tile = LANES // tiles
     lane, sub = tile_iotas()
     lane_f = lane.astype(jnp.float32)
-    table_copies(shape, self_ref, table_refs, part_ref, part_sem)
+    table_copies(shape, self_ref, table_ref, part_ref, part_sem)
+    none = jnp.full((ROWS, LANES), BIG, jnp.float32)
+    for tile in range(devices // per_tile):
+        code_ref[tile] = none
+        lead_ref[tile] = none
 
     def survey(device, carry):
-        float_ref[pl.ds(device, 1), :] = part_ref[device, 1:2, 0:LANES]
-        whole_ref[pl.ds(device, 1), :] = part_ref[device, 2:3, 0:LANES].astype(jnp.int32)
-        ids = jnp.broadcast_to(part_ref[device, 0:1, 0:LANES], (LANES, LANES)).T
+        float_ref[pl.ds(device, 1), :] = part_ref[device, 0, 1:2, :]
+        whole_ref[pl.ds(device, 1), :] = part_ref[device, 0, 2:3, :].astype(jnp.int32)
+        ids = jnp.broadcast_to(part_ref[device, 0, 0:1, :], (LANES, LANES)).T
         ids = [ids[j * ROWS : (j + 1) * ROWS] for j in range(tiles)]
 
-        def compare(other, state):
+        def compare(step, state):
             key, least = state
-            row = wide(part_ref[other, 0:1, 0:LANES])
-            least = [
-                jnp.minimum(least[j], jnp.where(ids[j] == row, key, BIG)) for j in range(tiles)
-            ]
-            return key + LANES, least
-
-        none = jnp.full((ROWS, LANES), BIG, jnp.float32)
-        _, least = lax.fori_loop(0, device + 1, compare, (lane_f, [none] * tiles))
+            for k in range(2):
+                row = wide(part_ref[2 * step + k, 0, 0:1, :])
+                least = [
+                    jnp.minimum(least[j], jnp.where(ids[j] == row, key, BIG)) for j in range(tiles)
+                ]
+                key = key + LANES
+            return key, least
+
+        steps = lax.shift_right_logical(device, 1) + 1
+        _, least = lax.fori_loop(0, steps, compare, (lane_f, [none] * tiles))
         codes, leads = none, none
         for j in range(tiles):
             lead = jnp.min(least[j], axis=1, keepdims=True)
@@ -308,16 +319,18 @@
             later = lead < mine
             leads = jnp.where(lane == j, jnp.where(later, lead, BIG), leads)
             codes = jnp.where(lane == j, jnp.where(later, mine * float(total) + lead, BIG), codes)
-        code_ref[device] = codes
-        lead_ref[device] = leads
+        tile, part = lax.div(device, per_tile), lax.rem(device, per_tile)
+        inside = lax.shift_right_logical(lane, tiles.bit_length() - 1) == part
+        for ref, found in ((code_ref, codes), (lead_ref, leads)):
+            ref[tile] = jnp.where(inside, pltpu.roll(found, part * tiles, 1), ref[tile])
         return carry
 
     lax.fori_loop(0, devices, survey, 0)
 
     def next_code(last):
         found = jnp.full((ROWS, LANES), BIG, jnp.float32)
-        for device in range(devices):
-            codes = code_ref[device]
+        for tile in range(devices // per_tile):
+            codes = code_ref[tile]
             found = jnp.minimum(found, jnp.where(codes > last, codes, BIG))
         return jnp.min(found)
 
@@ -333,8 +346,8 @@
         shift = (3 * (detector(key) - detector(lead))) & (PBLOCK - 1)
         wanted = lead.astype(jnp.float32)
         same = jnp.zeros((ROWS, LANES), jnp.float32)
-        for device in range(devices):
-            same = same + jnp.where(lead_ref[device] == wanted, 1.0, 0.0)
+        for tile in range(devices // per_tile):
+            same = same + jnp.where(lead_ref[tile] == wanted, 1.0, 0.0)
         alone = jnp.sum(same) < 1.5
         entry = twin_entry(key, lead, shift)
         pair_ref[pairs] = entry
@@ -366,39 +379,39 @@
     return entry >> 19, (entry >> 6) & ((1 << 13) - 1), entry & (PBLOCK - 1)
 
 
-def place_kernel(shape, self_ref, *refs):
+def place_kernel(
+    shape, self_ref, table_ref, place_ref, start_ref, move_ref, part_ref, rank_ref, hits_ref,
+    part_sem,
+):
     wafers, dets, reps, tiles, owners, capacity, owner_rows, lag_count = shape
     devices = wafers * dets * reps
     slots = devices * capacity
-    table_refs, refs = refs[: wafers * dets], refs[wafers * dets :]
-    place_ref, start_ref, move_ref = refs[:3]
-    part_ref, rank_ref, hits_ref, rank_smem, hits_smem, part_sem, table_sem = refs[3:]
     lane, sub = tile_iotas()
     own = self_ref[1] * wafers + self_ref[0]
     first_row = (own * owner_rows).astype(jnp.float32)
-    table_copies(shape, self_ref, table_refs, part_ref, part_sem)
+    table_copies(shape, self_ref, table_ref, part_ref, part_sem)
     depth = 2 * LANES
     tall = lax.broadcasted_iota(jnp.int32, (depth, LANES), 0).astype(jnp.float32)
 
     def one_hots(device):
-        local_row = part_ref[device, 0:1, 0:LANES] - first_row
+        local_row = part_ref[device, 0, 0:1, :] - first_row
         high = jnp.floor(local_row * (1.0 / LANES))
         low = local_row - high * LANES
         high = (jnp.broadcast_to(high, (depth, LANES)) == tall).astype(jnp.float32)
         low = (jnp.broadcast_to(low, (LANES, LANES)) == tall[0:LANES]).astype(jnp.float32)
         return high, low
 
-    def survey(pair, hits):
-        for k in range(2):
-            device = 2 * pair + k
-            own_hits = jnp.where(sub == own, part_ref[device, :, LANES : 2 * LANES], 0.0)
+    def survey(batch, hits):
+        for k in range(4):
+            device = 4 * batch + k
+            own_hits = jnp.where(sub == own, part_ref[device, 1], 0.0)
             own_hits = jnp.sum(own_hits, axis=0, keepdims=True)
             hits_ref[pl.ds(device, 1), :] = own_hits.astype(jnp.int32)
             high, low = one_hots(device)
             hits = hits + exact_dot(high, low, ((1,), (1,)))
         return hits
 
-    hits = lax.fori_loop(0, devices // 2, survey, jnp.zeros((depth, LANES), jnp.float32))
+    hits = lax.fori_loop(0, devices // 4, survey, jnp.zeros((depth, LANES), jnp.float32))
     full = jnp.minimum(hits, 1.0)
 
     def ordered(size, axis):
@@ -414,9 +427,9 @@
     place_high = jnp.floor(place * (1.0 / LANES))
     place_parts = jnp.concatenate([place_high, place - place_high * LANES], axis=0)
 
-    def rank_of(pair, carry):
-        for k in range(2):
-            device = 2 * pair + k
+    def rank_of(batch, carry):
+        for k in range(4):
+            device = 4 * batch + k
             high, low = one_hots(device)
             parts = exact_dot(place_parts, low)
             rank = high * (parts[0:depth] * LANES + parts[depth : 2 * depth])
@@ -424,26 +437,15 @@
             rank_ref[pl.ds(device, 1), :] = rank.astype(jnp.int32)
         return carry
 
-    lax.fori_loop(0, devices // 2, rank_of, 0)
-    copies = (
-        pltpu.make_async_copy(rank_ref, rank_smem, table_sem.at[0]),
-        pltpu.make_async_copy(hits_ref, hits_smem, table_sem.at[1]),
-    )
-    for copy in copies:
-        copy.start()
-    for copy in copies:
-        copy.wait()
-
-    def pick(device, carry):
-        for c in range(capacity):
-            number = hits_smem[device, c]
-            valid = number < LANES
-            number = number & (LANES - 1)
-            target = jnp.where(valid, rank_smem[device, number], slots + LANES)
-            move_ref[device * capacity + c] = target * (1 << 16) + device * LANES + number
-        return carry
-
-    lax.fori_loop(0, devices, pick, 0)
+    lax.fori_loop(0, devices // 4, rank_of, 0)
+    for tile in range(devices // ROWS):
+        rows = slice(tile * ROWS, (tile + 1) * ROWS)
+        number = hits_ref[rows, :]
+        valid = number < LANES
+        number = number & (LANES - 1)
+        rank = jnp.take_along_axis(rank_ref[rows, :], number, axis=1, mode="promise_in_bounds")
+        target = jnp.where(valid, rank, slots + LANES)
+        move_ref[rows, :] = target * (1 << 16) + (tile * ROWS + sub) * LANES + number
 
 
 def map_kernel(
@@ -607,7 +609,7 @@
                     first_sums[wafer][group, rows_of(octet), :] += stream
             return carry
 
-        carry = loop(wafer_dets, one_detector, carry, 2)
+        carry = loop(wafer_dets, one_detector, carry, 4)
         average(first_sums)
         return carry
 
@@ -641,7 +643,7 @@
                     carry = carry + here * result
             return carry
 
-        product = loop(wafer_dets, one_filter, zero, 1)
+        product = loop(wafer_dets, one_filter, zero, 2)
         average(second_sums)
         return product
 
@@ -658,7 +660,7 @@
                     target[at, 2] = fold(sin_ref[at] * stream)
             return carry
 
-        loop(wafer_dets, one_return, 0, 2)
+        loop(wafer_dets, one_return, 0, 4)
         merge_twins(target)
 
     merge_twins(image_map)
@@ -714,7 +716,7 @@
                     parts = parts + residual * (inverse_ref[at, c] * residual)
                 return carry + weight_ref[at] * parts
 
-            next_energy = whole_sum(loop(count, update, zero, 8))
+            next_energy = whole_sum(loop(count, update, zero, 16))
             factor = next_energy / energy
             energy = next_energy
         else:
@@ -742,7 +744,7 @@
 
     def pick(device, carry):
         for c in range(capacity):
-            move = move_ref[device * capacity + c]
+            move = move_ref[device, c]
             source, target = move & ((1 << 16) - 1), move >> 16
             sorted_ref[pl.ds(target, 1), :] = rows_ref[pl.ds(source, 1), :]
         return carry
@@ -764,44 +766,31 @@
 def write_kernel(start_ref, column_ref, place_ref, x_ref, r_ref):
     height = 3 * PBLOCK
     depth = lax.broadcasted_iota(jnp.int32, (LANES, LANES), 0)
-    step = pl.program_id(0) * OUT_TILES
-
-    def spread(group, tile):
+    group = pl.program_id(0) * OUT_TILES
+    start, end = start_ref[0, group], start_ref[0, group + OUT_TILES]
+    first = lax.shift_right_logical(start, 7)
+    last = lax.shift_right_logical(jnp.maximum(end - 1, start), 7)
+
+    def spread(tile):
         chosen = []
-        for k in range(2):
+        for k in range(OUT_TILES):
             place = jnp.broadcast_to(place_ref[pl.ds(group + k, 1), :], (LANES, LANES))
             chosen.append(jnp.where(place == depth + tile * LANES, 1.0, 0.0).astype(jnp.bfloat16))
         chosen = jnp.concatenate(chosen, axis=1)
         chosen = jnp.concatenate([chosen, chosen], axis=0)
         return jnp.dot(column_ref[tile], chosen, preferred_element_type=jnp.float32)
 
-    def tiles_of(group):
-        start, end = start_ref[0, group], start_ref[0, group + 2]
-        first = lax.shift_right_logical(start, 7)
-        return first, lax.shift_right_logical(jnp.maximum(end - 1, start), 7)
-
-    further = 0
-    for pair in range(OUT_TILES // 2):
-        first, last = tiles_of(step + 2 * pair)
-        further = further + (last - first)
-        values = spread(step + 2 * pair, first)
-        columns = slice(pair * 2 * LANES, (pair + 1) * 2 * LANES)
-        x_ref[:, columns] = values[:height]
-        r_ref[:, columns] = values[height:]
-
-    @pl.when(further > 0)
-    def _():
-        for pair in range(OUT_TILES // 2):
-            first, last = tiles_of(step + 2 * pair)
-            columns = slice(pair * 2 * LANES, (pair + 1) * 2 * LANES)
-
-            def add_tile(tile, carry):
-                values = spread(step + 2 * pair, tile)
-                x_ref[:, columns] += values[:height]
-                r_ref[:, columns] += values[height:]
-                return carry
-
-            lax.fori_loop(first + 1, last + 1, add_tile, 0)
+    values = spread(first)
+    x_ref[...] = values[:height]
+    r_ref[...] = values[height:]
+
+    def add_tile(tile, carry):
+        values = spread(tile)
+        x_ref[...] += values[:height]
+        r_ref[...] += values[height:]
+        return carry
+
+    lax.fori_loop(first + 1, last + 1, add_tile, 0)
 
 
 def part_shape(sizes, tod, hit_list, band_lag):
@@ -828,7 +817,8 @@
         and capacity <= LANES
         and devices * capacity % LANES == 0
         and owner_rows % (LANES * OUT_TILES) == 0
-        and groups + 2 <= 2 * LANES
+        and groups + 1 <= 2 * LANES
+        and devices % ROWS == 0
         and total * total < BIG
     )
 
@@ -861,37 +851,33 @@
     def other_rep(here, across):
         return here, across, lax.ppermute(jnp.stack([here, across]), "rep", swap)
 
-    tables, angles, samples = pl.pallas_call(
+    angles, samples = pl.pallas_call(
         functools.partial(pack_kernel, shape),
         out_shape=[
-            jax.ShapeDtypeStruct((ROWS, 2 * LANES), f32),
-            jax.ShapeDtypeStruct((ROWS, tiles, LANES), f32),
+            jax.ShapeDtypeStruct((ROWS + 1, tiles, LANES), f32),
             jax.ShapeDtypeStruct((ROWS, tiles, LANES), f32),
         ],
         in_specs=[vmem] * 8,
-        out_specs=[vmem] * 3,
+        out_specs=[vmem] * 2,
         compiler_params=params,
         name="pack",
     )(
         psi[0], tod[0], point_row[0], hit_list[0, 0, 0], group_id, a_zero, band_coef[0].T,
         band_lag[0].T,
     )
-    angles, samples = (stream.reshape(tiles, ROWS, LANES) for stream in (angles, samples))
+    angles = angles.reshape(tiles + 2, ROWS, LANES)
+    samples = samples.reshape(tiles, ROWS, LANES)
     place_here = jnp.stack([lax.axis_index(axis) for axis in ("wafer", "det", "rep")]).astype(i32)
-    chips = wafers * dets
-    tables = lax.all_gather(tables, "rep", axis=0, tiled=False)
-    angles, tables = lax.optimization_barrier((angles, tables))
-    tables = [tables] + [
-        lax.ppermute(tables, ("det", "wafer"), [(i, (i + shift) % chips) for i in range(chips)])
-        for shift in range(1, chips)
-    ]
-    samples, angles, *tables = lax.optimization_barrier(
-        (samples, jnp.stack(along_det(angles)), *tables)
-    )
+    angles = along_det(angles)
+    tables = jnp.stack([block[tiles:] for block in angles])
+    angles = jnp.stack([block[:tiles] for block in angles])
+    tables = jnp.stack([tables, other_wafer(tables)])
+    samples, angles, tables = lax.optimization_barrier((samples, angles, tables))
     angles_across = other_wafer(angles)
     samples = jnp.stack(along_det(samples))
-    table_scratch = pltpu.VMEM((devices, ROWS, 2 * LANES), f32)
-    table_sem = pltpu.SemaphoreType.DMA((chips,))
+    tables = lax.all_gather(tables, "rep", axis=0, tiled=False)
+    table_scratch = pltpu.VMEM((devices, 2, ROWS, LANES), f32)
+    table_sem = pltpu.SemaphoreType.DMA((devices,))
     twins = pl.pallas_call(
         functools.partial(twin_kernel, shape),
         out_shape=[
@@ -902,18 +888,18 @@
             jax.ShapeDtypeStruct((total,), i32),
             jax.ShapeDtypeStruct((total,), i32),
         ],
-        in_specs=[smem] + [anywhere] * chips,
+        in_specs=[smem, anywhere],
         out_specs=[vmem] * 3 + [smem] * 3,
         scratch_shapes=[
             table_scratch,
-            pltpu.VMEM((devices, ROWS, LANES), f32),
-            pltpu.VMEM((devices, ROWS, LANES), f32),
+            pltpu.VMEM((devices * tiles // LANES, ROWS, LANES), f32),
+            pltpu.VMEM((devices * tiles // LANES, ROWS, LANES), f32),
             table_sem,
         ],
         compiler_params=params,
         cost_estimate=pl.CostEstimate(flops=10**9, bytes_accessed=3 * 10**7, transcendentals=0),
         name="twins",
-    )(place_here, *tables)
+    )(place_here, tables)
     angles, angles_across, samples, tables, twins = lax.optimization_barrier(
         (angles, angles_across, samples, tables, twins)
     )
@@ -924,27 +910,24 @@
         out_shape=[
             jax.ShapeDtypeStruct((2 * LANES, LANES), i32),
             jax.ShapeDtypeStruct((ROWS, 2 * LANES), i32),
-            jax.ShapeDtypeStruct((slots,), i32),
+            jax.ShapeDtypeStruct((devices, LANES), i32),
         ],
-        in_specs=[smem] + [anywhere] * chips,
-        out_specs=[vmem, vmem, smem],
+        in_specs=[smem, anywhere],
+        out_specs=[vmem, vmem, vmem],
         scratch_shapes=[
             table_scratch,
             pltpu.VMEM((devices, LANES), i32),
             pltpu.VMEM((devices, LANES), i32),
-            pltpu.SMEM((devices, LANES), i32),
-            pltpu.SMEM((devices, LANES), i32),
             table_sem,
-            pltpu.SemaphoreType.DMA((2,)),
         ],
         compiler_params=params,
         cost_estimate=pl.CostEstimate(flops=10**9, bytes_accessed=2 * 10**7, transcendentals=0),
         name="places",
-    )(place_here, *tables)
+    )(place_here, tables)
+    angles, angles_across, samples, samples_across, place, start, moves = lax.optimization_barrier(
+        (angles, angles_across, samples, samples_across, place, start, moves)
+    )
     angle_blocks = other_rep(angles, angles_across)
-    samples, samples_across, place, start, moves = lax.optimization_barrier(
-        (samples, samples_across, place, start, moves)
-    )
     sample_blocks = other_rep(samples, samples_across)
     stream = pltpu.VMEM((count, ROWS, LANES), f32)
     sky = pltpu.VMEM((count, 3, ROWS, LANES), f32)

time: 128 us -> 112 us (0.88)
  Pallas kernels: 90.5 us -> 77.9 us
  starting transfers between devices: 26 us -> 14.3 us
  waiting for transfers between devices: 3.86 us -> 11.9 us
  local copies, waits for them, and re-layouts: 0.86 us -> 2.45 us
    ppermute x7 -> x0, starting transfers between devices: 14.2 us -> none  [whole_part(): lax.ppermute(tables, ('det', 'wafer'), [(i, (i + shift) % chips) for i in...]
    pallas_call x1, Pallas kernels: 50.7 us -> 42 us  [whole_part(): pl.pallas_call(functools.partial(map_kernel, shape), out_shape=jax.ShapeD...]
    ppermute x2 -> x3, waiting for transfers between devices: 0.01 us -> 5.21 us  [other_wafer(): return lax.ppermute(here, 'wafer', swap)]
    ppermute x6, waiting for transfers between devices: 0.02 us -> 4.63 us  [along_det(): lax.ppermute(block, 'det', [(i, (i + shift) % dets) for i in range(dets)])]
    pallas_call x1, Pallas kernels: 9.05 us -> 4.97 us  [whole_part(): pl.pallas_call(functools.partial(place_kernel, shape), out_shape=[jax.Sha...]
    ppermute x7 -> x0, waiting for transfers between devices: 2.31 us -> none  [whole_part(): lax.ppermute(tables, ('det', 'wafer'), [(i, (i + shift) % chips) for i in...]
    ppermute x6, starting transfers between devices: 8.29 us -> 10 us  [along_det(): lax.ppermute(block, 'det', [(i, (i + shift) % dets) for i in range(dets)])]
    ppermute x2 -> x3, starting transfers between devices: 2.79 us -> 3.65 us  [other_wafer(): return lax.ppermute(here, 'wafer', swap)]
  transfers between devices with their start and end apart: 17 -> 11, of which waited for: 4 -> 6; matrix products, arithmetic and copies ran while one was open for 2% -> 3% of each run, Pallas kernels for 14% -> 13%
where the time goes in v1:
time: 112 us; the launch traced here: 111 us
  Pallas kernels  77.9 us (70%)
  starting transfers between devices  14.3 us (13%)
  waiting for transfers between devices  11.9 us (11%)
  local copies, waits for them, and re-layouts  2.45 us (2%)
  blocking collectives  2.02 us (2%)
  other arithmetic  1.52 us (1%)
    pallas_call x1, Pallas kernels, whole_part(): pl.pallas_call(functools.partial(map_kernel, shape), out_shape=jax.ShapeD...  42 us
    pallas_call x1, Pallas kernels, whole_part(): pl.pallas_call(write_kernel, grid=(owner_rows // (OUT_TILES * LANES),), o...  20.2 us
    ppermute x6, starting transfers between devices, along_det(): lax.ppermute(block, 'det', [(i, (i + shift) % dets) for i in range(dets)])  10 us
    pallas_call x1, Pallas kernels, whole_part(): pl.pallas_call(functools.partial(twin_kernel, shape), out_shape=[jax.Shap...  9.02 us
    ppermute x3, waiting for transfers between devices, other_wafer(): return lax.ppermute(here, 'wafer', swap)  5.21 us
    pallas_call x1, Pallas kernels, whole_part(): pl.pallas_call(functools.partial(place_kernel, shape), out_shape=[jax.Sha...  4.97 us
    ppermute x6, waiting for transfers between devices, along_det(): lax.ppermute(block, 'det', [(i, (i + shift) % dets) for i in range(dets)])  4.63 us
    ppermute x3, starting transfers between devices, other_wafer(): return lax.ppermute(here, 'wafer', swap)  3.65 us
  transfers between devices with their start and end apart: 11, of which 6 were waited for; matrix products, arithmetic and copies ran while one was open for 3% of the time, Pallas kernels for 13%

profile of v1, /device:TPU:0, one launch (start us, length us, event | category | flops | bytes accessed | tf_op | source)
XLA Modules:
  0.0 110.8 jit_solution(13031006312588878825)
XLA Ops:
  0.6 1.7 %pack.1 = (f32[9,16,128]{2,1,0:T(8,128)}, f32[8,16,128]{2,1,0:T(8,128)}) custom-call(f32[8,2048]{1,0:T(8,128)} %bitcast.54, f32[8,2048]{1,0:T(8,128)} %bitcast.55, s32[8,16]{1,0:T(8,128)} %bitcast.64, s32[8,32]{1,0:T(8,128)} %bitcast.65, s32[1,8]{1,0:T(1,128)} %group_ref.1, f32[1,8]{1,0:T(1,128)} %base_ref.1, f32[4,8]{1,0:T(4,128)} %bitcast.66, s32[4,8]{1,0:T(4,128)} %bitcast.67), custom_call_target="tpu_custom_call" | custom-call | tf_op jit(solution)/shard_map/pack/pallas_call | solution.py:854
  2.3 5.0 %collective-permute-start.2 = (f32[18,8,128]{2,1,0:T(8,128)}, f32[18,8,128]{2,1,0:T(8,128)S(1)}, u32[]{:S(2)}, u32[]{:S(2)}) collective-permute-start(f32[18,8,128]{2,1,0:T(8,128)} %bitcast.51), channel_id=1, source_target_pairs={{0,12},{4,0},{8,4},{12,8},{1,13},{5,1},{9,5},{13,9},{2,14},{6,2},{... | collective-permute-start | bytes 221192 | tf_op jit(solution)/shard_map/ppermute | solution.py:843
  7.4 1.0 collective-permute-start
  8.4 0.7 slice_bitcast_fusion.6
  9.1 0.8 slice.26
  10.4 4.2 %collective-permute-done.1 = f32[18,8,128]{2,1,0:T(8,128)S(1)} collective-permute-done((f32[18,8,128]{2,1,0:T(8,128)}, f32[18,8,128]{2,1,0:T(8,128)S(1)}, u32[]{:S(2)}, u32[]{:S(2)}) %collective-permute-start.1) | collective-permute-done | bytes 73760 | tf_op jit(solution)/shard_map/ppermute | solution.py:843
  14.6 1.6 %collective-permute-start.3 = (f32[4,2,8,128]{3,2,1,0:T(8,128)S(1)}, f32[4,2,8,128]{3,2,1,0:T(8,128)S(1)}, u32[]{:S(2)}, u32[]{:S(2)}) collective-permute-start(f32[4,2,8,128]{3,2,1,0:T(8,128)S(1)} %get-tuple-element.69), channel_id=1, source_target_pairs={{0,2},{2,0},{1,3},{3,1},{4,6},{6,4},{5,7},{7,5},{8,10},{10,8},{9,1... | collective-permute-start | bytes 98312 | tf_op jit(solution)/shard_map/ppermute | solution.py:849
  16.2 2.4 %collective-permute-done.3 = f32[4,2,8,128]{3,2,1,0:T(8,128)S(1)} collective-permute-done((f32[4,2,8,128]{3,2,1,0:T(8,128)S(1)}, f32[4,2,8,128]{3,2,1,0:T(8,128)S(1)}, u32[]{:S(2)}, u32[]{:S(2)}) %collective-permute-start.3) | collective-permute-done | bytes 32800 | tf_op jit(solution)/shard_map/ppermute | solution.py:849
  18.6 1.5 %collective-permute-start.4 = (f32[4,16,8,128]{3,2,1,0:T(8,128)S(1)}, f32[4,16,8,128]{3,2,1,0:T(8,128)S(1)}, u32[]{:S(2)}, u32[]{:S(2)}) collective-permute-start(f32[4,16,8,128]{3,2,1,0:T(8,128)S(1)} %pad_maximum_fusion.2.angle_here_ref), channel_id=1, source_target_pairs={{0,2},{2,0},{1,3},{3,1},{4,6},{6,4},{5,7},{7,5},{8,10},{10,8},{9,1... | collective-permute-start | bytes 786440 | tf_op jit(solution)/shard_map/ppermute | solution.py:849
  20.1 0.6 pad_add_fusion.self_ref
  20.6 2.3 %collective-permute-start.7 = (f32[16,8,128]{2,1,0:T(8,128)}, f32[16,8,128]{2,1,0:T(8,128)S(1)}, u32[]{:S(2)}, u32[]{:S(2)}) collective-permute-start(f32[16,8,128]{2,1,0:T(8,128)} %bitcast.56), channel_id=1, source_target_pairs={{0,12},{4,0},{8,4},{12,8},{1,13},{5,1},{9,5},{13,9},{2,14},{6,2},{... | collective-permute-start | bytes 196616 | tf_op jit(solution)/shard_map/ppermute | solution.py:843
  23.0 1.6 %collective-permute-start.5 = (f32[16,8,128]{2,1,0:T(8,128)}, f32[16,8,128]{2,1,0:T(8,128)S(1)}, u32[]{:S(2)}, u32[]{:S(2)}) collective-permute-start(f32[16,8,128]{2,1,0:T(8,128)} %bitcast.58), channel_id=1, source_target_pairs={{0,4},{4,8},{8,12},{12,0},{1,5},{5,9},{9,13},{13,1},{2,6},{6,10},{... | collective-permute-start | bytes 196616 | tf_op jit(solution)/shard_map/ppermute | solution.py:843
  24.6 2.0 %all-gather = f32[4,4,2,8,128]{4,3,2,1,0:T(8,128)} all-gather(f32[2,4,2,8,128]{4,3,2,1,0:T(8,128)S(1)} %pad_maximum_fusion.4), channel_id=2, replica_groups=mesh['groups'=2,'det'=4,'wafer'=2,'rep'=2] {'rep'}, dimensions={0}, use_global_device_ids=true | all-gather | bytes 196608 | tf_op jit(solution)/shard_map/all_gather | solution.py:878
  26.6 9.0 %twins.1 = (f32[256,8,128]{2,1,0:T(8,128)}, f32[16,128]{1,0:T(8,128)}, s32[16,128]{1,0:T(8,128)}, s32[2]{0:T(128)}, s32[2048]{0:T(1024)}, /*index=5*/s32[2048]{0:T(1024)}) custom-call(s32[3]{0:T(128)} %pad_add_fusion.self_ref, f32[2,2,4,2,8,128]{5,4,3,2,1,0:T(8,128)} %bitcast.49), custom_call_target="tpu_custom_call" | custom-call | flops 1000000000 | bytes 30000000 | tf_op jit(solution)/shard_map/twins/pallas_call | solution.py:881
  35.7 0.9 pad_maximum_fusion.3.tod_here_ref
  36.6 0.6 collective-permute-start.8
  37.2 5.0 %places.1 = (s32[256,128]{1,0:T(8,128)}, s32[8,256]{1,0:T(8,128)}, s32[16,128]{1,0:T(8,128)}) custom-call(s32[3]{0:T(128)} %pad_add_fusion.self_ref, f32[2,2,4,2,8,128]{5,4,3,2,1,0:T(8,128)} %bitcast.50), custom_call_target="tpu_custom_call" | custom-call | flops 1000000000 | bytes 20000000 | tf_op jit(solution)/shard_map/places/pallas_call | solution.py:908
  42.1 2.9 %collective-permute-done.8.tod_across_ref = f32[4,16,8,128]{3,2,1,0:T(8,128)S(1)} collective-permute-done((f32[4,16,8,128]{3,2,1,0:T(8,128)S(1)}, f32[4,16,8,128]{3,2,1,0:T(8,128)S(1)}, u32[]{:S(2)}, u32[]{:S(2)}) %collective-permute-start.8) | collective-permute-done | bytes 262176 | tf_op jit(solution)/shard_map/ppermute | solution.py:849
  45.1 0.6 collective-permute-start.10
  45.7 1.3 %collective-permute-done.9.angle_other_ref = f32[2,4,16,8,128]{4,3,2,1,0:T(8,128)S(1)} collective-permute-done((f32[2,4,16,8,128]{4,3,2,1,0:T(8,128)S(1)}, f32[2,4,16,8,128]{4,3,2,1,0:T(8,128)S(1)}, u32[]{:S(2)}, u32[]{:S(2)}) %collective-permute-start.9) | collective-permute-done | bytes 524320 | tf_op jit(solution)/shard_map/ppermute | solution.py:852
  47.0 0.7 collective-permute-done.10.tod_other_ref
  47.8 0.8 copy-done.5
  48.6 42.0 %map_maker.1.column_ref = bf16[5,384,256]{2,1,0:T(8,128)(2,1)} custom-call(s32[3]{0:T(128)} %pad_add_fusion.self_ref, s32[2]{0:T(128)} %get-tuple-element.54.size_ref, s32[2048]{0:T(1024)} %get-tuple-element.55.pair_ref, s32[2048]{0:T(1024)} %get-tuple-element.56.group_ref, s32[16,128]{1,0:T(8,128)} %get-tuple-element.57.move_ref, ...), custom_call_target="tpu_custom_call" | custom-call | tf_op jit(solution)/shard_map/map_maker/pallas_call | solution.py:936
  90.6 20.2 %write.1 = (f32[192,24576]{1,0:T(8,128)}, f32[192,24576]{1,0:T(8,128)}) custom-call(s32[8,256]{1,0:T(8,128)} %get-tuple-element.53.start_ref, bf16[5,384,256]{2,1,0:T(8,128)(2,1)} %map_maker.1.column_ref, s32[256,128]{1,0:T(8,128)} %get-tuple-element.65.place_ref), custom_call_target="tpu_custom_call" | custom-call | tf_op jit(solution)/shard_map/write/pallas_call | solution.py:959
  (31 shorter events, 0.7 us)
Async XLA Ops:
  2.3 8.1 %collective-permute-start.2 = (f32[18,8,128]{2,1,0:T(8,128)}, f32[18,8,128]{2,1,0:T(8,128)S(1)}, u32[]{:S(2)}, u32[]{:S(2)}) collective-permute-start(f32[18,8,128]{2,1,0:T(8,128)} %bitcast.51), channel_id=1, source_target_pairs={{0,12},{4,0},{8,4},{12,8},{1,13},{5,1},{9,5},{13,9},{2,14},{6,2},{... | collective-permute-start | bytes 221192 | tf_op jit(solution)/shard_map/ppermute | solution.py:843
  7.4 7.2 %collective-permute-start.1 = (f32[18,8,128]{2,1,0:T(8,128)}, f32[18,8,128]{2,1,0:T(8,128)S(1)}, u32[]{:S(2)}, u32[]{:S(2)}) collective-permute-start(f32[18,8,128]{2,1,0:T(8,128)} %bitcast.52), channel_id=1, source_target_pairs={{0,8},{4,12},{8,0},{12,4},{1,9},{5,13},{9,1},{13,5},{2,10},{6,14},... | collective-permute-start | bytes 221192 | tf_op jit(solution)/shard_map/ppermute | solution.py:843
  7.4 7.2 %collective-permute-start = (f32[18,8,128]{2,1,0:T(8,128)}, f32[18,8,128]{2,1,0:T(8,128)S(1)}, u32[]{:S(2)}, u32[]{:S(2)}) collective-permute-start(f32[18,8,128]{2,1,0:T(8,128)} %bitcast.53), channel_id=1, source_target_pairs={{0,4},{4,8},{8,12},{12,0},{1,5},{5,9},{9,13},{13,1},{2,6},{6,10},{... | collective-permute-start | bytes 221192 | tf_op jit(solution)/shard_map/ppermute | solution.py:843
  14.6 4.0 %collective-permute-start.3 = (f32[4,2,8,128]{3,2,1,0:T(8,128)S(1)}, f32[4,2,8,128]{3,2,1,0:T(8,128)S(1)}, u32[]{:S(2)}, u32[]{:S(2)}) collective-permute-start(f32[4,2,8,128]{3,2,1,0:T(8,128)S(1)} %get-tuple-element.69), channel_id=1, source_target_pairs={{0,2},{2,0},{1,3},{3,1},{4,6},{6,4},{5,7},{7,5},{8,10},{10,8},{9,1... | collective-permute-start | bytes 98312 | tf_op jit(solution)/shard_map/ppermute | solution.py:849
  16.2 31.5 %copy-start = (f32[4,16,8,128]{3,2,1,0:T(8,128)}, f32[4,16,8,128]{3,2,1,0:T(8,128)S(1)}, u32[]{:S(2)}) copy-start(f32[4,16,8,128]{3,2,1,0:T(8,128)S(1)} %pad_maximum_fusion.2.angle_here_ref) | copy-start | bytes 786436
  18.6 17.9 %collective-permute-start.4 = (f32[4,16,8,128]{3,2,1,0:T(8,128)S(1)}, f32[4,16,8,128]{3,2,1,0:T(8,128)S(1)}, u32[]{:S(2)}, u32[]{:S(2)}) collective-permute-start(f32[4,16,8,128]{3,2,1,0:T(8,128)S(1)} %pad_maximum_fusion.2.angle_here_ref), channel_id=1, source_target_pairs={{0,2},{2,0},{1,3},{3,1},{4,6},{6,4},{5,7},{7,5},{8,10},{10,8},{9,1... | collective-permute-start | bytes 786440 | tf_op jit(solution)/shard_map/ppermute | solution.py:849
  20.6 15.0 %collective-permute-start.7 = (f32[16,8,128]{2,1,0:T(8,128)}, f32[16,8,128]{2,1,0:T(8,128)S(1)}, u32[]{:S(2)}, u32[]{:S(2)}) collective-permute-start(f32[16,8,128]{2,1,0:T(8,128)} %bitcast.56), channel_id=1, source_target_pairs={{0,12},{4,0},{8,4},{12,8},{1,13},{5,1},{9,5},{13,9},{2,14},{6,2},{... | collective-permute-start | bytes 196616 | tf_op jit(solution)/shard_map/ppermute | solution.py:843
  23.0 12.7 %collective-permute-start.6 = (f32[16,8,128]{2,1,0:T(8,128)}, f32[16,8,128]{2,1,0:T(8,128)S(1)}, u32[]{:S(2)}, u32[]{:S(2)}) collective-permute-start(f32[16,8,128]{2,1,0:T(8,128)} %bitcast.57), channel_id=1, source_target_pairs={{0,8},{4,12},{8,0},{12,4},{1,9},{5,13},{9,1},{13,5},{2,10},{6,14},... | collective-permute-start | bytes 196616 | tf_op jit(solution)/shard_map/ppermute | solution.py:843
  23.0 12.7 %collective-permute-start.5 = (f32[16,8,128]{2,1,0:T(8,128)}, f32[16,8,128]{2,1,0:T(8,128)S(1)}, u32[]{:S(2)}, u32[]{:S(2)}) collective-permute-start(f32[16,8,128]{2,1,0:T(8,128)} %bitcast.58), channel_id=1, source_target_pairs={{0,4},{4,8},{8,12},{12,0},{1,5},{5,9},{9,13},{13,1},{2,6},{6,10},{... | collective-permute-start | bytes 196616 | tf_op jit(solution)/shard_map/ppermute | solution.py:843
  36.5 11.2 %copy-start.1 = (f32[4,16,8,128]{3,2,1,0:T(8,128)}, f32[4,16,8,128]{3,2,1,0:T(8,128)S(1)}, u32[]{:S(2)}) copy-start(f32[4,16,8,128]{3,2,1,0:T(8,128)S(1)} %pad_maximum_fusion.3.tod_here_ref) | copy-start | bytes 786436
  36.5 11.2 %copy-start.2 = (f32[4,16,8,128]{3,2,1,0:T(8,128)}, f32[4,16,8,128]{3,2,1,0:T(8,128)S(1)}, u32[]{:S(2)}) copy-start(f32[4,16,8,128]{3,2,1,0:T(8,128)S(1)} %collective-permute-done.4.angle_across_ref) | copy-start | bytes 786436
  36.6 8.4 %collective-permute-start.8 = (f32[4,16,8,128]{3,2,1,0:T(8,128)S(1)}, f32[4,16,8,128]{3,2,1,0:T(8,128)S(1)}, u32[]{:S(2)}, u32[]{:S(2)}) collective-permute-start(f32[4,16,8,128]{3,2,1,0:T(8,128)S(1)} %pad_maximum_fusion.3.tod_here_ref), channel_id=1, source_target_pairs={{0,2},{2,0},{1,3},{3,1},{4,6},{6,4},{5,7},{7,5},{8,10},{10,8},{9,1... | collective-permute-start | bytes 786440 | tf_op jit(solution)/shard_map/ppermute | solution.py:849
  45.0 2.8 %copy-start.3 = (f32[4,16,8,128]{3,2,1,0:T(8,128)}, f32[4,16,8,128]{3,2,1,0:T(8,128)S(1)}, u32[]{:S(2)}) copy-start(f32[4,16,8,128]{3,2,1,0:T(8,128)S(1)} %collective-permute-done.8.tod_across_ref) | copy-start | bytes 786436
  45.0 2.0 %collective-permute-start.9 = (f32[2,4,16,8,128]{4,3,2,1,0:T(8,128)S(1)}, f32[2,4,16,8,128]{4,3,2,1,0:T(8,128)S(1)}, u32[]{:S(2)}, u32[]{:S(2)}) collective-permute-start(f32[2,4,16,8,128]{4,3,2,1,0:T(8,128)S(1)} %pad_maximum_fusion), channel_id=1, source_target_pairs={{0,1},{1,0},{2,3},{3,2},{4,5},{5,4},{6,7},{7,6},{8,9},{9,8},{10,11... | collective-permute-start | bytes 1572872 | tf_op jit(solution)/shard_map/ppermute | solution.py:852
  45.1 2.6 %collective-permute-start.10 = (f32[2,4,16,8,128]{4,3,2,1,0:T(8,128)S(1)}, f32[2,4,16,8,128]{4,3,2,1,0:T(8,128)S(1)}, u32[]{:S(2)}, u32[]{:S(2)}) collective-permute-start(f32[2,4,16,8,128]{4,3,2,1,0:T(8,128)S(1)} %pad_maximum_fusion.1), channel_id=1, source_target_pairs={{0,1},{1,0},{2,3},{3,2},{4,5},{5,4},{6,7},{7,6},{8,9},{9,8},{10,11... | collective-permute-start | bytes 1572872 | tf_op jit(solution)/shard_map/ppermute | solution.py:852
  47.0 0.8 copy-start.4
  47.8 0.8 copy-start.5

commit v2 on v1

--- a/solution.py
+++ b/solution.py
@@ -194,7 +194,7 @@
 
 def pack_kernel(
     shape, angle_ref, tod_ref, row_ref, hit_ref, group_ref, base_ref, coef_ref, lag_ref,
-    angle_rows_ref, tod_rows_ref,
+    table_ref, angle_rows_ref, tod_rows_ref,
 ):
     wafers, dets, reps, tiles, owners, capacity, owner_rows, lag_count = shape
     lane, sub = tile_iotas()
@@ -221,30 +221,27 @@
         lag = lag_ref[j : j + 1, :].astype(jnp.float32)
         whole = whole + pltpu.roll(spread(lag, ROWS), at, 1)
     table = jnp.where(sub == 0, wide(ids), jnp.where(sub == 1, wide(floats), wide(whole)))
-    angle_rows_ref[ROWS, 0:ROWS, :] = table
-    angle_rows_ref[ROWS, ROWS : 2 * ROWS, :] = spread(lists.astype(jnp.float32), capacity)
+    table_ref[0] = table
+    table_ref[1] = spread(lists.astype(jnp.float32), capacity)
     for b in range(tiles):
-        angle_rows_ref[0:ROWS, b, :] = angle_ref[:, b * LANES : (b + 1) * LANES]
+        angle_rows_ref[:, b, :] = angle_ref[:, b * LANES : (b + 1) * LANES]
         tod_rows_ref[:, b, :] = tod_ref[:, b * LANES : (b + 1) * LANES]
 
 
-def part_copies(shape, self_ref, refs, target, sem):
+def part_copies(shape, self_ref, source, target, sem):
     wafers, dets, reps = shape[:3]
-    here_ref, across_ref, other_ref = refs
     copies = []
     for swap_rep in range(reps):
         for swap_wafer in range(wafers):
             for shift in range(dets):
-                if swap_rep:
-                    source = other_ref.at[swap_wafer, shift]
-                else:
-                    source = (across_ref if swap_wafer else here_ref).at[shift]
-                wafer = self_ref[0] ^ swap_wafer
                 det = self_ref[1] - shift
                 det = jnp.where(det < 0, det + dets, det)
-                device = (wafer * dets + det) * reps + (self_ref[2] ^ swap_rep)
+                device = ((self_ref[0] ^ swap_wafer) * dets + det) * reps
+                device = device + (self_ref[2] ^ swap_rep)
                 copies.append(
-                    pltpu.make_async_copy(source, target(device), sem.at[len(copies)])
+                    pltpu.make_async_copy(
+                        source(swap_rep, swap_wafer, shift), target(device), sem.at[len(copies)]
+                    )
                 )
     return copies
 
@@ -252,18 +249,17 @@
 def table_copies(shape, self_ref, source_ref, part_ref, sem):
     wafers, dets, reps = shape[:3]
     copies = []
-    for rep in range(reps):
-        for swap_wafer in range(wafers):
-            for shift in range(dets):
-                det = self_ref[1] - shift
-                det = jnp.where(det < 0, det + dets, det)
-                device = ((self_ref[0] ^ swap_wafer) * dets + det) * reps + rep
-                copies.append(
-                    pltpu.make_async_copy(
-                        source_ref.at[rep, swap_wafer, shift], part_ref.at[device],
-                        sem.at[len(copies)],
-                    )
+    for swap_wafer in range(wafers):
+        for shift in range(dets):
+            det = self_ref[1] - shift
+            det = jnp.where(det < 0, det + dets, det)
+            device = ((self_ref[0] ^ swap_wafer) * dets + det) * reps
+            copies.append(
+                pltpu.make_async_copy(
+                    source_ref.at[swap_wafer, shift], part_ref.at[pl.ds(device, reps)],
+                    sem.at[len(copies)],
                 )
+            )
     for copy in copies:
         copy.start()
     for copy in copies:
@@ -278,59 +274,53 @@
 
 
 def twin_kernel(
-    shape, self_ref, table_ref, weight_ref, float_ref, whole_ref, size_ref, pair_ref, group_ref,
-    part_ref, code_ref, lead_ref, part_sem,
+    shape, self_ref, table_ref, float_ref, whole_ref, size_ref, pair_ref, group_ref,
+    part_ref, column_ref, code_ref, lead_ref, part_sem,
 ):
     wafers, dets, reps, tiles, owners, capacity, owner_rows, lag_count = shape
     devices = wafers * dets * reps
     total = devices * LANES
-    per_tile = LANES // tiles
     lane, sub = tile_iotas()
-    lane_f = lane.astype(jnp.float32)
+    sub_f = sub.astype(jnp.float32)
+    none = jnp.full((ROWS, LANES), BIG, jnp.float32)
+    along = lax.broadcasted_iota(jnp.int32, (1, LANES), 1).astype(jnp.float32)
     table_copies(shape, self_ref, table_ref, part_ref, part_sem)
-    none = jnp.full((ROWS, LANES), BIG, jnp.float32)
-    for tile in range(devices // per_tile):
-        code_ref[tile] = none
-        lead_ref[tile] = none
+
+    def turn(batch, carry):
+        for k in range(4):
+            device = 4 * batch + k
+            float_ref[pl.ds(device, 1), :] = part_ref[device, 0, 1:2, :]
+            whole_ref[pl.ds(device, 1), :] = part_ref[device, 0, 2:3, :].astype(jnp.int32)
+            column_ref[device] = jnp.broadcast_to(part_ref[device, 0, 0:1, :], (LANES, LANES)).T
+        return carry
+
+    lax.fori_loop(0, devices // 4, turn, 0)
 
     def survey(device, carry):
-        float_ref[pl.ds(device, 1), :] = part_ref[device, 0, 1:2, :]
-        whole_ref[pl.ds(device, 1), :] = part_ref[device, 0, 2:3, :].astype(jnp.int32)
-        ids = jnp.broadcast_to(part_ref[device, 0, 0:1, :], (LANES, LANES)).T
-        ids = [ids[j * ROWS : (j + 1) * ROWS] for j in range(tiles)]
-
-        def compare(step, state):
-            key, least = state
-            for k in range(2):
-                row = wide(part_ref[2 * step + k, 0, 0:1, :])
-                least = [
-                    jnp.minimum(least[j], jnp.where(ids[j] == row, key, BIG)) for j in range(tiles)
-                ]
-                key = key + LANES
-            return key, least
-
-        steps = lax.shift_right_logical(device, 1) + 1
-        _, least = lax.fori_loop(0, steps, compare, (lane_f, [none] * tiles))
-        codes, leads = none, none
-        for j in range(tiles):
-            lead = jnp.min(least[j], axis=1, keepdims=True)
-            mine = (device * LANES + j * ROWS + sub[:, 0:1]).astype(jnp.float32)
-            weight_ref[device * tiles + j] = wide(jnp.where(lead == mine, 0.5, 0.0))
-            later = lead < mine
-            leads = jnp.where(lane == j, jnp.where(later, lead, BIG), leads)
-            codes = jnp.where(lane == j, jnp.where(later, mine * float(total) + lead, BIG), codes)
-        tile, part = lax.div(device, per_tile), lax.rem(device, per_tile)
-        inside = lax.shift_right_logical(lane, tiles.bit_length() - 1) == part
-        for ref, found in ((code_ref, codes), (lead_ref, leads)):
-            ref[tile] = jnp.where(inside, pltpu.roll(found, part * tiles, 1), ref[tile])
+        row = wide(part_ref[device, 0, 0:1, :])
+
+        def compare(other, least):
+            found = [none] * 4
+            for j in range(tiles):
+                same = column_ref[other, j * ROWS : (j + 1) * ROWS, :] == row
+                found[j % 4] = jnp.minimum(found[j % 4], jnp.where(same, sub_f + float(j * ROWS), BIG))
+            here = jnp.minimum(jnp.minimum(found[0], found[1]), jnp.minimum(found[2], found[3]))
+            return jnp.minimum(least, here + (other * LANES).astype(jnp.float32))
+
+        least = lax.fori_loop(0, device + 1, compare, none)
+        lead = jnp.min(least, axis=0, keepdims=True)
+        mine = (device * LANES).astype(jnp.float32) + along
+        later = lead < mine
+        code_ref[pl.ds(device, 1), :] = jnp.where(later, mine * float(total) + lead, BIG)
+        lead_ref[pl.ds(device, 1), :] = jnp.where(later, lead, BIG)
         return carry
 
     lax.fori_loop(0, devices, survey, 0)
 
     def next_code(last):
-        found = jnp.full((ROWS, LANES), BIG, jnp.float32)
-        for tile in range(devices // per_tile):
-            codes = code_ref[tile]
+        found = none
+        for tile in range(devices // ROWS):
+            codes = code_ref[tile * ROWS : (tile + 1) * ROWS, :]
             found = jnp.minimum(found, jnp.where(codes > last, codes, BIG))
         return jnp.min(found)
 
@@ -346,8 +336,9 @@
         shift = (3 * (detector(key) - detector(lead))) & (PBLOCK - 1)
         wanted = lead.astype(jnp.float32)
         same = jnp.zeros((ROWS, LANES), jnp.float32)
-        for tile in range(devices // per_tile):
-            same = same + jnp.where(lead_ref[tile] == wanted, 1.0, 0.0)
+        for tile in range(devices // ROWS):
+            leads = lead_ref[tile * ROWS : (tile + 1) * ROWS, :]
+            same = same + jnp.where(leads == wanted, 1.0, 0.0)
         alone = jnp.sum(same) < 1.5
         entry = twin_entry(key, lead, shift)
         pair_ref[pairs] = entry
@@ -450,34 +441,48 @@
 
 def map_kernel(
     shape, self_ref, size_ref, pair_ref, group_ref, move_ref, float_smem, whole_smem,
-    angle_here_ref, angle_across_ref, angle_other_ref, tod_here_ref, tod_across_ref, tod_other_ref,
-    weight_ref, column_ref,
-    angle_ref, tod_ref, cos_ref, sin_ref, clean_ref, noise_ref,
+    angle_here_ref, angle_across_ref, angle_other_ref, tod_here_ref, tod_other_ref, column_ref,
+    angle_ref, tod_ref, cos_ref, sin_ref, clean_ref, noise_ref, weight_ref,
     inverse_ref, r_map, image_map, share_ref, rows_ref, sorted_ref, angle_sem, tod_sem, *more_refs,
 ):
     wafers, dets, reps, tiles, owners, capacity, owner_rows, lag_count = shape
     devices = wafers * dets * reps
-    halves = tiles // ROWS
-    octets = reps * halves
+    octets = 2 * reps
     wafer_dets = dets * ROWS
-    count = devices * tiles
+    count = devices * ROWS
     lane, sub = tile_iotas()
     zero = jnp.zeros((ROWS, LANES), jnp.float32)
+    low = lane < PBLOCK
     d_maps, sum_refs = more_refs[:ITERS], more_refs[ITERS:]
     first_sums, second_sums = sum_refs[:wafers], sum_refs[wafers:]
 
-    def copies_of(refs, to_ref, sem):
+    def copies_of(source, to_ref, sem):
         return part_copies(
-            shape, self_ref, refs, lambda d: to_ref.at[pl.ds(d * tiles, tiles)], sem
+            shape, self_ref, source, lambda d: to_ref.at[pl.ds(d * tiles, tiles)], sem
         )
 
-    angle_moves = copies_of((angle_here_ref, angle_across_ref, angle_other_ref), angle_ref, angle_sem)
-    tod_moves = copies_of((tod_here_ref, tod_across_ref, tod_other_ref), tod_ref, tod_sem)
+    def angle_source(swap_rep, swap_wafer, shift):
+        if swap_rep:
+            return angle_other_ref.at[swap_wafer, shift]
+        return (angle_across_ref if swap_wafer else angle_here_ref).at[shift]
+
+    def tod_source(swap_rep, swap_wafer, shift):
+        return (tod_other_ref if swap_rep else tod_here_ref).at[shift, swap_wafer]
+
+    angle_moves = copies_of(angle_source, angle_ref, angle_sem)
+    tod_moves = copies_of(tod_source, tod_ref, tod_sem)
     for copy in angle_moves + tod_moves:
         copy.start()
 
-    def fold(block):
-        return block + pltpu.roll(block, LANES // 2, 1)
+    def turn_half(block):
+        return pltpu.roll(block, PBLOCK, 1)
+
+    def fold(first, second):
+        return jnp.where(low, first, second) + turn_half(jnp.where(low, second, first))
+
+    def unfold(block):
+        turned = turn_half(block)
+        return jnp.where(low, block, turned), jnp.where(low, turned, block)
 
     def whole_sum(values):
         values = jnp.sum(values, axis=0, keepdims=True)
@@ -493,10 +498,6 @@
 
     def device_of(wafer, n):
         return (wafer * dets + lax.shift_right_logical(n, 3)) * reps
-
-    def register_of(wafer, n, octet):
-        device = device_of(wafer, n) + octet // halves
-        return device * tiles + (n & (ROWS - 1)) * halves + octet % halves
 
     def group_of(wafer, n):
         return whole_smem[device_of(wafer, n), n & (ROWS - 1)]
@@ -526,64 +527,91 @@
         return carry
 
     lax.fori_loop(0, sorted_ref.shape[0] // ROWS, clear_sorted, 0)
-    for copy in angle_moves:
-        copy.wait()
-
-    def survey(at, carry):
-        first, second = cosine_sine_double(angle_ref[at])
-        inside = lax.shift_right_logical(at, halves.bit_length() - 1) & (ROWS - 1)
-        base = float_smem[lax.div(at, tiles), inside]
-        cos_ref[at] = first
-        sin_ref[at] = second
-        image_map[at, 0] = zero + (base + base)
-        image_map[at, 1] = fold(base * (first * first))
-        image_map[at, 2] = fold(base * (second * second))
+
+    def spot_of(key):
+        return lax.shift_right_logical(key, 4), (key >> 3) & 1, pl.ds(key & (ROWS - 1), 1)
+
+    def in_half(half):
+        return (lane[0:1] >> 6) == half
+
+    def set_weight(at, carry):
+        weight_ref[at] = zero + 1.0
         return carry
 
-    loop(count, survey, 0, 8)
+    loop(count, set_weight, 0, 16)
+
+    def drop(list_ref):
+        def one(n, carry):
+            at, half, row = spot_of(twin_of(list_ref[n])[0])
+            weight_ref[at, row, :] = jnp.where(in_half(half), 0.0, weight_ref[at, row, :])
+            return carry
+
+        return one
+
+    lax.fori_loop(0, size_ref[0] * PAIR_BATCH, drop(pair_ref), 0)
+    lax.fori_loop(0, size_ref[1], drop(group_ref), 0)
+
+    def moved_from(target, spot, shift):
+        at, half, row = spot
+        result = []
+        for c in range(3):
+            values = wide(target[at, c, row, :])
+            values = jnp.where((lane >> 6) == half, values, turn_half(values))
+            result.append(pltpu.roll(values, shift, 1)[0:1])
+        return result
 
     def merge_twins(target):
+        def add(spot, values):
+            at, half, row = spot
+            for c in range(3):
+                target[at, c, row, :] += jnp.where(in_half(half), values[c], 0.0)
+
         def pair_batch(n, carry):
             found = []
             for k in range(PAIR_BATCH):
                 key, lead, shift = twin_of(pair_ref[n * PAIR_BATCH + k])
-                spots = [
-                    (lax.shift_right_logical(spot, 3), pl.ds(spot & (ROWS - 1), 1))
-                    for spot in (key, lead)
-                ]
-                values = [[target[at, c, row, :] for c in range(3)] for at, row in spots]
-                found.append((spots, shift, values))
-            for spots, shift, values in found:
-                turns = (shift, (LANES - shift) & (LANES - 1))
-                for (at, row), own, other, turn in zip(
-                    spots, values, values[::-1], turns[::-1]
-                ):
-                    for c in range(3):
-                        target[at, c, row, :] = own[c] + pltpu.roll(wide(other[c]), turn, 1)[0:1]
+                key, lead = spot_of(key), spot_of(lead)
+                back = (PBLOCK - shift) & (PBLOCK - 1)
+                found.append((lead, moved_from(target, key, shift)))
+                found.append((key, moved_from(target, lead, back)))
+            for spot, values in found:
+                add(spot, values)
             return carry
 
         def gather_one(n, carry):
             key, lead, shift = twin_of(group_ref[n])
-            at, row = lax.shift_right_logical(key, 3), key & (ROWS - 1)
-            lead_at, lead_row = lax.shift_right_logical(lead, 3), lead & (ROWS - 1)
-            for c in range(3):
-                moved = pltpu.roll(wide(target[at, c, pl.ds(row, 1), :]), shift, 1)
-                target[lead_at, c, pl.ds(lead_row, 1), :] += moved[0:1]
+            add(spot_of(lead), moved_from(target, spot_of(key), shift))
             return carry
 
         def spread_one(n, carry):
             key, lead, shift = twin_of(group_ref[n])
-            at, row = lax.shift_right_logical(key, 3), key & (ROWS - 1)
-            lead_at, lead_row = lax.shift_right_logical(lead, 3), lead & (ROWS - 1)
-            turn = (LANES - shift) & (LANES - 1)
+            values = moved_from(target, spot_of(lead), (PBLOCK - shift) & (PBLOCK - 1))
+            at, half, row = spot_of(key)
             for c in range(3):
-                moved = pltpu.roll(wide(target[lead_at, c, pl.ds(lead_row, 1), :]), turn, 1)
-                target[at, c, pl.ds(row, 1), :] = moved[0:1]
+                target[at, c, row, :] = jnp.where(in_half(half), values[c], target[at, c, row, :])
             return carry
 
         lax.fori_loop(0, size_ref[0], pair_batch, 0)
         lax.fori_loop(0, size_ref[1], gather_one, 0)
         lax.fori_loop(0, size_ref[1], spread_one, 0)
+
+    for copy in angle_moves:
+        copy.wait()
+
+    def survey(at, carry):
+        base = float_smem[lax.shift_right_logical(at, 3), at & (ROWS - 1)]
+        squares = []
+        for half in range(2):
+            first, second = cosine_sine_double(angle_ref[2 * at + half])
+            cos_ref[2 * at + half] = first
+            sin_ref[2 * at + half] = second
+            squares.append((base * (first * first), base * (second * second)))
+        image_map[at, 0] = zero + (base + base)
+        for c in range(2):
+            image_map[at, c + 1] = fold(squares[0][c], squares[1][c])
+        return carry
+
+    loop(count, survey, 0, 8)
 
     def clear_sums(refs):
         for ref in refs:
@@ -597,16 +625,19 @@
                 for octet in range(octets):
                     ref[group, rows_of(octet), :] *= share_ref[wafer * NSUB + group]
 
-    def sum_streams(stream_of, carry):
+    def sum_streams(streams_of, carry):
         clear_sums(first_sums)
 
         def one_detector(n, carry):
             for wafer in range(wafers):
                 group = group_of(wafer, n)
-                for octet in range(octets):
-                    stream, carry = stream_of(register_of(wafer, n, octet), carry)
-                    clean_ref[wafer * wafer_dets + n, rows_of(octet), :] = stream
-                    first_sums[wafer][group, rows_of(octet), :] += stream
+                for rep in range(reps):
+                    at = (device_of(wafer, n) + rep) * ROWS + (n & (ROWS - 1))
+                    streams, carry = streams_of(at, carry)
+                    for half, stream in enumerate(streams):
+                        rows = rows_of(2 * rep + half)
+                        clean_ref[wafer * wafer_dets + n, rows, :] = stream
+                        first_sums[wafer][group, rows, :] += stream
             return carry
 
         carry = loop(wafer_dets, one_detector, carry, 4)
@@ -643,7 +674,7 @@
                     carry = carry + here * result
             return carry
 
-        product = loop(wafer_dets, one_filter, zero, 2)
+        product = loop(wafer_dets, one_filter, zero, 4)
         average(second_sums)
         return product
 
@@ -651,13 +682,16 @@
         def one_return(n, carry):
             for wafer in range(wafers):
                 group = group_of(wafer, n)
-                for octet in range(octets):
-                    at = register_of(wafer, n, octet)
-                    stream = noise_ref[wafer * wafer_dets + n, rows_of(octet), :]
-                    stream = stream - second_sums[wafer][group, rows_of(octet), :]
-                    target[at, 0] = fold(stream)
-                    target[at, 1] = fold(cos_ref[at] * stream)
-                    target[at, 2] = fold(sin_ref[at] * stream)
+                for rep in range(reps):
+                    at = (device_of(wafer, n) + rep) * ROWS + (n & (ROWS - 1))
+                    streams = []
+                    for half in range(2):
+                        rows = rows_of(2 * rep + half)
+                        stream = noise_ref[wafer * wafer_dets + n, rows, :]
+                        streams.append(stream - second_sums[wafer][group, rows, :])
+                    target[at, 0] = fold(*streams)
+                    for c, ref in ((1, cos_ref), (2, sin_ref)):
+                        target[at, c] = fold(*(ref[2 * at + h] * streams[h] for h in range(2)))
             return carry
 
         loop(wafer_dets, one_return, 0, 4)
@@ -666,7 +700,7 @@
     merge_twins(image_map)
     for copy in tod_moves:
         copy.wait()
-    sum_streams(lambda at, carry: (tod_ref[at], carry), 0)
+    sum_streams(lambda at, carry: ([tod_ref[2 * at + half] for half in range(2)], carry), 0)
     filter_streams()
     return_streams(r_map)
 
@@ -685,19 +719,24 @@
     for iteration, d_map in enumerate(d_maps):
         last = iteration == ITERS - 1
 
-        def seen_stream(at, carry):
-            parts = []
+        def seen_streams(at, carry):
+            squares = zero
+            streams = [None, None]
             for c in range(3):
                 part = inverse_ref[at, c] * r_map[at, c]
                 if iteration:
                     part = part + factor * d_maps[iteration - 1][at, c]
                 d_map[at, c] = part
-                parts.append(part)
-            squares = parts[0] * parts[0] + parts[1] * parts[1] + parts[2] * parts[2]
-            stream = parts[0] + cos_ref[at] * parts[1] + sin_ref[at] * parts[2]
-            return stream, carry + weight_ref[at] * squares
-
-        prior = sum_streams(seen_stream, zero)
+                squares = squares + part * part
+                for half, seen in enumerate(unfold(part)):
+                    if c == 0:
+                        streams[half] = seen
+                    else:
+                        ref = cos_ref if c == 1 else sin_ref
+                        streams[half] = streams[half] + ref[2 * at + half] * seen
+            return streams, carry + weight_ref[at] * squares
+
+        prior = sum_streams(seen_streams, zero)
         product = filter_streams()
         return_streams(image_map)
         step = energy / whole_sum(product + prior_weight * prior)
@@ -722,9 +761,9 @@
         else:
 
             def place_pixels(at, carry):
-                team = lax.rem(lax.div(at, reps * tiles), dets)
-                inside = lax.shift_right_logical(at, halves.bit_length() - 1) & (ROWS - 1)
-                turn = (3 * (team * ROWS + inside)) & (PBLOCK - 1)
+                team = lax.rem(lax.div(at, reps * ROWS), dets)
+                turn = (3 * (team * ROWS + (at & (ROWS - 1)))) & (PBLOCK - 1)
+                inside = (lane & (PBLOCK - 1)) >= turn
                 values = []
                 for c in range(3):
                     value = steps[0] * d_maps[0][at, c]
@@ -732,12 +771,17 @@
                         value = value + steps[k] * d_maps[k][at, c]
                     values.append(value)
                 values += [new_residual(at, c) for c in range(3)]
-                values = [pltpu.roll(value, turn, 1) for value in values]
-                rows = pl.ds(pl.multiple_of(at * ROWS, ROWS), ROWS)
                 for c in range(3):
-                    rows_ref[rows, c * LANES : (c + 1) * LANES] = jnp.where(
-                        lane < PBLOCK, values[2 * c], values[2 * c + 1]
+                    left, right = values[2 * c], values[2 * c + 1]
+                    halves = (
+                        jnp.where(low, left, turn_half(right)), jnp.where(low, turn_half(left), right)
                     )
+                    for half, value in enumerate(halves):
+                        value = jnp.where(
+                            inside, pltpu.roll(value, turn, 1), pltpu.roll(value, turn + PBLOCK, 1)
+                        )
+                        rows = pl.ds(pl.multiple_of((2 * at + half) * ROWS, ROWS), ROWS)
+                        rows_ref[rows, c * LANES : (c + 1) * LANES] = value
                 return carry
 
             loop(count, place_pixels, 0, 8)
@@ -811,7 +855,7 @@
         det_count == ROWS
         and owners == ROWS
         and tiles * ROWS == LANES
-        and tiles % ROWS == 0
+        and tiles == 2 * ROWS
         and (wafers, reps) == (2, 2)
         and (1 + lag_count) * ROWS <= LANES
         and capacity <= LANES
@@ -851,37 +895,40 @@
     def other_rep(here, across):
         return here, across, lax.ppermute(jnp.stack([here, across]), "rep", swap)
 
-    angles, samples = pl.pallas_call(
+    tables, angles, samples = pl.pallas_call(
         functools.partial(pack_kernel, shape),
         out_shape=[
-            jax.ShapeDtypeStruct((ROWS + 1, tiles, LANES), f32),
+            jax.ShapeDtypeStruct((2, ROWS, LANES), f32),
+            jax.ShapeDtypeStruct((ROWS, tiles, LANES), f32),
             jax.ShapeDtypeStruct((ROWS, tiles, LANES), f32),
         ],
         in_specs=[vmem] * 8,
-        out_specs=[vmem] * 2,
+        out_specs=[vmem] * 3,
         compiler_params=params,
         name="pack",
     )(
         psi[0], tod[0], point_row[0], hit_list[0, 0, 0], group_id, a_zero, band_coef[0].T,
         band_lag[0].T,
     )
-    angles = angles.reshape(tiles + 2, ROWS, LANES)
-    samples = samples.reshape(tiles, ROWS, LANES)
+    angles, samples = (stream.reshape(tiles, ROWS, LANES) for stream in (angles, samples))
     place_here = jnp.stack([lax.axis_index(axis) for axis in ("wafer", "det", "rep")]).astype(i32)
-    angles = along_det(angles)
-    tables = jnp.stack([block[tiles:] for block in angles])
-    angles = jnp.stack([block[:tiles] for block in angles])
+    tables = lax.all_gather(tables, "rep", axis=0, tiled=False)
+    riders = jnp.concatenate([angles, tables.reshape(2 * reps, ROWS, LANES)])
+    samples, riders = lax.optimization_barrier((samples, riders))
+    samples = jnp.stack([samples, other_wafer(samples)])
+    blocks = along_det(riders)
+    tables = jnp.stack([block[tiles:] for block in blocks])
+    angles = jnp.stack([block[:tiles] for block in blocks])
     tables = jnp.stack([tables, other_wafer(tables)])
+    tables = tables.reshape(wafers, dets, reps, 2, ROWS, LANES)
     samples, angles, tables = lax.optimization_barrier((samples, angles, tables))
     angles_across = other_wafer(angles)
-    samples = jnp.stack(along_det(samples))
-    tables = lax.all_gather(tables, "rep", axis=0, tiled=False)
+    samples = along_det(samples)
     table_scratch = pltpu.VMEM((devices, 2, ROWS, LANES), f32)
     table_sem = pltpu.SemaphoreType.DMA((devices,))
     twins = pl.pallas_call(
         functools.partial(twin_kernel, shape),
         out_shape=[
-            jax.ShapeDtypeStruct((count, ROWS, LANES), f32),
             jax.ShapeDtypeStruct((devices, LANES), f32),
             jax.ShapeDtypeStruct((devices, LANES), i32),
             jax.ShapeDtypeStruct((2,), i32),
@@ -889,22 +936,18 @@
             jax.ShapeDtypeStruct((total,), i32),
         ],
         in_specs=[smem, anywhere],
-        out_specs=[vmem] * 3 + [smem] * 3,
+        out_specs=[vmem] * 2 + [smem] * 3,
         scratch_shapes=[
             table_scratch,
-            pltpu.VMEM((devices * tiles // LANES, ROWS, LANES), f32),
-            pltpu.VMEM((devices * tiles // LANES, ROWS, LANES), f32),
+            pltpu.VMEM((devices, LANES, LANES), f32),
+            pltpu.VMEM((devices, LANES), f32),
+            pltpu.VMEM((devices, LANES), f32),
             table_sem,
         ],
         compiler_params=params,
         cost_estimate=pl.CostEstimate(flops=10**9, bytes_accessed=3 * 10**7, transcendentals=0),
         name="twins",
     )(place_here, tables)
-    angles, angles_across, samples, tables, twins = lax.optimization_barrier(
-        (angles, angles_across, samples, tables, twins)
-    )
-    weight, floats, whole, size, pair, group = twins
-    samples_across = other_wafer(samples)
     place, start, moves = pl.pallas_call(
         functools.partial(place_kernel, shape),
         out_shape=[
@@ -924,24 +967,27 @@
         cost_estimate=pl.CostEstimate(flops=10**9, bytes_accessed=2 * 10**7, transcendentals=0),
         name="places",
     )(place_here, tables)
-    angles, angles_across, samples, samples_across, place, start, moves = lax.optimization_barrier(
-        (angles, angles_across, samples, samples_across, place, start, moves)
+    angles, angles_across, samples, twins, place, start, moves = lax.optimization_barrier(
+        (angles, angles_across, samples, twins, place, start, moves)
     )
+    floats, whole, size, pair, group = twins
     angle_blocks = other_rep(angles, angles_across)
-    sample_blocks = other_rep(samples, samples_across)
+    samples = jnp.stack(samples)
+    sample_blocks = samples, lax.ppermute(samples, "rep", swap)
     stream = pltpu.VMEM((count, ROWS, LANES), f32)
-    sky = pltpu.VMEM((count, 3, ROWS, LANES), f32)
-    sky_and_spare = pltpu.VMEM((count + 1, 3, ROWS, LANES), f32)
+    sky = pltpu.VMEM((devices * ROWS, 3, ROWS, LANES), f32)
+    sky_and_spare = pltpu.VMEM((devices * ROWS + 1, 3, ROWS, LANES), f32)
     group_sums = pltpu.VMEM((NSUB, octets * ROWS, LANES), f32)
     columns = pl.pallas_call(
         functools.partial(map_kernel, shape),
         out_shape=jax.ShapeDtypeStruct((slots // LANES + 1, 2 * height, 2 * LANES), jnp.bfloat16),
-        in_specs=[smem] * 7 + [anywhere] * 6 + [vmem],
+        in_specs=[smem] * 7 + [anywhere] * 5,
         out_specs=vmem,
         scratch_shapes=[
             stream, stream, stream, stream,
             pltpu.VMEM((detectors, octets * ROWS, LANES), f32),
             pltpu.VMEM((detectors, octets * ROWS, LANES), f32),
+            pltpu.VMEM((devices * ROWS + 1, ROWS, LANES), f32),
             sky, sky_and_spare, sky_and_spare,
             pltpu.VMEM((wafers * NSUB, ROWS, LANES), f32),
             pltpu.VMEM((total, 2 * height), f32),
@@ -953,7 +999,7 @@
         name="map_maker",
     )(
         place_here, size, pair, group, moves, floats, whole, *angle_blocks,
-        *sample_blocks, weight,
+        *sample_blocks,
     )
     out_block = pl.BlockSpec((height, OUT_TILES * LANES), lambda n: (0, n))
     x_turned, r_turned = pl.pallas_call(

time: 112 us -> 105 us (0.938)
  Pallas kernels: 77.9 us -> 72.2 us
  waiting for transfers between devices: 11.9 us -> 9.43 us
  local copies, waits for them, and re-layouts: 2.45 us -> 0.9 us
  other arithmetic: 1.52 us -> 3.04 us
    pallas_call x1, Pallas kernels: 42 us -> 38.6 us  [whole_part(): pl.pallas_call(functools.partial(map_kernel, shape), out_shape=jax.ShapeD...]
    ppermute x6, waiting for transfers between devices: 4.63 us -> 1.72 us  [along_det(): lax.ppermute(block, 'det', [(i, (i + shift) % dets) for i in range(dets)])]
    pallas_call x1, Pallas kernels: 9.02 us -> 6.76 us  [whole_part(): pl.pallas_call(functools.partial(twin_kernel, shape), out_shape=[jax.Shap...]
  transfers between devices with their start and end apart: 11 -> 11, of which waited for: 6 -> 5; matrix products, arithmetic and copies ran while one was open for 3% -> 1% of each run, Pallas kernels for 13% -> 11%
where the time goes in v2:
time: 105 us; the launch traced here: 104 us
  Pallas kernels  72.2 us (69%)
  starting transfers between devices  15 us (14%)
  waiting for transfers between devices  9.43 us (9%)
  other arithmetic  3.04 us (3%)
  blocking collectives  2.14 us (2%)
    pallas_call x1, Pallas kernels, whole_part(): pl.pallas_call(functools.partial(map_kernel, shape), out_shape=jax.ShapeD...  38.6 us
    pallas_call x1, Pallas kernels, whole_part(): pl.pallas_call(write_kernel, grid=(owner_rows // (OUT_TILES * LANES),), o...  20.2 us
    ppermute x6, starting transfers between devices, along_det(): lax.ppermute(block, 'det', [(i, (i + shift) % dets) for i in range(dets)])  9.84 us
    pallas_call x1, Pallas kernels, whole_part(): pl.pallas_call(functools.partial(twin_kernel, shape), out_shape=[jax.Shap...  6.76 us
    ppermute x3, waiting for transfers between devices, other_wafer(): return lax.ppermute(here, 'wafer', swap)  5.68 us
    pallas_call x1, Pallas kernels, whole_part(): pl.pallas_call(functools.partial(place_kernel, shape), out_shape=[jax.Sha...  4.94 us
    ppermute x3, starting transfers between devices, other_wafer(): return lax.ppermute(here, 'wafer', swap)  4.54 us
    all_gather x1, blocking collectives, whole_part(): tables = lax.all_gather(tables, 'rep', axis=0, tiled=False)  2.14 us
  transfers between devices with their start and end apart: 11, of which 5 were waited for; matrix products, arithmetic and copies ran while one was open for 1% of the time, Pallas kernels for 11%

profile of v2, /device:TPU:0, one launch (start us, length us, event | category | flops | bytes accessed | tf_op | source)
XLA Modules:
  0.0 103.6 jit_solution(15401974189366624161)
XLA Ops:
  0.6 1.7 %pack.1 = (f32[2,8,128]{2,1,0:T(8,128)}, f32[8,16,128]{2,1,0:T(8,128)}, f32[8,16,128]{2,1,0:T(8,128)}) custom-call(f32[8,2048]{1,0:T(8,128)} %bitcast.56, f32[8,2048]{1,0:T(8,128)} %bitcast.57, s32[8,16]{1,0:T(8,128)} %bitcast.63, s32[8,32]{1,0:T(8,128)} %bitcast.64, s32[1,8]{1,0:T(1,128)} %group_ref.1, f32[1,8]{1,0:T(1,128)} %base_ref.1, f32[4,8]{1,0:T(4,128)} %bitcast.65, ...), custom_call_target="tpu_custom_call" | custom-call | tf_op jit(solution)/shard_map/pack/pallas_call | solution.py:898
  2.3 2.1 %all-gather = f32[4,8,128]{2,1,0:T(8,128)S(1)} all-gather(f32[2,8,128]{2,1,0:T(8,128)} %get-tuple-element.36), channel_id=2, replica_groups=mesh['groups'=2,'det'=4,'wafer'=2,'rep'=2] {'rep'}, dimensions={0}, use_global_device_ids=true | all-gather | bytes 24576 | tf_op jit(solution)/shard_map/all_gather | solution.py:915
  4.5 0.8 pad_maximum_fusion.5
  5.3 4.9 %collective-permute-start.3 = (f32[20,8,128]{2,1,0:T(8,128)S(1)}, f32[20,8,128]{2,1,0:T(8,128)S(1)}, u32[]{:S(2)}, u32[]{:S(2)}) collective-permute-start(f32[20,8,128]{2,1,0:T(8,128)S(1)} %pad_maximum_fusion.5), channel_id=1, source_target_pairs={{0,12},{4,0},{8,4},{12,8},{1,13},{5,1},{9,5},{13,9},{2,14},{6,2},{... | collective-permute-start | bytes 245768 | tf_op jit(solution)/shard_map/ppermute | solution.py:887
  10.2 1.0 collective-permute-start.1
  11.2 1.5 %collective-permute-start = (f32[16,8,128]{2,1,0:T(8,128)}, f32[16,8,128]{2,1,0:T(8,128)S(1)}, u32[]{:S(2)}, u32[]{:S(2)}) collective-permute-start(f32[16,8,128]{2,1,0:T(8,128)} %bitcast.59), channel_id=1, source_target_pairs={{0,2},{2,0},{1,3},{3,1},{4,6},{6,4},{5,7},{7,5},{8,10},{10,8},{9,1... | collective-permute-start | bytes 196616 | tf_op jit(solution)/shard_map/ppermute | solution.py:893
  12.8 3.0 %collective-permute-done = f32[16,8,128]{2,1,0:T(8,128)S(1)} collective-permute-done((f32[16,8,128]{2,1,0:T(8,128)}, f32[16,8,128]{2,1,0:T(8,128)S(1)}, u32[]{:S(2)}, u32[]{:S(2)}) %collective-permute-start) | collective-permute-done | bytes 65568 | tf_op jit(solution)/shard_map/ppermute | solution.py:893
  15.7 0.8 pad_maximum_fusion.3
  16.6 1.7 %collective-permute-done.2 = f32[20,8,128]{2,1,0:T(8,128)S(1)} collective-permute-done((f32[20,8,128]{2,1,0:T(8,128)S(1)}, f32[20,8,128]{2,1,0:T(8,128)S(1)}, u32[]{:S(2)}, u32[]{:S(2)}) %collective-permute-start.2) | collective-permute-done | bytes 81952 | tf_op jit(solution)/shard_map/ppermute | solution.py:887
  18.3 1.6 %collective-permute-start.4 = (f32[4,4,8,128]{3,2,1,0:T(8,128)S(1)}, f32[4,4,8,128]{3,2,1,0:T(8,128)S(1)}, u32[]{:S(2)}, u32[]{:S(2)}) collective-permute-start(f32[4,4,8,128]{3,2,1,0:T(8,128)S(1)} %pad_maximum_fusion.6), channel_id=1, source_target_pairs={{0,2},{2,0},{1,3},{3,1},{4,6},{6,4},{5,7},{7,5},{8,10},{10,8},{9,1... | collective-permute-start | bytes 196616 | tf_op jit(solution)/shard_map/ppermute | solution.py:893
  20.0 2.7 %collective-permute-done.4 = f32[4,4,8,128]{3,2,1,0:T(8,128)S(1)} collective-permute-done((f32[4,4,8,128]{3,2,1,0:T(8,128)S(1)}, f32[4,4,8,128]{3,2,1,0:T(8,128)S(1)}, u32[]{:S(2)}, u32[]{:S(2)}) %collective-permute-start.4) | collective-permute-done | bytes 65568 | tf_op jit(solution)/shard_map/ppermute | solution.py:893
  22.7 0.7 pad_maximum_fusion.4.table_ref
  23.3 1.5 %collective-permute-start.5 = (f32[4,16,8,128]{3,2,1,0:T(8,128)S(1)}, f32[4,16,8,128]{3,2,1,0:T(8,128)S(1)}, u32[]{:S(2)}, u32[]{:S(2)}) collective-permute-start(f32[4,16,8,128]{3,2,1,0:T(8,128)S(1)} %pad_maximum_fusion.2.angle_here_ref), channel_id=1, source_target_pairs={{0,2},{2,0},{1,3},{3,1},{4,6},{6,4},{5,7},{7,5},{8,10},{10,8},{9,1... | collective-permute-start | bytes 786440 | tf_op jit(solution)/shard_map/ppermute | solution.py:893
  24.8 0.6 pad_add_fusion.self_ref
  25.4 1.9 %collective-permute-start.8 = (f32[2,16,8,128]{3,2,1,0:T(8,128)S(1)}, f32[2,16,8,128]{3,2,1,0:T(8,128)S(1)}, u32[]{:S(2)}, u32[]{:S(2)}) collective-permute-start(f32[2,16,8,128]{3,2,1,0:T(8,128)S(1)} %pad_maximum_fusion.3), channel_id=1, source_target_pairs={{0,12},{4,0},{8,4},{12,8},{1,13},{5,1},{9,5},{13,9},{2,14},{6,2},{... | collective-permute-start | bytes 393224 | tf_op jit(solution)/shard_map/ppermute | solution.py:887
  27.7 1.6 %collective-permute-start.6 = (f32[2,16,8,128]{3,2,1,0:T(8,128)S(1)}, f32[2,16,8,128]{3,2,1,0:T(8,128)S(1)}, u32[]{:S(2)}, u32[]{:S(2)}) collective-permute-start(f32[2,16,8,128]{3,2,1,0:T(8,128)S(1)} %pad_maximum_fusion.3), channel_id=1, source_target_pairs={{0,4},{4,8},{8,12},{12,0},{1,5},{5,9},{9,13},{13,1},{2,6},{6,10},{... | collective-permute-start | bytes 393224 | tf_op jit(solution)/shard_map/ppermute | solution.py:887
  29.3 6.8 %twins.1 = (f32[16,128]{1,0:T(8,128)}, s32[16,128]{1,0:T(8,128)}, s32[2]{0:T(128)}, s32[2048]{0:T(1024)}, s32[2048]{0:T(1024)}) custom-call(s32[3]{0:T(128)} %pad_add_fusion.self_ref, f32[2,4,2,2,8,128]{5,4,3,2,1,0:T(8,128)} %pad_maximum_fusion.4.table_ref), custom_call_target="tpu_custom_call" | custom-call | flops 1000000000 | bytes 30000000 | tf_op jit(solution)/shard_map/twins/pallas_call | solution.py:929
  36.1 4.9 %places.1 = (s32[256,128]{1,0:T(8,128)}, s32[8,256]{1,0:T(8,128)}, s32[16,128]{1,0:T(8,128)}) custom-call(s32[3]{0:T(128)} %pad_add_fusion.self_ref, f32[2,4,2,2,8,128]{5,4,3,2,1,0:T(8,128)} %pad_maximum_fusion.4.table_ref), custom_call_target="tpu_custom_call" | custom-call | flops 1000000000 | bytes 20000000 | tf_op jit(solution)/shard_map/places/pallas_call | solution.py:951
  41.3 0.6 collective-permute-start.10
  41.8 1.3 %collective-permute-done.9.angle_other_ref = f32[2,4,16,8,128]{4,3,2,1,0:T(8,128)S(1)} collective-permute-done((f32[2,4,16,8,128]{4,3,2,1,0:T(8,128)S(1)}, f32[2,4,16,8,128]{4,3,2,1,0:T(8,128)S(1)}, u32[]{:S(2)}, u32[]{:S(2)}) %collective-permute-start.9) | collective-permute-done | bytes 524320 | tf_op jit(solution)/shard_map/ppermute | solution.py:896
  43.1 0.7 collective-permute-done.10.tod_other_ref
  43.9 0.8 copy-done.4
  44.7 38.6 %map_maker.1.column_ref = bf16[5,384,256]{2,1,0:T(8,128)(2,1)} custom-call(s32[3]{0:T(128)} %pad_add_fusion.self_ref, s32[2]{0:T(128)} %get-tuple-element.51.size_ref, s32[2048]{0:T(1024)} %get-tuple-element.52.pair_ref, s32[2048]{0:T(1024)} %get-tuple-element.53.group_ref, s32[16,128]{1,0:T(8,128)} %get-tuple-element.54.move_ref, ...), custom_call_target="tpu_custom_call" | custom-call | tf_op jit(solution)/shard_map/map_maker/pallas_call | solution.py:981
  83.3 20.2 %write.1 = (f32[192,24576]{1,0:T(8,128)}, f32[192,24576]{1,0:T(8,128)}) custom-call(s32[8,256]{1,0:T(8,128)} %get-tuple-element.50.start_ref, bf16[5,384,256]{2,1,0:T(8,128)(2,1)} %map_maker.1.column_ref, s32[256,128]{1,0:T(8,128)} %get-tuple-element.63.place_ref), custom_call_target="tpu_custom_call" | custom-call | tf_op jit(solution)/shard_map/write/pallas_call | solution.py:1005
  (30 shorter events, 0.7 us)
Async XLA Ops:
  5.3 11.3 %collective-permute-start.3 = (f32[20,8,128]{2,1,0:T(8,128)S(1)}, f32[20,8,128]{2,1,0:T(8,128)S(1)}, u32[]{:S(2)}, u32[]{:S(2)}) collective-permute-start(f32[20,8,128]{2,1,0:T(8,128)S(1)} %pad_maximum_fusion.5), channel_id=1, source_target_pairs={{0,12},{4,0},{8,4},{12,8},{1,13},{5,1},{9,5},{13,9},{2,14},{6,2},{... | collective-permute-start | bytes 245768 | tf_op jit(solution)/shard_map/ppermute | solution.py:887
  10.2 8.1 %collective-permute-start.2 = (f32[20,8,128]{2,1,0:T(8,128)S(1)}, f32[20,8,128]{2,1,0:T(8,128)S(1)}, u32[]{:S(2)}, u32[]{:S(2)}) collective-permute-start(f32[20,8,128]{2,1,0:T(8,128)S(1)} %pad_maximum_fusion.5), channel_id=1, source_target_pairs={{0,8},{4,12},{8,0},{12,4},{1,9},{5,13},{9,1},{13,5},{2,10},{6,14},... | collective-permute-start | bytes 245768 | tf_op jit(solution)/shard_map/ppermute | solution.py:887
  10.2 8.1 %collective-permute-start.1 = (f32[20,8,128]{2,1,0:T(8,128)S(1)}, f32[20,8,128]{2,1,0:T(8,128)S(1)}, u32[]{:S(2)}, u32[]{:S(2)}) collective-permute-start(f32[20,8,128]{2,1,0:T(8,128)S(1)} %pad_maximum_fusion.5), channel_id=1, source_target_pairs={{0,4},{4,8},{8,12},{12,0},{1,5},{5,9},{9,13},{13,1},{2,6},{6,10},{... | collective-permute-start | bytes 245768 | tf_op jit(solution)/shard_map/ppermute | solution.py:887
  11.2 4.5 %collective-permute-start = (f32[16,8,128]{2,1,0:T(8,128)}, f32[16,8,128]{2,1,0:T(8,128)S(1)}, u32[]{:S(2)}, u32[]{:S(2)}) collective-permute-start(f32[16,8,128]{2,1,0:T(8,128)} %bitcast.59), channel_id=1, source_target_pairs={{0,2},{2,0},{1,3},{3,1},{4,6},{6,4},{5,7},{7,5},{8,10},{10,8},{9,1... | collective-permute-start | bytes 196616 | tf_op jit(solution)/shard_map/ppermute | solution.py:893
  18.3 4.3 %collective-permute-start.4 = (f32[4,4,8,128]{3,2,1,0:T(8,128)S(1)}, f32[4,4,8,128]{3,2,1,0:T(8,128)S(1)}, u32[]{:S(2)}, u32[]{:S(2)}) collective-permute-start(f32[4,4,8,128]{3,2,1,0:T(8,128)S(1)} %pad_maximum_fusion.6), channel_id=1, source_target_pairs={{0,2},{2,0},{1,3},{3,1},{4,6},{6,4},{5,7},{7,5},{8,10},{10,8},{9,1... | collective-permute-start | bytes 196616 | tf_op jit(solution)/shard_map/ppermute | solution.py:893
  20.0 23.9 %copy-start = (f32[4,16,8,128]{3,2,1,0:T(8,128)}, f32[4,16,8,128]{3,2,1,0:T(8,128)S(1)}, u32[]{:S(2)}) copy-start(f32[4,16,8,128]{3,2,1,0:T(8,128)S(1)} %pad_maximum_fusion.2.angle_here_ref) | copy-start | bytes 786436
  23.3 17.7 %collective-permute-start.5 = (f32[4,16,8,128]{3,2,1,0:T(8,128)S(1)}, f32[4,16,8,128]{3,2,1,0:T(8,128)S(1)}, u32[]{:S(2)}, u32[]{:S(2)}) collective-permute-start(f32[4,16,8,128]{3,2,1,0:T(8,128)S(1)} %pad_maximum_fusion.2.angle_here_ref), channel_id=1, source_target_pairs={{0,2},{2,0},{1,3},{3,1},{4,6},{6,4},{5,7},{7,5},{8,10},{10,8},{9,1... | collective-permute-start | bytes 786440 | tf_op jit(solution)/shard_map/ppermute | solution.py:893
  25.4 15.6 %collective-permute-start.8 = (f32[2,16,8,128]{3,2,1,0:T(8,128)S(1)}, f32[2,16,8,128]{3,2,1,0:T(8,128)S(1)}, u32[]{:S(2)}, u32[]{:S(2)}) collective-permute-start(f32[2,16,8,128]{3,2,1,0:T(8,128)S(1)} %pad_maximum_fusion.3), channel_id=1, source_target_pairs={{0,12},{4,0},{8,4},{12,8},{1,13},{5,1},{9,5},{13,9},{2,14},{6,2},{... | collective-permute-start | bytes 393224 | tf_op jit(solution)/shard_map/ppermute | solution.py:887
  27.3 13.8 %collective-permute-start.7 = (f32[2,16,8,128]{3,2,1,0:T(8,128)S(1)}, f32[2,16,8,128]{3,2,1,0:T(8,128)S(1)}, u32[]{:S(2)}, u32[]{:S(2)}) collective-permute-start(f32[2,16,8,128]{3,2,1,0:T(8,128)S(1)} %pad_maximum_fusion.3), channel_id=1, source_target_pairs={{0,8},{4,12},{8,0},{12,4},{1,9},{5,13},{9,1},{13,5},{2,10},{6,14},... | collective-permute-start | bytes 393224 | tf_op jit(solution)/shard_map/ppermute | solution.py:887
  27.7 13.4 %collective-permute-start.6 = (f32[2,16,8,128]{3,2,1,0:T(8,128)S(1)}, f32[2,16,8,128]{3,2,1,0:T(8,128)S(1)}, u32[]{:S(2)}, u32[]{:S(2)}) collective-permute-start(f32[2,16,8,128]{3,2,1,0:T(8,128)S(1)} %pad_maximum_fusion.3), channel_id=1, source_target_pairs={{0,4},{4,8},{8,12},{12,0},{1,5},{5,9},{9,13},{13,1},{2,6},{6,10},{... | collective-permute-start | bytes 393224 | tf_op jit(solution)/shard_map/ppermute | solution.py:887
  41.1 2.8 %copy-start.2 = (f32[4,16,8,128]{3,2,1,0:T(8,128)}, f32[4,16,8,128]{3,2,1,0:T(8,128)S(1)}, u32[]{:S(2)}) copy-start(f32[4,16,8,128]{3,2,1,0:T(8,128)S(1)} %collective-permute-done.5.angle_across_ref) | copy-start | bytes 786436
  41.1 2.0 %collective-permute-start.9 = (f32[2,4,16,8,128]{4,3,2,1,0:T(8,128)S(1)}, f32[2,4,16,8,128]{4,3,2,1,0:T(8,128)S(1)}, u32[]{:S(2)}, u32[]{:S(2)}) collective-permute-start(f32[2,4,16,8,128]{4,3,2,1,0:T(8,128)S(1)} %pad_maximum_fusion), channel_id=1, source_target_pairs={{0,1},{1,0},{2,3},{3,2},{4,5},{5,4},{6,7},{7,6},{8,9},{9,8},{10,11... | collective-permute-start | bytes 1572872 | tf_op jit(solution)/shard_map/ppermute | solution.py:896
  41.3 2.6 %copy-start.1 = (f32[4,2,16,8,128]{4,3,2,1,0:T(8,128)}, f32[4,2,16,8,128]{4,3,2,1,0:T(8,128)S(1)}, u32[]{:S(2)}) copy-start(f32[4,2,16,8,128]{4,3,2,1,0:T(8,128)S(1)} %pad_maximum_fusion.1.tod_here_ref) | copy-start | bytes 1572868
  41.3 2.6 %collective-permute-start.10 = (f32[4,2,16,8,128]{4,3,2,1,0:T(8,128)S(1)}, f32[4,2,16,8,128]{4,3,2,1,0:T(8,128)S(1)}, u32[]{:S(2)}, u32[]{:S(2)}) collective-permute-start(f32[4,2,16,8,128]{4,3,2,1,0:T(8,128)S(1)} %pad_maximum_fusion.1.tod_here_ref), channel_id=1, source_target_pairs={{0,1},{1,0},{2,3},{3,2},{4,5},{5,4},{6,7},{7,6},{8,9},{9,8},{10,11... | collective-permute-start | bytes 1572872 | tf_op jit(solution)/shard_map/ppermute | solution.py:976
  43.1 0.8 copy-start.3
  43.9 0.8 copy-start.4

commit v3 on v2

--- a/solution.py
+++ b/solution.py
@@ -159,6 +159,9 @@
 ROWS = 8
 OUT_TILES = 8
 PAIR_BATCH = 4
+DET_BATCH = 8
+SUM_SETS = 2
+MAP_BATCH = 8
 BIG = float(1 << 24)
 VMEM_BYTES = 60 << 20
 
@@ -249,14 +252,14 @@
 def table_copies(shape, self_ref, source_ref, part_ref, sem):
     wafers, dets, reps = shape[:3]
     copies = []
-    for swap_wafer in range(wafers):
-        for shift in range(dets):
+    for shift in range(dets):
+        for wafer in range(wafers):
             det = self_ref[1] - shift
             det = jnp.where(det < 0, det + dets, det)
-            device = ((self_ref[0] ^ swap_wafer) * dets + det) * reps
+            device = (wafer * dets + det) * reps
             copies.append(
                 pltpu.make_async_copy(
-                    source_ref.at[swap_wafer, shift], part_ref.at[pl.ds(device, reps)],
+                    source_ref.at[shift, wafer], part_ref.at[pl.ds(device, reps)],
                     sem.at[len(copies)],
                 )
             )
@@ -275,7 +278,7 @@
 
 def twin_kernel(
     shape, self_ref, table_ref, float_ref, whole_ref, size_ref, pair_ref, group_ref,
-    part_ref, column_ref, code_ref, lead_ref, part_sem,
+    part_ref, column_ref, code_ref, lead_ref, used_ref, part_sem,
 ):
     wafers, dets, reps, tiles, owners, capacity, owner_rows, lag_count = shape
     devices = wafers * dets * reps
@@ -328,18 +331,26 @@
         team = lax.rem(lax.div(key, reps * LANES), dets)
         return team * ROWS + lax.rem(lax.div(key, tiles), ROWS)
 
-    def take(state):
+    number_of = [lane + (sub + tile * ROWS) * LANES for tile in range(devices // ROWS)]
+    tile_rows = [slice(tile * ROWS, (tile + 1) * ROWS) for tile in range(devices // ROWS)]
+    for rows in tile_rows:
+        used_ref[rows, :] = jnp.zeros((ROWS, LANES), jnp.int32)
+
+    def take(as_pairs, state):
         pairs, grouped, code = state
         number = code.astype(jnp.int32)
         key = lax.div(number, total)
         lead = lax.rem(number, total)
         shift = (3 * (detector(key) - detector(lead))) & (PBLOCK - 1)
-        wanted = lead.astype(jnp.float32)
-        same = jnp.zeros((ROWS, LANES), jnp.float32)
-        for tile in range(devices // ROWS):
-            leads = lead_ref[tile * ROWS : (tile + 1) * ROWS, :]
-            same = same + jnp.where(leads == wanted, 1.0, 0.0)
-        alone = jnp.sum(same) < 1.5
+        alone = False
+        if as_pairs:
+            wanted = lead.astype(jnp.float32)
+            same = jnp.zeros((ROWS, LANES), jnp.float32)
+            for rows, numbers in zip(tile_rows, number_of):
+                same = same + jnp.where(lead_ref[rows, :] == wanted, 1.0, 0.0)
+                used = (numbers == key) | (numbers == lead)
+                used_ref[rows, :] = jnp.where(used, 1, used_ref[rows, :])
+            alone = jnp.sum(same) < 1.5
         entry = twin_entry(key, lead, shift)
         pair_ref[pairs] = entry
         group_ref[grouped] = entry
@@ -347,9 +358,23 @@
             pairs + jnp.where(alone, 1, 0), grouped + jnp.where(alone, 0, 1), next_code(code)
         )
 
+    def more(state):
+        return state[2] < BIG
+
+    none_yet = (jnp.int32(0), jnp.int32(0))
+    first_code = next_code(jnp.float32(-1.0))
     pairs, grouped, _ = lax.while_loop(
-        lambda state: state[2] < BIG, take,
-        (jnp.int32(0), jnp.int32(0), next_code(jnp.float32(-1.0))),
+        more, functools.partial(take, True), none_yet + (first_code,)
+    )
+    shared = jnp.zeros((ROWS, LANES), jnp.int32)
+    for rows in tile_rows:
+        used = used_ref[rows, :]
+        shared = shared + jnp.where((lane & ROWS) == 0, used * pltpu.roll(used, LANES - ROWS, 1), 0)
+    shared = jnp.sum(shared.astype(jnp.float32)) > 0.5
+    pairs, grouped = jnp.where(shared, 0, pairs), jnp.where(shared, 0, grouped)
+    _, grouped, _ = lax.while_loop(
+        more, functools.partial(take, False),
+        (pairs, grouped, jnp.where(shared, first_code, BIG)),
     )
     batches = lax.div(pairs + PAIR_BATCH - 1, PAIR_BATCH)
 
@@ -443,7 +468,7 @@
     shape, self_ref, size_ref, pair_ref, group_ref, move_ref, float_smem, whole_smem,
     angle_here_ref, angle_across_ref, angle_other_ref, tod_here_ref, tod_other_ref, column_ref,
     angle_ref, tod_ref, cos_ref, sin_ref, clean_ref, noise_ref, weight_ref,
-    inverse_ref, r_map, image_map, share_ref, rows_ref, sorted_ref, angle_sem, tod_sem, *more_refs,
+    share_ref, rows_ref, sorted_ref, angle_sem, tod_sem, *more_refs,
 ):
     wafers, dets, reps, tiles, owners, capacity, owner_rows, lag_count = shape
     devices = wafers * dets * reps
@@ -453,8 +478,12 @@
     lane, sub = tile_iotas()
     zero = jnp.zeros((ROWS, LANES), jnp.float32)
     low = lane < PBLOCK
-    d_maps, sum_refs = more_refs[:ITERS], more_refs[ITERS:]
-    first_sums, second_sums = sum_refs[:wafers], sum_refs[wafers:]
+    skies = [more_refs[3 * k : 3 * k + 3] for k in range(3 + ITERS)]
+    inverse_ref, r_map, image_map, *d_maps = skies
+    sum_refs = more_refs[3 * len(skies) :]
+    first_sums = [sum_refs[SUM_SETS * wafer : SUM_SETS * (wafer + 1)] for wafer in range(wafers)]
+    sum_refs = sum_refs[SUM_SETS * wafers :]
+    second_sums = [sum_refs[SUM_SETS * wafer : SUM_SETS * (wafer + 1)] for wafer in range(wafers)]
 
     def copies_of(source, to_ref, sem):
         return part_copies(
@@ -518,8 +547,8 @@
     for k, member in enumerate(members):
         share_ref[k] = 1.0 / jnp.maximum(zero + member.astype(jnp.float32), 1.0)
     for c in range(3):
-        image_map[count, c] = zero
-        r_map[count, c] = zero
+        image_map[c][count] = zero
+        r_map[c][count] = zero
 
     def clear_sorted(n, carry):
         at = pl.ds(pl.multiple_of(n * ROWS, ROWS), ROWS)
@@ -554,33 +583,37 @@
     def moved_from(target, spot, shift):
         at, half, row = spot
         result = []
-        for c in range(3):
-            values = wide(target[at, c, row, :])
+        for ref in target:
+            values = wide(ref[at, row, :])
             values = jnp.where((lane >> 6) == half, values, turn_half(values))
             result.append(pltpu.roll(values, shift, 1)[0:1])
         return result
 
     def merge_twins(target):
-        def add(spot, values):
-            at, half, row = spot
-            for c in range(3):
-                target[at, c, row, :] += jnp.where(in_half(half), values[c], 0.0)
-
         def pair_batch(n, carry):
             found = []
             for k in range(PAIR_BATCH):
                 key, lead, shift = twin_of(pair_ref[n * PAIR_BATCH + k])
                 key, lead = spot_of(key), spot_of(lead)
                 back = (PBLOCK - shift) & (PBLOCK - 1)
-                found.append((lead, moved_from(target, key, shift)))
-                found.append((key, moved_from(target, lead, back)))
-            for spot, values in found:
-                add(spot, values)
+                for spot, values in (
+                    (lead, moved_from(target, key, shift)), (key, moved_from(target, lead, back))
+                ):
+                    at, half, row = spot
+                    for c in range(3):
+                        values[c] = target[c][at, row, :] + jnp.where(in_half(half), values[c], 0.0)
+                    found.append((at, row, values))
+            for at, row, values in found:
+                for c in range(3):
+                    target[c][at, row, :] = values[c]
             return carry
 
         def gather_one(n, carry):
             key, lead, shift = twin_of(group_ref[n])
-            add(spot_of(lead), moved_from(target, spot_of(key), shift))
+            values = moved_from(target, spot_of(key), shift)
+            at, half, row = spot_of(lead)
+            for c in range(3):
+                target[c][at, row, :] += jnp.where(in_half(half), values[c], 0.0)
             return carry
 
         def spread_one(n, carry):
@@ -588,7 +621,7 @@
             values = moved_from(target, spot_of(lead), (PBLOCK - shift) & (PBLOCK - 1))
             at, half, row = spot_of(key)
             for c in range(3):
-                target[at, c, row, :] = jnp.where(in_half(half), values[c], target[at, c, row, :])
+                target[c][at, row, :] = jnp.where(in_half(half), values[c], target[c][at, row, :])
             return carry
 
         lax.fori_loop(0, size_ref[0], pair_batch, 0)
@@ -606,29 +639,41 @@
             cos_ref[2 * at + half] = first
             sin_ref[2 * at + half] = second
             squares.append((base * (first * first), base * (second * second)))
-        image_map[at, 0] = zero + (base + base)
+        image_map[0][at] = zero + (base + base)
         for c in range(2):
-            image_map[at, c + 1] = fold(squares[0][c], squares[1][c])
+            image_map[c + 1][at] = fold(squares[0][c], squares[1][c])
         return carry
 
     loop(count, survey, 0, 8)
 
     def clear_sums(refs):
-        for ref in refs:
+        for sets in refs:
+            for ref in sets:
+                for group in range(NSUB):
+                    for octet in range(octets):
+                        ref[group, rows_of(octet), :] = zero
+
+    def average(refs):
+        for wafer, sets in enumerate(refs):
             for group in range(NSUB):
                 for octet in range(octets):
-                    ref[group, rows_of(octet), :] = zero
-
-    def average(refs):
-        for wafer, ref in enumerate(refs):
-            for group in range(NSUB):
-                for octet in range(octets):
-                    ref[group, rows_of(octet), :] *= share_ref[wafer * NSUB + group]
+                    total = sets[0][group, rows_of(octet), :]
+                    for ref in sets[1:]:
+                        total = total + ref[group, rows_of(octet), :]
+                    sets[0][group, rows_of(octet), :] = total * share_ref[wafer * NSUB + group]
+
+    def over_detectors(body, carry):
+        def several(step, carry):
+            for k in range(DET_BATCH):
+                carry = body(step * DET_BATCH + k, k % SUM_SETS, carry)
+            return carry
+
+        return lax.fori_loop(0, wafer_dets // DET_BATCH, several, carry)
 
     def sum_streams(streams_of, carry):
         clear_sums(first_sums)
 
-        def one_detector(n, carry):
+        def one_detector(n, part, carry):
             for wafer in range(wafers):
                 group = group_of(wafer, n)
                 for rep in range(reps):
@@ -637,17 +682,17 @@
                     for half, stream in enumerate(streams):
                         rows = rows_of(2 * rep + half)
                         clean_ref[wafer * wafer_dets + n, rows, :] = stream
-                        first_sums[wafer][group, rows, :] += stream
+                        first_sums[wafer][part][group, rows, :] += stream
             return carry
 
-        carry = loop(wafer_dets, one_detector, carry, 4)
+        carry = over_detectors(one_detector, carry)
         average(first_sums)
         return carry
 
     def filter_streams():
         clear_sums(second_sums)
 
-        def one_filter(n, carry):
+        def one_filter(n, part, carry):
             for wafer in range(wafers):
                 device, inside = device_of(wafer, n), n & (ROWS - 1)
                 detector = wafer * wafer_dets + n
@@ -656,7 +701,8 @@
                 coefs = [float_smem[device, (j + 1) * ROWS + inside] for j in range(lag_count)]
                 lags = [whole_smem[device, (j + 1) * ROWS + inside] for j in range(lag_count)]
                 clean = [
-                    clean_ref[detector, rows_of(octet), :] - first_sums[wafer][group, rows_of(octet), :]
+                    clean_ref[detector, rows_of(octet), :]
+                    - first_sums[wafer][0][group, rows_of(octet), :]
                     for octet in range(octets)
                 ]
                 up = [pltpu.roll(here, ROWS - 1, 0) for here in clean] + [zero]
@@ -670,16 +716,16 @@
                         earlier = pltpu.roll(jnp.where(lane >= LANES - lag, ahead, here), lag, 1)
                         result = result + coef * (later + earlier)
                     noise_ref[detector, rows_of(octet), :] = result
-                    second_sums[wafer][group, rows_of(octet), :] += result
+                    second_sums[wafer][part][group, rows_of(octet), :] += result
                     carry = carry + here * result
             return carry
 
-        product = loop(wafer_dets, one_filter, zero, 4)
+        product = over_detectors(one_filter, zero)
         average(second_sums)
         return product
 
     def return_streams(target):
-        def one_return(n, carry):
+        def one_return(n, part, carry):
             for wafer in range(wafers):
                 group = group_of(wafer, n)
                 for rep in range(reps):
@@ -688,13 +734,13 @@
                     for half in range(2):
                         rows = rows_of(2 * rep + half)
                         stream = noise_ref[wafer * wafer_dets + n, rows, :]
-                        streams.append(stream - second_sums[wafer][group, rows, :])
-                    target[at, 0] = fold(*streams)
+                        streams.append(stream - second_sums[wafer][0][group, rows, :])
+                    target[0][at] = fold(*streams)
                     for c, ref in ((1, cos_ref), (2, sin_ref)):
-                        target[at, c] = fold(*(ref[2 * at + h] * streams[h] for h in range(2)))
+                        target[c][at] = fold(*(ref[2 * at + h] * streams[h] for h in range(2)))
             return carry
 
-        loop(wafer_dets, one_return, 0, 4)
+        over_detectors(one_return, 0)
         merge_twins(target)
 
     merge_twins(image_map)
@@ -707,13 +753,13 @@
     def begin(at, carry):
         parts = zero
         for c in range(3):
-            inverse = 1.0 / (image_map[at, c] + prior_weight)
-            inverse_ref[at, c] = inverse
-            residual = r_map[at, c]
+            inverse = 1.0 / (image_map[c][at] + prior_weight)
+            inverse_ref[c][at] = inverse
+            residual = r_map[c][at]
             parts = parts + residual * (inverse * residual)
         return carry + weight_ref[at] * parts
 
-    energy = whole_sum(loop(count, begin, zero, 8))
+    energy = whole_sum(loop(count, begin, zero, 16))
     factor = zero
     steps = []
     for iteration, d_map in enumerate(d_maps):
@@ -723,10 +769,10 @@
             squares = zero
             streams = [None, None]
             for c in range(3):
-                part = inverse_ref[at, c] * r_map[at, c]
+                part = inverse_ref[c][at] * r_map[c][at]
                 if iteration:
-                    part = part + factor * d_maps[iteration - 1][at, c]
-                d_map[at, c] = part
+                    part = part + factor * d_maps[iteration - 1][c][at]
+                d_map[c][at] = part
                 squares = squares + part * part
                 for half, seen in enumerate(unfold(part)):
                     if c == 0:
@@ -743,19 +789,26 @@
         steps.append(step)
 
         def new_residual(at, c):
-            return r_map[at, c] - step * (image_map[at, c] + prior_weight * d_map[at, c])
+            return r_map[c][at] - step * (image_map[c][at] + prior_weight * d_map[c][at])
 
         if not last:
 
-            def update(at, carry):
-                parts = zero
-                for c in range(3):
-                    residual = new_residual(at, c)
-                    r_map[at, c] = residual
-                    parts = parts + residual * (inverse_ref[at, c] * residual)
-                return carry + weight_ref[at] * parts
-
-            next_energy = whole_sum(loop(count, update, zero, 16))
+            def update(batch, carry):
+                found = []
+                for k in range(MAP_BATCH):
+                    at = batch * MAP_BATCH + k
+                    residual = [new_residual(at, c) for c in range(3)]
+                    parts = zero
+                    for c in range(3):
+                        parts = parts + residual[c] * (inverse_ref[c][at] * residual[c])
+                    carry = carry + weight_ref[at] * parts
+                    found.append((at, residual))
+                for at, residual in found:
+                    for c in range(3):
+                        r_map[c][at] = residual[c]
+                return carry
+
+            next_energy = whole_sum(loop(count // MAP_BATCH, update, zero, 2))
             factor = next_energy / energy
             energy = next_energy
         else:
@@ -766,9 +819,9 @@
                 inside = (lane & (PBLOCK - 1)) >= turn
                 values = []
                 for c in range(3):
-                    value = steps[0] * d_maps[0][at, c]
+                    value = steps[0] * d_maps[0][c][at]
                     for k in range(1, ITERS):
-                        value = value + steps[k] * d_maps[k][at, c]
+                        value = value + steps[k] * d_maps[k][c][at]
                     values.append(value)
                 values += [new_residual(at, c) for c in range(3)]
                 for c in range(3):
@@ -863,6 +916,7 @@
         and owner_rows % (LANES * OUT_TILES) == 0
         and groups + 1 <= 2 * LANES
         and devices % ROWS == 0
+        and dets % (DET_BATCH // ROWS) == 0
         and total * total < BIG
     )
 
@@ -912,15 +966,14 @@
     )
     angles, samples = (stream.reshape(tiles, ROWS, LANES) for stream in (angles, samples))
     place_here = jnp.stack([lax.axis_index(axis) for axis in ("wafer", "det", "rep")]).astype(i32)
-    tables = lax.all_gather(tables, "rep", axis=0, tiled=False)
-    riders = jnp.concatenate([angles, tables.reshape(2 * reps, ROWS, LANES)])
+    tables = lax.all_gather(tables, ("wafer", "rep"), axis=0, tiled=False)
+    riders = jnp.concatenate([angles, tables.reshape(2 * wafers * reps, ROWS, LANES)])
     samples, riders = lax.optimization_barrier((samples, riders))
     samples = jnp.stack([samples, other_wafer(samples)])
     blocks = along_det(riders)
     tables = jnp.stack([block[tiles:] for block in blocks])
+    tables = tables.reshape(dets, wafers, reps, 2, ROWS, LANES)
     angles = jnp.stack([block[:tiles] for block in blocks])
-    tables = jnp.stack([tables, other_wafer(tables)])
-    tables = tables.reshape(wafers, dets, reps, 2, ROWS, LANES)
     samples, angles, tables = lax.optimization_barrier((samples, angles, tables))
     angles_across = other_wafer(angles)
     samples = along_det(samples)
@@ -942,6 +995,7 @@
             pltpu.VMEM((devices, LANES, LANES), f32),
             pltpu.VMEM((devices, LANES), f32),
             pltpu.VMEM((devices, LANES), f32),
+            pltpu.VMEM((devices, LANES), i32),
             table_sem,
         ],
         compiler_params=params,
@@ -975,8 +1029,7 @@
     samples = jnp.stack(samples)
     sample_blocks = samples, lax.ppermute(samples, "rep", swap)
     stream = pltpu.VMEM((count, ROWS, LANES), f32)
-    sky = pltpu.VMEM((devices * ROWS, 3, ROWS, LANES), f32)
-    sky_and_spare = pltpu.VMEM((devices * ROWS + 1, 3, ROWS, LANES), f32)
+    sky = pltpu.VMEM((devices * ROWS + 1, ROWS, LANES), f32)
     group_sums = pltpu.VMEM((NSUB, octets * ROWS, LANES), f32)
     columns = pl.pallas_call(
         functools.partial(map_kernel, shape),
@@ -987,14 +1040,13 @@
             stream, stream, stream, stream,
             pltpu.VMEM((detectors, octets * ROWS, LANES), f32),
             pltpu.VMEM((detectors, octets * ROWS, LANES), f32),
-            pltpu.VMEM((devices * ROWS + 1, ROWS, LANES), f32),
-            sky, sky_and_spare, sky_and_spare,
+            sky,
             pltpu.VMEM((wafers * NSUB, ROWS, LANES), f32),
             pltpu.VMEM((total, 2 * height), f32),
             pltpu.VMEM((slots + LANES + ROWS, 2 * height), f32),
             pltpu.SemaphoreType.DMA((devices,)),
             pltpu.SemaphoreType.DMA((devices,)),
-        ] + [sky] * ITERS + [group_sums] * (2 * wafers),
+        ] + [sky] * (3 * (3 + ITERS)) + [group_sums] * (2 * wafers * SUM_SETS),
         compiler_params=params,
         name="map_maker",
     )(

time: 105 us -> 103 us (0.981); the launches traced: 104 us -> 104 us
  blocking collectives: 2.14 us -> 6.37 us
  starting transfers between devices: 15 us -> 12.7 us
  waiting for transfers between devices: 9.43 us -> 8.15 us
    all_gather x1, blocking collectives: 2.14 us -> 6.37 us  [whole_part(): tables = lax.all_gather(tables, ('wafer', 'rep'), axis=0, tiled=False)]
    ppermute x3 -> x2, waiting for transfers between devices: 5.68 us -> 2.97 us  [other_wafer(): return lax.ppermute(here, 'wafer', swap)]
    pallas_call x1, Pallas kernels: 38.6 us -> 36.6 us  [whole_part(): pl.pallas_call(functools.partial(map_kernel, shape), out_shape=jax.ShapeD...]
    ppermute x3 -> x2, starting transfers between devices: 4.54 us -> 2.98 us  [other_wafer(): return lax.ppermute(here, 'wafer', swap)]
    ppermute x6, waiting for transfers between devices: 1.72 us -> 3.15 us  [along_det(): lax.ppermute(block, 'det', [(i, (i + shift) % dets) for i in range(dets)])]
  transfers between devices with their start and end apart: 11 -> 10, of which waited for: 5 -> 4; matrix products, arithmetic and copies ran while one was open for 1% -> 1% of each run, Pallas kernels for 11% -> 12%
where the time goes in v3:
time: 103 us; the launch traced here: 104 us
  Pallas kernels  71.6 us (70%)
  starting transfers between devices  12.7 us (12%)
  waiting for transfers between devices  8.15 us (8%)
  blocking collectives  6.37 us (6%)
  other arithmetic  3.08 us (3%)
    pallas_call x1, Pallas kernels, whole_part(): pl.pallas_call(functools.partial(map_kernel, shape), out_shape=jax.ShapeD...  36.6 us
    pallas_call x1, Pallas kernels, whole_part(): pl.pallas_call(write_kernel, grid=(owner_rows // (OUT_TILES * LANES),), o...  21.1 us
    ppermute x6, starting transfers between devices, along_det(): lax.ppermute(block, 'det', [(i, (i + shift) % dets) for i in range(dets)])  9.08 us
    pallas_call x1, Pallas kernels, whole_part(): pl.pallas_call(functools.partial(twin_kernel, shape), out_shape=[jax.Shap...  7.35 us
    all_gather x1, blocking collectives, whole_part(): tables = lax.all_gather(tables, ('wafer', 'rep'), axis=0, tiled=False)  6.37 us
    pallas_call x1, Pallas kernels, whole_part(): pl.pallas_call(functools.partial(place_kernel, shape), out_shape=[jax.Sha...  4.95 us
    ppermute x6, waiting for transfers between devices, along_det(): lax.ppermute(block, 'det', [(i, (i + shift) % dets) for i in range(dets)])  3.15 us
    ppermute x2, starting transfers between devices, other_wafer(): return lax.ppermute(here, 'wafer', swap)  2.98 us
  transfers between devices with their start and end apart: 10, of which 4 were waited for; matrix products, arithmetic and copies ran while one was open for 1% of the time, Pallas kernels for 12%

profile of v3, /device:TPU:0, one launch (start us, length us, event | category | flops | bytes accessed | tf_op | source)
XLA Modules:
  0.0 103.7 jit_solution(5978307795019168298)
XLA Ops:
  0.6 1.7 %pack.1 = (f32[2,8,128]{2,1,0:T(8,128)}, f32[8,16,128]{2,1,0:T(8,128)}, f32[8,16,128]{2,1,0:T(8,128)}) custom-call(f32[8,2048]{1,0:T(8,128)} %bitcast.48, f32[8,2048]{1,0:T(8,128)} %bitcast.49, s32[8,16]{1,0:T(8,128)} %bitcast.53, s32[8,32]{1,0:T(8,128)} %bitcast.54, s32[1,8]{1,0:T(1,128)} %group_ref.1, f32[1,8]{1,0:T(1,128)} %base_ref.1, f32[4,8]{1,0:T(4,128)} %bitcast.55, ...), custom_call_target="tpu_custom_call" | custom-call | tf_op jit(solution)/shard_map/pack/pallas_call | solution.py:952
  2.3 6.4 %all-gather = f32[8,8,128]{2,1,0:T(8,128)S(1)} all-gather(f32[2,8,128]{2,1,0:T(8,128)} %get-tuple-element.36), channel_id=2, replica_groups=mesh['groups'=2,'det'=4,'wafer'=2,'rep'=2] {'wafer','rep'}, dimensions={0}, use_global_device_ids=true | all-gather | bytes 40960 | tf_op jit(solution)/shard_map/all_gather | solution.py:969
  8.7 0.8 pad_maximum_fusion.5
  9.5 4.1 %collective-permute-start.3 = (f32[24,8,128]{2,1,0:T(8,128)S(1)}, f32[24,8,128]{2,1,0:T(8,128)S(1)}, u32[]{:S(2)}, u32[]{:S(2)}) collective-permute-start(f32[24,8,128]{2,1,0:T(8,128)S(1)} %pad_maximum_fusion.5), channel_id=1, source_target_pairs={{0,12},{4,0},{8,4},{12,8},{1,13},{5,1},{9,5},{13,9},{2,14},{6,2},{... | collective-permute-start | bytes 294920 | tf_op jit(solution)/shard_map/ppermute | solution.py:941
  13.6 1.0 collective-permute-start.1
  14.6 1.5 %collective-permute-start = (f32[16,8,128]{2,1,0:T(8,128)}, f32[16,8,128]{2,1,0:T(8,128)S(1)}, u32[]{:S(2)}, u32[]{:S(2)}) collective-permute-start(f32[16,8,128]{2,1,0:T(8,128)} %bitcast.50), channel_id=1, source_target_pairs={{0,2},{2,0},{1,3},{3,1},{4,6},{6,4},{5,7},{7,5},{8,10},{10,8},{9,1... | collective-permute-start | bytes 196616 | tf_op jit(solution)/shard_map/ppermute | solution.py:947
  16.1 3.0 %collective-permute-done = f32[16,8,128]{2,1,0:T(8,128)S(1)} collective-permute-done((f32[16,8,128]{2,1,0:T(8,128)}, f32[16,8,128]{2,1,0:T(8,128)S(1)}, u32[]{:S(2)}, u32[]{:S(2)}) %collective-permute-start) | collective-permute-done | bytes 65568 | tf_op jit(solution)/shard_map/ppermute | solution.py:947
  19.1 0.8 pad_maximum_fusion.3
  20.0 3.1 %collective-permute-done.2 = f32[24,8,128]{2,1,0:T(8,128)S(1)} collective-permute-done((f32[24,8,128]{2,1,0:T(8,128)S(1)}, f32[24,8,128]{2,1,0:T(8,128)S(1)}, u32[]{:S(2)}, u32[]{:S(2)}) %collective-permute-start.2) | collective-permute-done | bytes 98336 | tf_op jit(solution)/shard_map/ppermute | solution.py:941
  23.2 0.7 pad_maximum_fusion.4.table_ref
  23.9 1.5 %collective-permute-start.4 = (f32[4,16,8,128]{3,2,1,0:T(8,128)S(1)}, f32[4,16,8,128]{3,2,1,0:T(8,128)S(1)}, u32[]{:S(2)}, u32[]{:S(2)}) collective-permute-start(f32[4,16,8,128]{3,2,1,0:T(8,128)S(1)} %pad_maximum_fusion.2.angle_here_ref), channel_id=1, source_target_pairs={{0,2},{2,0},{1,3},{3,1},{4,6},{6,4},{5,7},{7,5},{8,10},{10,8},{9,1... | collective-permute-start | bytes 786440 | tf_op jit(solution)/shard_map/ppermute | solution.py:947
  25.4 0.6 pad_add_fusion.self_ref
  26.0 1.6 %collective-permute-start.7 = (f32[2,16,8,128]{3,2,1,0:T(8,128)S(1)}, f32[2,16,8,128]{3,2,1,0:T(8,128)S(1)}, u32[]{:S(2)}, u32[]{:S(2)}) collective-permute-start(f32[2,16,8,128]{3,2,1,0:T(8,128)S(1)} %pad_maximum_fusion.3), channel_id=1, source_target_pairs={{0,12},{4,0},{8,4},{12,8},{1,13},{5,1},{9,5},{13,9},{2,14},{6,2},{... | collective-permute-start | bytes 393224 | tf_op jit(solution)/shard_map/ppermute | solution.py:941
  27.6 0.4 collective-permute-start.6
  28.0 2.0 %collective-permute-start.5 = (f32[2,16,8,128]{3,2,1,0:T(8,128)S(1)}, f32[2,16,8,128]{3,2,1,0:T(8,128)S(1)}, u32[]{:S(2)}, u32[]{:S(2)}) collective-permute-start(f32[2,16,8,128]{3,2,1,0:T(8,128)S(1)} %pad_maximum_fusion.3), channel_id=1, source_target_pairs={{0,4},{4,8},{8,12},{12,0},{1,5},{5,9},{9,13},{13,1},{2,6},{6,10},{... | collective-permute-start | bytes 393224 | tf_op jit(solution)/shard_map/ppermute | solution.py:941
  30.0 7.3 %twins.1 = (f32[16,128]{1,0:T(8,128)}, s32[16,128]{1,0:T(8,128)}, s32[2]{0:T(128)}, s32[2048]{0:T(1024)}, s32[2048]{0:T(1024)}) custom-call(s32[3]{0:T(128)} %pad_add_fusion.self_ref, f32[4,2,2,2,8,128]{5,4,3,2,1,0:T(8,128)} %pad_maximum_fusion.4.table_ref), custom_call_target="tpu_custom_call" | custom-call | flops 1000000000 | bytes 30000000 | tf_op jit(solution)/shard_map/twins/pallas_call | solution.py:982
  37.4 4.9 %places.1 = (s32[256,128]{1,0:T(8,128)}, s32[8,256]{1,0:T(8,128)}, s32[16,128]{1,0:T(8,128)}) custom-call(s32[3]{0:T(128)} %pad_add_fusion.self_ref, f32[4,2,2,2,8,128]{5,4,3,2,1,0:T(8,128)} %pad_maximum_fusion.4.table_ref), custom_call_target="tpu_custom_call" | custom-call | flops 1000000000 | bytes 20000000 | tf_op jit(solution)/shard_map/places/pallas_call | solution.py:1005
  42.4 0.1 collective-permute-start.8
  42.5 0.6 collective-permute-start.9
  43.1 1.3 %collective-permute-done.8.angle_other_ref = f32[2,4,16,8,128]{4,3,2,1,0:T(8,128)S(1)} collective-permute-done((f32[2,4,16,8,128]{4,3,2,1,0:T(8,128)S(1)}, f32[2,4,16,8,128]{4,3,2,1,0:T(8,128)S(1)}, u32[]{:S(2)}, u32[]{:S(2)}) %collective-permute-start.8) | collective-permute-done | bytes 524320 | tf_op jit(solution)/shard_map/ppermute | solution.py:950
  44.4 0.7 collective-permute-done.9.tod_other_ref
  45.2 0.8 copy-done.4
  46.0 36.6 %map_maker.1.column_ref = bf16[5,384,256]{2,1,0:T(8,128)(2,1)} custom-call(s32[3]{0:T(128)} %pad_add_fusion.self_ref, s32[2]{0:T(128)} %get-tuple-element.51.size_ref, s32[2048]{0:T(1024)} %get-tuple-element.52.pair_ref, s32[2048]{0:T(1024)} %get-tuple-element.53.group_ref, s32[16,128]{1,0:T(8,128)} %get-tuple-element.54.move_ref, ...), custom_call_target="tpu_custom_call" | custom-call | tf_op jit(solution)/shard_map/map_maker/pallas_call | solution.py:1034
  82.6 21.1 %write.1 = (f32[192,24576]{1,0:T(8,128)}, f32[192,24576]{1,0:T(8,128)}) custom-call(s32[8,256]{1,0:T(8,128)} %get-tuple-element.50.start_ref, bf16[5,384,256]{2,1,0:T(8,128)(2,1)} %map_maker.1.column_ref, s32[256,128]{1,0:T(8,128)} %get-tuple-element.63.place_ref), custom_call_target="tpu_custom_call" | custom-call | tf_op jit(solution)/shard_map/write/pallas_call | solution.py:1057
  (27 shorter events, 0.2 us)
Async XLA Ops:
  9.5 10.4 %collective-permute-start.3 = (f32[24,8,128]{2,1,0:T(8,128)S(1)}, f32[24,8,128]{2,1,0:T(8,128)S(1)}, u32[]{:S(2)}, u32[]{:S(2)}) collective-permute-start(f32[24,8,128]{2,1,0:T(8,128)S(1)} %pad_maximum_fusion.5), channel_id=1, source_target_pairs={{0,12},{4,0},{8,4},{12,8},{1,13},{5,1},{9,5},{13,9},{2,14},{6,2},{... | collective-permute-start | bytes 294920 | tf_op jit(solution)/shard_map/ppermute | solution.py:941
  13.6 9.5 %collective-permute-start.2 = (f32[24,8,128]{2,1,0:T(8,128)S(1)}, f32[24,8,128]{2,1,0:T(8,128)S(1)}, u32[]{:S(2)}, u32[]{:S(2)}) collective-permute-start(f32[24,8,128]{2,1,0:T(8,128)S(1)} %pad_maximum_fusion.5), channel_id=1, source_target_pairs={{0,8},{4,12},{8,0},{12,4},{1,9},{5,13},{9,1},{13,5},{2,10},{6,14},... | collective-permute-start | bytes 294920 | tf_op jit(solution)/shard_map/ppermute | solution.py:941
  13.6 9.5 %collective-permute-start.1 = (f32[24,8,128]{2,1,0:T(8,128)S(1)}, f32[24,8,128]{2,1,0:T(8,128)S(1)}, u32[]{:S(2)}, u32[]{:S(2)}) collective-permute-start(f32[24,8,128]{2,1,0:T(8,128)S(1)} %pad_maximum_fusion.5), channel_id=1, source_target_pairs={{0,4},{4,8},{8,12},{12,0},{1,5},{5,9},{9,13},{13,1},{2,6},{6,10},{... | collective-permute-start | bytes 294920 | tf_op jit(solution)/shard_map/ppermute | solution.py:941
  14.6 4.5 %collective-permute-start = (f32[16,8,128]{2,1,0:T(8,128)}, f32[16,8,128]{2,1,0:T(8,128)S(1)}, u32[]{:S(2)}, u32[]{:S(2)}) collective-permute-start(f32[16,8,128]{2,1,0:T(8,128)} %bitcast.50), channel_id=1, source_target_pairs={{0,2},{2,0},{1,3},{3,1},{4,6},{6,4},{5,7},{7,5},{8,10},{10,8},{9,1... | collective-permute-start | bytes 196616 | tf_op jit(solution)/shard_map/ppermute | solution.py:947
  23.2 22.0 %copy-start = (f32[4,16,8,128]{3,2,1,0:T(8,128)}, f32[4,16,8,128]{3,2,1,0:T(8,128)S(1)}, u32[]{:S(2)}) copy-start(f32[4,16,8,128]{3,2,1,0:T(8,128)S(1)} %pad_maximum_fusion.2.angle_here_ref) | copy-start | bytes 786436
  23.9 18.4 %collective-permute-start.4 = (f32[4,16,8,128]{3,2,1,0:T(8,128)S(1)}, f32[4,16,8,128]{3,2,1,0:T(8,128)S(1)}, u32[]{:S(2)}, u32[]{:S(2)}) collective-permute-start(f32[4,16,8,128]{3,2,1,0:T(8,128)S(1)} %pad_maximum_fusion.2.angle_here_ref), channel_id=1, source_target_pairs={{0,2},{2,0},{1,3},{3,1},{4,6},{6,4},{5,7},{7,5},{8,10},{10,8},{9,1... | collective-permute-start | bytes 786440 | tf_op jit(solution)/shard_map/ppermute | solution.py:947
  26.0 16.3 %collective-permute-start.7 = (f32[2,16,8,128]{3,2,1,0:T(8,128)S(1)}, f32[2,16,8,128]{3,2,1,0:T(8,128)S(1)}, u32[]{:S(2)}, u32[]{:S(2)}) collective-permute-start(f32[2,16,8,128]{3,2,1,0:T(8,128)S(1)} %pad_maximum_fusion.3), channel_id=1, source_target_pairs={{0,12},{4,0},{8,4},{12,8},{1,13},{5,1},{9,5},{13,9},{2,14},{6,2},{... | collective-permute-start | bytes 393224 | tf_op jit(solution)/shard_map/ppermute | solution.py:941
  27.6 14.7 %collective-permute-start.6 = (f32[2,16,8,128]{3,2,1,0:T(8,128)S(1)}, f32[2,16,8,128]{3,2,1,0:T(8,128)S(1)}, u32[]{:S(2)}, u32[]{:S(2)}) collective-permute-start(f32[2,16,8,128]{3,2,1,0:T(8,128)S(1)} %pad_maximum_fusion.3), channel_id=1, source_target_pairs={{0,8},{4,12},{8,0},{12,4},{1,9},{5,13},{9,1},{13,5},{2,10},{6,14},... | collective-permute-start | bytes 393224 | tf_op jit(solution)/shard_map/ppermute | solution.py:941
  28.0 14.4 %collective-permute-start.5 = (f32[2,16,8,128]{3,2,1,0:T(8,128)S(1)}, f32[2,16,8,128]{3,2,1,0:T(8,128)S(1)}, u32[]{:S(2)}, u32[]{:S(2)}) collective-permute-start(f32[2,16,8,128]{3,2,1,0:T(8,128)S(1)} %pad_maximum_fusion.3), channel_id=1, source_target_pairs={{0,4},{4,8},{8,12},{12,0},{1,5},{5,9},{9,13},{13,1},{2,6},{6,10},{... | collective-permute-start | bytes 393224 | tf_op jit(solution)/shard_map/ppermute | solution.py:941
  42.4 2.8 %copy-start.2 = (f32[4,16,8,128]{3,2,1,0:T(8,128)}, f32[4,16,8,128]{3,2,1,0:T(8,128)S(1)}, u32[]{:S(2)}) copy-start(f32[4,16,8,128]{3,2,1,0:T(8,128)S(1)} %collective-permute-done.4.angle_across_ref) | copy-start | bytes 786436
  42.4 2.0 %collective-permute-start.8 = (f32[2,4,16,8,128]{4,3,2,1,0:T(8,128)S(1)}, f32[2,4,16,8,128]{4,3,2,1,0:T(8,128)S(1)}, u32[]{:S(2)}, u32[]{:S(2)}) collective-permute-start(f32[2,4,16,8,128]{4,3,2,1,0:T(8,128)S(1)} %pad_maximum_fusion), channel_id=1, source_target_pairs={{0,1},{1,0},{2,3},{3,2},{4,5},{5,4},{6,7},{7,6},{8,9},{9,8},{10,11... | collective-permute-start | bytes 1572872 | tf_op jit(solution)/shard_map/ppermute | solution.py:950
  42.5 2.6 %copy-start.1 = (f32[4,2,16,8,128]{4,3,2,1,0:T(8,128)}, f32[4,2,16,8,128]{4,3,2,1,0:T(8,128)S(1)}, u32[]{:S(2)}) copy-start(f32[4,2,16,8,128]{4,3,2,1,0:T(8,128)S(1)} %pad_maximum_fusion.1.tod_here_ref) | copy-start | bytes 1572868
  42.5 2.6 %collective-permute-start.9 = (f32[4,2,16,8,128]{4,3,2,1,0:T(8,128)S(1)}, f32[4,2,16,8,128]{4,3,2,1,0:T(8,128)S(1)}, u32[]{:S(2)}, u32[]{:S(2)}) collective-permute-start(f32[4,2,16,8,128]{4,3,2,1,0:T(8,128)S(1)} %pad_maximum_fusion.1.tod_here_ref), channel_id=1, source_target_pairs={{0,1},{1,0},{2,3},{3,2},{4,5},{5,4},{6,7},{7,6},{8,9},{9,8},{10,11... | collective-permute-start | bytes 1572872 | tf_op jit(solution)/shard_map/ppermute | solution.py:1030
  44.4 0.8 copy-start.3
  45.2 0.8 copy-start.4

commit v4 on v3

--- a/solution.py
+++ b/solution.py
@@ -158,7 +158,8 @@
 LANES = 128
 ROWS = 8
 OUT_TILES = 8
-PAIR_BATCH = 4
+PAIR_BATCH = 8
+WRITES = 6
 DET_BATCH = 8
 SUM_SETS = 2
 MAP_BATCH = 8
@@ -252,14 +253,14 @@
 def table_copies(shape, self_ref, source_ref, part_ref, sem):
     wafers, dets, reps = shape[:3]
     copies = []
-    for shift in range(dets):
-        for wafer in range(wafers):
+    for swap_wafer in range(wafers):
+        for shift in range(dets):
             det = self_ref[1] - shift
             det = jnp.where(det < 0, det + dets, det)
-            device = (wafer * dets + det) * reps
+            device = ((self_ref[0] ^ swap_wafer) * dets + det) * reps
             copies.append(
                 pltpu.make_async_copy(
-                    source_ref.at[shift, wafer], part_ref.at[pl.ds(device, reps)],
+                    source_ref.at[swap_wafer, shift], part_ref.at[pl.ds(device, reps)],
                     sem.at[len(copies)],
                 )
             )
@@ -276,9 +277,23 @@
     )
 
 
-def twin_kernel(
-    shape, self_ref, table_ref, float_ref, whole_ref, size_ref, pair_ref, group_ref,
-    part_ref, column_ref, code_ref, lead_ref, used_ref, part_sem,
+def list_kernel(
+    shape, wafer_ref, det_ref, table_ref, float_ref, whole_ref, place_ref, start_ref, move_ref,
+    size_ref, pair_ref, group_ref,
+    part_ref, column_ref, code_ref, lead_ref, used_ref, rank_ref, hits_ref, part_sem,
+):
+    self_ref = wafer_ref[0], det_ref[0]
+    table_copies(shape, self_ref, table_ref, part_ref, part_sem)
+    list_twins(
+        shape, float_ref, whole_ref, size_ref, pair_ref, group_ref, part_ref, column_ref, code_ref,
+        lead_ref, used_ref,
+    )
+    list_places(shape, self_ref, place_ref, start_ref, move_ref, part_ref, rank_ref, hits_ref)
+
+
+def list_twins(
+    shape, float_ref, whole_ref, size_ref, pair_ref, group_ref, part_ref, column_ref, code_ref,
+    lead_ref, used_ref,
 ):
     wafers, dets, reps, tiles, owners, capacity, owner_rows, lag_count = shape
     devices = wafers * dets * reps
@@ -287,7 +302,6 @@
     sub_f = sub.astype(jnp.float32)
     none = jnp.full((ROWS, LANES), BIG, jnp.float32)
     along = lax.broadcasted_iota(jnp.int32, (1, LANES), 1).astype(jnp.float32)
-    table_copies(shape, self_ref, table_ref, part_ref, part_sem)
 
     def turn(batch, carry):
         for k in range(4):
@@ -302,15 +316,19 @@
     def survey(device, carry):
         row = wide(part_ref[device, 0, 0:1, :])
 
-        def compare(other, least):
-            found = [none] * 4
-            for j in range(tiles):
-                same = column_ref[other, j * ROWS : (j + 1) * ROWS, :] == row
-                found[j % 4] = jnp.minimum(found[j % 4], jnp.where(same, sub_f + float(j * ROWS), BIG))
-            here = jnp.minimum(jnp.minimum(found[0], found[1]), jnp.minimum(found[2], found[3]))
-            return jnp.minimum(least, here + (other * LANES).astype(jnp.float32))
-
-        least = lax.fori_loop(0, device + 1, compare, none)
+        def compare(step, least):
+            for k in range(2):
+                other = 2 * step + k
+                found = [none] * 4
+                for j in range(tiles):
+                    same = column_ref[other, j * ROWS : (j + 1) * ROWS, :] == row
+                    at = jnp.where(same, sub_f + float(j * ROWS), BIG)
+                    found[j % 4] = jnp.minimum(found[j % 4], at)
+                here = jnp.minimum(jnp.minimum(found[0], found[1]), jnp.minimum(found[2], found[3]))
+                least = jnp.minimum(least, here + (other * LANES).astype(jnp.float32))
+            return least
+
+        least = lax.fori_loop(0, lax.shift_right_logical(device, 1) + 1, compare, none)
         lead = jnp.min(least, axis=0, keepdims=True)
         mine = (device * LANES).astype(jnp.float32) + along
         later = lead < mine
@@ -336,21 +354,24 @@
     for rows in tile_rows:
         used_ref[rows, :] = jnp.zeros((ROWS, LANES), jnp.int32)
 
-    def take(as_pairs, state):
+    def take(state):
         pairs, grouped, code = state
         number = code.astype(jnp.int32)
         key = lax.div(number, total)
         lead = lax.rem(number, total)
         shift = (3 * (detector(key) - detector(lead))) & (PBLOCK - 1)
-        alone = False
-        if as_pairs:
-            wanted = lead.astype(jnp.float32)
-            same = jnp.zeros((ROWS, LANES), jnp.float32)
-            for rows, numbers in zip(tile_rows, number_of):
-                same = same + jnp.where(lead_ref[rows, :] == wanted, 1.0, 0.0)
-                used = (numbers == key) | (numbers == lead)
-                used_ref[rows, :] = jnp.where(used, 1, used_ref[rows, :])
-            alone = jnp.sum(same) < 1.5
+        wanted = lead.astype(jnp.float32)
+        same = jnp.zeros((ROWS, LANES), jnp.float32)
+        for rows, numbers in zip(tile_rows, number_of):
+            same = same + jnp.where(lead_ref[rows, :] == wanted, 1.0, 0.0)
+            beside = numbers ^ ROWS
+            beside = (beside == key) | (beside == lead)
+            same = same + jnp.where(beside & (used_ref[rows, :] > 0), 2.0, 0.0)
+        alone = jnp.sum(same) + jnp.where((key ^ lead) == ROWS, 2.0, 0.0) < 1.5
+        mark = jnp.where(alone, 1, 0)
+        for rows, numbers in zip(tile_rows, number_of):
+            listed = (numbers == key) | (numbers == lead)
+            used_ref[rows, :] = jnp.where(listed, mark, used_ref[rows, :])
         entry = twin_entry(key, lead, shift)
         pair_ref[pairs] = entry
         group_ref[grouped] = entry
@@ -358,23 +379,9 @@
             pairs + jnp.where(alone, 1, 0), grouped + jnp.where(alone, 0, 1), next_code(code)
         )
 
-    def more(state):
-        return state[2] < BIG
-
-    none_yet = (jnp.int32(0), jnp.int32(0))
-    first_code = next_code(jnp.float32(-1.0))
     pairs, grouped, _ = lax.while_loop(
-        more, functools.partial(take, True), none_yet + (first_code,)
-    )
-    shared = jnp.zeros((ROWS, LANES), jnp.int32)
-    for rows in tile_rows:
-        used = used_ref[rows, :]
-        shared = shared + jnp.where((lane & ROWS) == 0, used * pltpu.roll(used, LANES - ROWS, 1), 0)
-    shared = jnp.sum(shared.astype(jnp.float32)) > 0.5
-    pairs, grouped = jnp.where(shared, 0, pairs), jnp.where(shared, 0, grouped)
-    _, grouped, _ = lax.while_loop(
-        more, functools.partial(take, False),
-        (pairs, grouped, jnp.where(shared, first_code, BIG)),
+        lambda state: state[2] < BIG, take,
+        (jnp.int32(0), jnp.int32(0), next_code(jnp.float32(-1.0))),
     )
     batches = lax.div(pairs + PAIR_BATCH - 1, PAIR_BATCH)
 
@@ -395,17 +402,13 @@
     return entry >> 19, (entry >> 6) & ((1 << 13) - 1), entry & (PBLOCK - 1)
 
 
-def place_kernel(
-    shape, self_ref, table_ref, place_ref, start_ref, move_ref, part_ref, rank_ref, hits_ref,
-    part_sem,
-):
+def list_places(shape, self_ref, place_ref, start_ref, move_ref, part_ref, rank_ref, hits_ref):
     wafers, dets, reps, tiles, owners, capacity, owner_rows, lag_count = shape
     devices = wafers * dets * reps
     slots = devices * capacity
     lane, sub = tile_iotas()
     own = self_ref[1] * wafers + self_ref[0]
     first_row = (own * owner_rows).astype(jnp.float32)
-    table_copies(shape, self_ref, table_ref, part_ref, part_sem)
     depth = 2 * LANES
     tall = lax.broadcasted_iota(jnp.int32, (depth, LANES), 0).astype(jnp.float32)
 
@@ -465,7 +468,7 @@
 
 
 def map_kernel(
-    shape, self_ref, size_ref, pair_ref, group_ref, move_ref, float_smem, whole_smem,
+    shape, wafer_ref, det_ref, rep_ref, size_ref, pair_ref, group_ref, move_ref, float_smem, whole_smem,
     angle_here_ref, angle_across_ref, angle_other_ref, tod_here_ref, tod_other_ref, column_ref,
     angle_ref, tod_ref, cos_ref, sin_ref, clean_ref, noise_ref, weight_ref,
     share_ref, rows_ref, sorted_ref, angle_sem, tod_sem, *more_refs,
@@ -474,6 +477,7 @@
     devices = wafers * dets * reps
     octets = 2 * reps
     wafer_dets = dets * ROWS
+    self_ref = wafer_ref[0], det_ref[0], rep_ref[0]
     count = devices * ROWS
     lane, sub = tile_iotas()
     zero = jnp.zeros((ROWS, LANES), jnp.float32)
@@ -860,15 +864,20 @@
     lax.fori_loop(0, column_ref.shape[0], turn_tile, 0)
 
 
-def write_kernel(start_ref, column_ref, place_ref, x_ref, r_ref):
+def write_kernel(start_ref, column_ref, place_ref, x_ref, r_ref, x_buffer, r_buffer, x_sem, r_sem):
     height = 3 * PBLOCK
+    width = OUT_TILES * LANES
+    steps = x_ref.shape[1] // width
     depth = lax.broadcasted_iota(jnp.int32, (LANES, LANES), 0)
-    group = pl.program_id(0) * OUT_TILES
-    start, end = start_ref[0, group], start_ref[0, group + OUT_TILES]
-    first = lax.shift_right_logical(start, 7)
-    last = lax.shift_right_logical(jnp.maximum(end - 1, start), 7)
-
-    def spread(tile):
+
+    def copies(step, slot):
+        to = pl.ds(pl.multiple_of(step * width, width), width)
+        return (
+            pltpu.make_async_copy(x_buffer.at[slot], x_ref.at[:, to], x_sem.at[slot]),
+            pltpu.make_async_copy(r_buffer.at[slot], r_ref.at[:, to], r_sem.at[slot]),
+        )
+
+    def spread(group, tile):
         chosen = []
         for k in range(OUT_TILES):
             place = jnp.broadcast_to(place_ref[pl.ds(group + k, 1), :], (LANES, LANES))
@@ -877,17 +886,37 @@
         chosen = jnp.concatenate([chosen, chosen], axis=0)
         return jnp.dot(column_ref[tile], chosen, preferred_element_type=jnp.float32)
 
-    values = spread(first)
-    x_ref[...] = values[:height]
-    r_ref[...] = values[height:]
-
-    def add_tile(tile, carry):
-        values = spread(tile)
-        x_ref[...] += values[:height]
-        r_ref[...] += values[height:]
+    def one_step(step, carry):
+        slot = lax.rem(step, WRITES)
+
+        @pl.when(step >= WRITES)
+        def _():
+            for copy in copies(step - WRITES, slot):
+                copy.wait()
+
+        group = step * OUT_TILES
+        start, end = start_ref[0, group], start_ref[0, group + OUT_TILES]
+        first = lax.shift_right_logical(start, 7)
+        last = lax.shift_right_logical(jnp.maximum(end - 1, start), 7)
+        values = spread(group, first)
+        x_buffer[slot] = values[:height]
+        r_buffer[slot] = values[height:]
+
+        def add_tile(tile, carry):
+            values = spread(group, tile)
+            x_buffer[slot] += values[:height]
+            r_buffer[slot] += values[height:]
+            return carry
+
+        lax.fori_loop(first + 1, last + 1, add_tile, 0)
+        for copy in copies(step, slot):
+            copy.start()
         return carry
 
-    lax.fori_loop(first + 1, last + 1, add_tile, 0)
+    lax.fori_loop(0, steps, one_step, 0)
+    for step in range(steps - WRITES, steps):
+        for copy in copies(step, step % WRITES):
+            copy.wait()
 
 
 def part_shape(sizes, tod, hit_list, band_lag):
@@ -914,6 +943,7 @@
         and capacity <= LANES
         and devices * capacity % LANES == 0
         and owner_rows % (LANES * OUT_TILES) == 0
+        and owner_rows >= LANES * OUT_TILES * WRITES
         and groups + 1 <= 2 * LANES
         and devices % ROWS == 0
         and dets % (DET_BATCH // ROWS) == 0
@@ -965,66 +995,54 @@
         band_lag[0].T,
     )
     angles, samples = (stream.reshape(tiles, ROWS, LANES) for stream in (angles, samples))
-    place_here = jnp.stack([lax.axis_index(axis) for axis in ("wafer", "det", "rep")]).astype(i32)
-    tables = lax.all_gather(tables, ("wafer", "rep"), axis=0, tiled=False)
-    riders = jnp.concatenate([angles, tables.reshape(2 * wafers * reps, ROWS, LANES)])
+    place_here = [
+        lax.axis_index(axis).astype(i32).reshape(1) for axis in ("wafer", "det", "rep")
+    ]
+    tables = lax.all_gather(tables, "rep", axis=0, tiled=False)
+    riders = jnp.concatenate([angles, tables.reshape(2 * reps, ROWS, LANES)])
     samples, riders = lax.optimization_barrier((samples, riders))
     samples = jnp.stack([samples, other_wafer(samples)])
     blocks = along_det(riders)
     tables = jnp.stack([block[tiles:] for block in blocks])
-    tables = tables.reshape(dets, wafers, reps, 2, ROWS, LANES)
     angles = jnp.stack([block[:tiles] for block in blocks])
+    tables = jnp.stack([tables, other_wafer(tables)])
+    tables = tables.reshape(wafers, dets, reps, 2, ROWS, LANES)
     samples, angles, tables = lax.optimization_barrier((samples, angles, tables))
     angles_across = other_wafer(angles)
     samples = along_det(samples)
-    table_scratch = pltpu.VMEM((devices, 2, ROWS, LANES), f32)
-    table_sem = pltpu.SemaphoreType.DMA((devices,))
-    twins = pl.pallas_call(
-        functools.partial(twin_kernel, shape),
+    table_rows = jax.ShapeDtypeStruct((devices, LANES), i32)
+    lists = pl.pallas_call(
+        functools.partial(list_kernel, shape),
         out_shape=[
             jax.ShapeDtypeStruct((devices, LANES), f32),
-            jax.ShapeDtypeStruct((devices, LANES), i32),
+            table_rows,
+            jax.ShapeDtypeStruct((2 * LANES, LANES), i32),
+            jax.ShapeDtypeStruct((ROWS, 2 * LANES), i32),
+            table_rows,
             jax.ShapeDtypeStruct((2,), i32),
             jax.ShapeDtypeStruct((total,), i32),
             jax.ShapeDtypeStruct((total,), i32),
         ],
-        in_specs=[smem, anywhere],
-        out_specs=[vmem] * 2 + [smem] * 3,
+        in_specs=[smem, smem, anywhere],
+        out_specs=[vmem] * 5 + [smem] * 3,
         scratch_shapes=[
-            table_scratch,
+            pltpu.VMEM((devices, 2, ROWS, LANES), f32),
             pltpu.VMEM((devices, LANES, LANES), f32),
             pltpu.VMEM((devices, LANES), f32),
             pltpu.VMEM((devices, LANES), f32),
             pltpu.VMEM((devices, LANES), i32),
-            table_sem,
+            pltpu.VMEM((devices, LANES), i32),
+            pltpu.VMEM((devices, LANES), i32),
+            pltpu.SemaphoreType.DMA((devices,)),
         ],
         compiler_params=params,
-        cost_estimate=pl.CostEstimate(flops=10**9, bytes_accessed=3 * 10**7, transcendentals=0),
-        name="twins",
-    )(place_here, tables)
-    place, start, moves = pl.pallas_call(
-        functools.partial(place_kernel, shape),
-        out_shape=[
-            jax.ShapeDtypeStruct((2 * LANES, LANES), i32),
-            jax.ShapeDtypeStruct((ROWS, 2 * LANES), i32),
-            jax.ShapeDtypeStruct((devices, LANES), i32),
-        ],
-        in_specs=[smem, anywhere],
-        out_specs=[vmem, vmem, vmem],
-        scratch_shapes=[
-            table_scratch,
-            pltpu.VMEM((devices, LANES), i32),
-            pltpu.VMEM((devices, LANES), i32),
-            table_sem,
-        ],
-        compiler_params=params,
-        cost_estimate=pl.CostEstimate(flops=10**9, bytes_accessed=2 * 10**7, transcendentals=0),
-        name="places",
-    )(place_here, tables)
-    angles, angles_across, samples, twins, place, start, moves = lax.optimization_barrier(
-        (angles, angles_across, samples, twins, place, start, moves)
+        cost_estimate=pl.CostEstimate(flops=10**9, bytes_accessed=5 * 10**7, transcendentals=0),
+        name="lists",
+    )(*place_here[:2], tables)
+    angles, angles_across, samples, lists = lax.optimization_barrier(
+        (angles, angles_across, samples, lists)
     )
-    floats, whole, size, pair, group = twins
+    floats, whole, place, start, moves, size, pair, group = lists
     angle_blocks = other_rep(angles, angles_across)
     samples = jnp.stack(samples)
     sample_blocks = samples, lax.ppermute(samples, "rep", swap)
@@ -1034,7 +1052,7 @@
     columns = pl.pallas_call(
         functools.partial(map_kernel, shape),
         out_shape=jax.ShapeDtypeStruct((slots // LANES + 1, 2 * height, 2 * LANES), jnp.bfloat16),
-        in_specs=[smem] * 7 + [anywhere] * 5,
+        in_specs=[smem] * 9 + [anywhere] * 5,
         out_specs=vmem,
         scratch_shapes=[
             stream, stream, stream, stream,
@@ -1050,16 +1068,16 @@
         compiler_params=params,
         name="map_maker",
     )(
-        place_here, size, pair, group, moves, floats, whole, *angle_blocks,
+        *place_here, size, pair, group, moves, floats, whole, *angle_blocks,
         *sample_blocks,
     )
-    out_block = pl.BlockSpec((height, OUT_TILES * LANES), lambda n: (0, n))
+    buffers = pltpu.VMEM((WRITES, height, OUT_TILES * LANES), f32)
     x_turned, r_turned = pl.pallas_call(
         write_kernel,
-        grid=(owner_rows // (OUT_TILES * LANES),),
         out_shape=[jax.ShapeDtypeStruct((height, owner_rows), f32)] * 2,
         in_specs=[smem, vmem, vmem],
-        out_specs=[out_block, out_block],
+        out_specs=[anywhere] * 2,
+        scratch_shapes=[buffers, buffers] + [pltpu.SemaphoreType.DMA((WRITES,))] * 2,
         compiler_params=params,
         name="write",
     )(start, columns, place)

time: 103 us -> 90.2 us (0.88); the launches traced: 104 us -> 89.6 us
  Pallas kernels: 71.6 us -> 58.9 us
  blocking collectives: 6.37 us -> 2.14 us
  starting transfers between devices: 12.7 us -> 15 us
  waiting for transfers between devices: 8.15 us -> 9.43 us
    pallas_call x3 -> x2, Pallas kernels: 33.4 us -> 22 us  [the longest x1 13.8 us: whole_part(): pl.pallas_call(write_kernel, out_shape=[jax.ShapeDtypeStruct((height, own...]
    all_gather x1, blocking collectives: 6.37 us -> 2.14 us  [whole_part(): tables = lax.all_gather(tables, 'rep', axis=0, tiled=False)]
    ppermute x2 -> x3, waiting for transfers between devices: 2.97 us -> 5.68 us  [other_wafer(): return lax.ppermute(here, 'wafer', swap)]
    ppermute x2 -> x3, starting transfers between devices: 2.98 us -> 4.54 us  [other_wafer(): return lax.ppermute(here, 'wafer', swap)]
    ppermute x6, waiting for transfers between devices: 3.15 us -> 1.72 us  [along_det(): lax.ppermute(block, 'det', [(i, (i + shift) % dets) for i in range(dets)])]
    pallas_call x1, Pallas kernels: 36.6 us -> 35.2 us  [whole_part(): pl.pallas_call(functools.partial(map_kernel, shape), out_shape=jax.ShapeD...]
  transfers between devices with their start and end apart: 10 -> 11, of which waited for: 4 -> 5; matrix products, arithmetic and copies ran while one was open for 1% -> 1% of each run, Pallas kernels for 12% -> 9%
where the time goes in v4:
time: 90.2 us; the launch traced here: 89.6 us
  Pallas kernels  58.9 us (65%)
  starting transfers between devices  15 us (17%)
  waiting for transfers between devices  9.43 us (10%)
  other arithmetic  2.46 us (3%)
  blocking collectives  2.14 us (2%)
    pallas_call x1, Pallas kernels, whole_part(): pl.pallas_call(functools.partial(map_kernel, shape), out_shape=jax.ShapeD...  35.2 us
    pallas_call x1, Pallas kernels, whole_part(): pl.pallas_call(write_kernel, out_shape=[jax.ShapeDtypeStruct((height, own...  13.8 us
    ppermute x6, starting transfers between devices, along_det(): lax.ppermute(block, 'det', [(i, (i + shift) % dets) for i in range(dets)])  9.84 us
    pallas_call x1, Pallas kernels, whole_part(): pl.pallas_call(functools.partial(list_kernel, shape), out_shape=[jax.Shap...  8.18 us
    ppermute x3, waiting for transfers between devices, other_wafer(): return lax.ppermute(here, 'wafer', swap)  5.68 us
    ppermute x3, starting transfers between devices, other_wafer(): return lax.ppermute(here, 'wafer', swap)  4.54 us
    all_gather x1, blocking collectives, whole_part(): tables = lax.all_gather(tables, 'rep', axis=0, tiled=False)  2.14 us
  transfers between devices with their start and end apart: 11, of which 5 were waited for; matrix products, arithmetic and copies ran while one was open for 1% of the time, Pallas kernels for 9%

profile of v4, /device:TPU:0, one launch (start us, length us, event | category | flops | bytes accessed | tf_op | source)
XLA Modules:
  0.0 89.6 jit_solution(4930970359708309136)
XLA Ops:
  0.6 1.7 %pack.1 = (f32[2,8,128]{2,1,0:T(8,128)}, f32[8,16,128]{2,1,0:T(8,128)}, f32[8,16,128]{2,1,0:T(8,128)}) custom-call(f32[8,2048]{1,0:T(8,128)} %bitcast.56, f32[8,2048]{1,0:T(8,128)} %bitcast.57, s32[8,16]{1,0:T(8,128)} %bitcast.63, s32[8,32]{1,0:T(8,128)} %bitcast.64, s32[1,8]{1,0:T(1,128)} %group_ref.1, f32[1,8]{1,0:T(1,128)} %base_ref.1, f32[4,8]{1,0:T(4,128)} %bitcast.65, ...), custom_call_target="tpu_custom_call" | custom-call | tf_op jit(solution)/shard_map/pack/pallas_call | solution.py:982
  2.3 2.1 %all-gather = f32[4,8,128]{2,1,0:T(8,128)S(1)} all-gather(f32[2,8,128]{2,1,0:T(8,128)} %get-tuple-element.36), channel_id=2, replica_groups=mesh['groups'=2,'det'=4,'wafer'=2,'rep'=2] {'rep'}, dimensions={0}, use_global_device_ids=true | all-gather | bytes 24576 | tf_op jit(solution)/shard_map/all_gather | solution.py:1001
  4.5 0.8 pad_maximum_fusion.5
  5.3 4.9 %collective-permute-start.3 = (f32[20,8,128]{2,1,0:T(8,128)S(1)}, f32[20,8,128]{2,1,0:T(8,128)S(1)}, u32[]{:S(2)}, u32[]{:S(2)}) collective-permute-start(f32[20,8,128]{2,1,0:T(8,128)S(1)} %pad_maximum_fusion.5), channel_id=1, source_target_pairs={{0,12},{4,0},{8,4},{12,8},{1,13},{5,1},{9,5},{13,9},{2,14},{6,2},{... | collective-permute-start | bytes 245768 | tf_op jit(solution)/shard_map/ppermute | solution.py:971
  10.2 1.0 %collective-permute-start.1 = (f32[20,8,128]{2,1,0:T(8,128)S(1)}, f32[20,8,128]{2,1,0:T(8,128)S(1)}, u32[]{:S(2)}, u32[]{:S(2)}) collective-permute-start(f32[20,8,128]{2,1,0:T(8,128)S(1)} %pad_maximum_fusion.5), channel_id=1, source_target_pairs={{0,4},{4,8},{8,12},{12,0},{1,5},{5,9},{9,13},{13,1},{2,6},{6,10},{... | collective-permute-start | bytes 245768 | tf_op jit(solution)/shard_map/ppermute | solution.py:971
  11.2 1.5 %collective-permute-start = (f32[16,8,128]{2,1,0:T(8,128)}, f32[16,8,128]{2,1,0:T(8,128)S(1)}, u32[]{:S(2)}, u32[]{:S(2)}) collective-permute-start(f32[16,8,128]{2,1,0:T(8,128)} %bitcast.59), channel_id=1, source_target_pairs={{0,2},{2,0},{1,3},{3,1},{4,6},{6,4},{5,7},{7,5},{8,10},{10,8},{9,1... | collective-permute-start | bytes 196616 | tf_op jit(solution)/shard_map/ppermute | solution.py:977
  12.8 3.0 %collective-permute-done = f32[16,8,128]{2,1,0:T(8,128)S(1)} collective-permute-done((f32[16,8,128]{2,1,0:T(8,128)}, f32[16,8,128]{2,1,0:T(8,128)S(1)}, u32[]{:S(2)}, u32[]{:S(2)}) %collective-permute-start) | collective-permute-done | bytes 65568 | tf_op jit(solution)/shard_map/ppermute | solution.py:977
  15.7 0.8 pad_maximum_fusion.3
  16.6 1.7 %collective-permute-done.2 = f32[20,8,128]{2,1,0:T(8,128)S(1)} collective-permute-done((f32[20,8,128]{2,1,0:T(8,128)S(1)}, f32[20,8,128]{2,1,0:T(8,128)S(1)}, u32[]{:S(2)}, u32[]{:S(2)}) %collective-permute-start.2) | collective-permute-done | bytes 81952 | tf_op jit(solution)/shard_map/ppermute | solution.py:971
  18.3 1.6 %collective-permute-start.4 = (f32[4,4,8,128]{3,2,1,0:T(8,128)S(1)}, f32[4,4,8,128]{3,2,1,0:T(8,128)S(1)}, u32[]{:S(2)}, u32[]{:S(2)}) collective-permute-start(f32[4,4,8,128]{3,2,1,0:T(8,128)S(1)} %pad_maximum_fusion.6), channel_id=1, source_target_pairs={{0,2},{2,0},{1,3},{3,1},{4,6},{6,4},{5,7},{7,5},{8,10},{10,8},{9,1... | collective-permute-start | bytes 196616 | tf_op jit(solution)/shard_map/ppermute | solution.py:977
  20.0 2.7 %collective-permute-done.4 = f32[4,4,8,128]{3,2,1,0:T(8,128)S(1)} collective-permute-done((f32[4,4,8,128]{3,2,1,0:T(8,128)S(1)}, f32[4,4,8,128]{3,2,1,0:T(8,128)S(1)}, u32[]{:S(2)}, u32[]{:S(2)}) %collective-permute-start.4) | collective-permute-done | bytes 65568 | tf_op jit(solution)/shard_map/ppermute | solution.py:977
  22.7 0.7 pad_maximum_fusion.4.table_ref
  23.3 1.5 %collective-permute-start.5 = (f32[4,16,8,128]{3,2,1,0:T(8,128)S(1)}, f32[4,16,8,128]{3,2,1,0:T(8,128)S(1)}, u32[]{:S(2)}, u32[]{:S(2)}) collective-permute-start(f32[4,16,8,128]{3,2,1,0:T(8,128)S(1)} %pad_maximum_fusion.2.angle_here_ref), channel_id=1, source_target_pairs={{0,2},{2,0},{1,3},{3,1},{4,6},{6,4},{5,7},{7,5},{8,10},{10,8},{9,1... | collective-permute-start | bytes 786440 | tf_op jit(solution)/shard_map/ppermute | solution.py:977
  24.8 1.9 %collective-permute-start.8 = (f32[2,16,8,128]{3,2,1,0:T(8,128)S(1)}, f32[2,16,8,128]{3,2,1,0:T(8,128)S(1)}, u32[]{:S(2)}, u32[]{:S(2)}) collective-permute-start(f32[2,16,8,128]{3,2,1,0:T(8,128)S(1)} %pad_maximum_fusion.3), channel_id=1, source_target_pairs={{0,12},{4,0},{8,4},{12,8},{1,13},{5,1},{9,5},{13,9},{2,14},{6,2},{... | collective-permute-start | bytes 393224 | tf_op jit(solution)/shard_map/ppermute | solution.py:971
  26.7 0.4 collective-permute-start.7
  27.1 1.6 %collective-permute-start.6 = (f32[2,16,8,128]{3,2,1,0:T(8,128)S(1)}, f32[2,16,8,128]{3,2,1,0:T(8,128)S(1)}, u32[]{:S(2)}, u32[]{:S(2)}) collective-permute-start(f32[2,16,8,128]{3,2,1,0:T(8,128)S(1)} %pad_maximum_fusion.3), channel_id=1, source_target_pairs={{0,4},{4,8},{8,12},{12,0},{1,5},{5,9},{9,13},{13,1},{2,6},{6,10},{... | collective-permute-start | bytes 393224 | tf_op jit(solution)/shard_map/ppermute | solution.py:971
  28.7 8.2 %lists.1 = (f32[16,128]{1,0:T(8,128)}, s32[16,128]{1,0:T(8,128)}, s32[256,128]{1,0:T(8,128)}, s32[8,256]{1,0:T(8,128)}, s32[16,128]{1,0:T(8,128)}, /*index=5*/s32[2]{0:T(128)}, s32[2048]{0:T(1024)}, s32[2048]{0:T(1024)}) custom-call(s32[1]{0:T(128)} %bitcast.25.wafer_ref, s32[1]{0:T(128)} %bitcast.26.det_ref, ...), custom_call_target="tpu_custom_call" | custom-call | flops 1000000000 | bytes 50000000 | tf_op jit(solution)/shard_map/lists/pallas_call | solution.py:1014
  37.0 0.1 collective-permute-start.9
  37.2 0.6 collective-permute-start.10
  37.7 1.3 %collective-permute-done.9.angle_other_ref = f32[2,4,16,8,128]{4,3,2,1,0:T(8,128)S(1)} collective-permute-done((f32[2,4,16,8,128]{4,3,2,1,0:T(8,128)S(1)}, f32[2,4,16,8,128]{4,3,2,1,0:T(8,128)S(1)}, u32[]{:S(2)}, u32[]{:S(2)}) %collective-permute-start.9) | collective-permute-done | bytes 524320 | tf_op jit(solution)/shard_map/ppermute | solution.py:980
  39.0 0.7 collective-permute-done.10.tod_other_ref
  39.8 0.8 copy-done.4
  40.6 35.2 %map_maker.1.column_ref = bf16[5,384,256]{2,1,0:T(8,128)(2,1)} custom-call(s32[1]{0:T(128)} %bitcast.25.wafer_ref, s32[1]{0:T(128)} %bitcast.26.det_ref, s32[1]{0:T(128)} %bitcast.27.rep_ref, s32[2]{0:T(128)} %get-tuple-element.51.size_ref, s32[2048]{0:T(1024)} %get-tuple-element.52.pair_ref, s32[2048]{0:T(1024)} %get-tuple-element.53.group_ref, ...), custom_call_target="tpu_custom_call" | custom-call | tf_op jit(solution)/shard_map/map_maker/pallas_call | solution.py:1052
  75.7 13.8 %write.1 = (f32[192,24576]{1,0:T(8,128)}, f32[192,24576]{1,0:T(8,128)}) custom-call(s32[8,256]{1,0:T(8,128)} %get-tuple-element.50.start_ref, bf16[5,384,256]{2,1,0:T(8,128)(2,1)} %map_maker.1.column_ref, s32[256,128]{1,0:T(8,128)} %get-tuple-element.63.place_ref), custom_call_target="tpu_custom_call" | custom-call | tf_op jit(solution)/shard_map/write/pallas_call | solution.py:1075
  (28 shorter events, 0.2 us)
Async XLA Ops:
  5.3 11.3 %collective-permute-start.3 = (f32[20,8,128]{2,1,0:T(8,128)S(1)}, f32[20,8,128]{2,1,0:T(8,128)S(1)}, u32[]{:S(2)}, u32[]{:S(2)}) collective-permute-start(f32[20,8,128]{2,1,0:T(8,128)S(1)} %pad_maximum_fusion.5), channel_id=1, source_target_pairs={{0,12},{4,0},{8,4},{12,8},{1,13},{5,1},{9,5},{13,9},{2,14},{6,2},{... | collective-permute-start | bytes 245768 | tf_op jit(solution)/shard_map/ppermute | solution.py:971
  10.2 8.1 %collective-permute-start.2 = (f32[20,8,128]{2,1,0:T(8,128)S(1)}, f32[20,8,128]{2,1,0:T(8,128)S(1)}, u32[]{:S(2)}, u32[]{:S(2)}) collective-permute-start(f32[20,8,128]{2,1,0:T(8,128)S(1)} %pad_maximum_fusion.5), channel_id=1, source_target_pairs={{0,8},{4,12},{8,0},{12,4},{1,9},{5,13},{9,1},{13,5},{2,10},{6,14},... | collective-permute-start | bytes 245768 | tf_op jit(solution)/shard_map/ppermute | solution.py:971
  10.2 8.1 %collective-permute-start.1 = (f32[20,8,128]{2,1,0:T(8,128)S(1)}, f32[20,8,128]{2,1,0:T(8,128)S(1)}, u32[]{:S(2)}, u32[]{:S(2)}) collective-permute-start(f32[20,8,128]{2,1,0:T(8,128)S(1)} %pad_maximum_fusion.5), channel_id=1, source_target_pairs={{0,4},{4,8},{8,12},{12,0},{1,5},{5,9},{9,13},{13,1},{2,6},{6,10},{... | collective-permute-start | bytes 245768 | tf_op jit(solution)/shard_map/ppermute | solution.py:971
  11.2 4.5 %collective-permute-start = (f32[16,8,128]{2,1,0:T(8,128)}, f32[16,8,128]{2,1,0:T(8,128)S(1)}, u32[]{:S(2)}, u32[]{:S(2)}) collective-permute-start(f32[16,8,128]{2,1,0:T(8,128)} %bitcast.59), channel_id=1, source_target_pairs={{0,2},{2,0},{1,3},{3,1},{4,6},{6,4},{5,7},{7,5},{8,10},{10,8},{9,1... | collective-permute-start | bytes 196616 | tf_op jit(solution)/shard_map/ppermute | solution.py:977
  18.3 4.3 %collective-permute-start.4 = (f32[4,4,8,128]{3,2,1,0:T(8,128)S(1)}, f32[4,4,8,128]{3,2,1,0:T(8,128)S(1)}, u32[]{:S(2)}, u32[]{:S(2)}) collective-permute-start(f32[4,4,8,128]{3,2,1,0:T(8,128)S(1)} %pad_maximum_fusion.6), channel_id=1, source_target_pairs={{0,2},{2,0},{1,3},{3,1},{4,6},{6,4},{5,7},{7,5},{8,10},{10,8},{9,1... | collective-permute-start | bytes 196616 | tf_op jit(solution)/shard_map/ppermute | solution.py:977
  20.0 19.8 %copy-start = (f32[4,16,8,128]{3,2,1,0:T(8,128)}, f32[4,16,8,128]{3,2,1,0:T(8,128)S(1)}, u32[]{:S(2)}) copy-start(f32[4,16,8,128]{3,2,1,0:T(8,128)S(1)} %pad_maximum_fusion.2.angle_here_ref) | copy-start | bytes 786436
  23.3 13.6 %collective-permute-start.5 = (f32[4,16,8,128]{3,2,1,0:T(8,128)S(1)}, f32[4,16,8,128]{3,2,1,0:T(8,128)S(1)}, u32[]{:S(2)}, u32[]{:S(2)}) collective-permute-start(f32[4,16,8,128]{3,2,1,0:T(8,128)S(1)} %pad_maximum_fusion.2.angle_here_ref), channel_id=1, source_target_pairs={{0,2},{2,0},{1,3},{3,1},{4,6},{6,4},{5,7},{7,5},{8,10},{10,8},{9,1... | collective-permute-start | bytes 786440 | tf_op jit(solution)/shard_map/ppermute | solution.py:977
  24.8 12.1 %collective-permute-start.8 = (f32[2,16,8,128]{3,2,1,0:T(8,128)S(1)}, f32[2,16,8,128]{3,2,1,0:T(8,128)S(1)}, u32[]{:S(2)}, u32[]{:S(2)}) collective-permute-start(f32[2,16,8,128]{3,2,1,0:T(8,128)S(1)} %pad_maximum_fusion.3), channel_id=1, source_target_pairs={{0,12},{4,0},{8,4},{12,8},{1,13},{5,1},{9,5},{13,9},{2,14},{6,2},{... | collective-permute-start | bytes 393224 | tf_op jit(solution)/shard_map/ppermute | solution.py:971
  26.7 10.2 %collective-permute-start.7 = (f32[2,16,8,128]{3,2,1,0:T(8,128)S(1)}, f32[2,16,8,128]{3,2,1,0:T(8,128)S(1)}, u32[]{:S(2)}, u32[]{:S(2)}) collective-permute-start(f32[2,16,8,128]{3,2,1,0:T(8,128)S(1)} %pad_maximum_fusion.3), channel_id=1, source_target_pairs={{0,8},{4,12},{8,0},{12,4},{1,9},{5,13},{9,1},{13,5},{2,10},{6,14},... | collective-permute-start | bytes 393224 | tf_op jit(solution)/shard_map/ppermute | solution.py:971
  27.1 9.9 %collective-permute-start.6 = (f32[2,16,8,128]{3,2,1,0:T(8,128)S(1)}, f32[2,16,8,128]{3,2,1,0:T(8,128)S(1)}, u32[]{:S(2)}, u32[]{:S(2)}) collective-permute-start(f32[2,16,8,128]{3,2,1,0:T(8,128)S(1)} %pad_maximum_fusion.3), channel_id=1, source_target_pairs={{0,4},{4,8},{8,12},{12,0},{1,5},{5,9},{9,13},{13,1},{2,6},{6,10},{... | collective-permute-start | bytes 393224 | tf_op jit(solution)/shard_map/ppermute | solution.py:971
  37.0 2.8 %copy-start.2 = (f32[4,16,8,128]{3,2,1,0:T(8,128)}, f32[4,16,8,128]{3,2,1,0:T(8,128)S(1)}, u32[]{:S(2)}) copy-start(f32[4,16,8,128]{3,2,1,0:T(8,128)S(1)} %collective-permute-done.5.angle_across_ref) | copy-start | bytes 786436
  37.0 2.0 %collective-permute-start.9 = (f32[2,4,16,8,128]{4,3,2,1,0:T(8,128)S(1)}, f32[2,4,16,8,128]{4,3,2,1,0:T(8,128)S(1)}, u32[]{:S(2)}, u32[]{:S(2)}) collective-permute-start(f32[2,4,16,8,128]{4,3,2,1,0:T(8,128)S(1)} %pad_maximum_fusion), channel_id=1, source_target_pairs={{0,1},{1,0},{2,3},{3,2},{4,5},{5,4},{6,7},{7,6},{8,9},{9,8},{10,11... | collective-permute-start | bytes 1572872 | tf_op jit(solution)/shard_map/ppermute | solution.py:980
  37.1 2.6 %copy-start.1 = (f32[4,2,16,8,128]{4,3,2,1,0:T(8,128)}, f32[4,2,16,8,128]{4,3,2,1,0:T(8,128)S(1)}, u32[]{:S(2)}) copy-start(f32[4,2,16,8,128]{4,3,2,1,0:T(8,128)S(1)} %pad_maximum_fusion.1.tod_here_ref) | copy-start | bytes 1572868
  37.2 2.6 %collective-permute-start.10 = (f32[4,2,16,8,128]{4,3,2,1,0:T(8,128)S(1)}, f32[4,2,16,8,128]{4,3,2,1,0:T(8,128)S(1)}, u32[]{:S(2)}, u32[]{:S(2)}) collective-permute-start(f32[4,2,16,8,128]{4,3,2,1,0:T(8,128)S(1)} %pad_maximum_fusion.1.tod_here_ref), channel_id=1, source_target_pairs={{0,1},{1,0},{2,3},{3,2},{4,5},{5,4},{6,7},{7,6},{8,9},{9,8},{10,11... | collective-permute-start | bytes 1572872 | tf_op jit(solution)/shard_map/ppermute | solution.py:1048
  39.0 0.8 copy-start.3
  39.7 0.8 copy-start.4

commit v5 on v4

--- a/solution.py
+++ b/solution.py
@@ -160,11 +160,10 @@
 OUT_TILES = 8
 PAIR_BATCH = 8
 WRITES = 6
-DET_BATCH = 8
+DET_BATCH = 16
 SUM_SETS = 2
 MAP_BATCH = 8
 BIG = float(1 << 24)
-VMEM_BYTES = 60 << 20
 
 
 def wide(values):
@@ -754,28 +753,24 @@
     filter_streams()
     return_streams(r_map)
 
-    def begin(at, carry):
-        parts = zero
-        for c in range(3):
-            inverse = 1.0 / (image_map[c][at] + prior_weight)
-            inverse_ref[c][at] = inverse
-            residual = r_map[c][at]
-            parts = parts + residual * (inverse * residual)
-        return carry + weight_ref[at] * parts
-
-    energy = whole_sum(loop(count, begin, zero, 16))
     factor = zero
     steps = []
     for iteration, d_map in enumerate(d_maps):
         last = iteration == ITERS - 1
 
         def seen_streams(at, carry):
-            squares = zero
+            prior, energy = carry
+            squares, products = zero, zero
             streams = [None, None]
             for c in range(3):
-                part = inverse_ref[c][at] * r_map[c][at]
+                residual = r_map[c][at]
                 if iteration:
-                    part = part + factor * d_maps[iteration - 1][c][at]
+                    part = inverse_ref[c][at] * residual + factor * d_maps[iteration - 1][c][at]
+                else:
+                    inverse = 1.0 / (image_map[c][at] + prior_weight)
+                    inverse_ref[c][at] = inverse
+                    part = inverse * residual
+                    products = products + residual * part
                 d_map[c][at] = part
                 squares = squares + part * part
                 for half, seen in enumerate(unfold(part)):
@@ -784,9 +779,14 @@
                     else:
                         ref = cos_ref if c == 1 else sin_ref
                         streams[half] = streams[half] + ref[2 * at + half] * seen
-            return streams, carry + weight_ref[at] * squares
-
-        prior = sum_streams(seen_streams, zero)
+            weight = weight_ref[at]
+            if not iteration:
+                energy = energy + weight * products
+            return streams, (prior + weight * squares, energy)
+
+        prior, first_energy = sum_streams(seen_streams, (zero, zero))
+        if not iteration:
+            energy = whole_sum(first_energy)
         product = filter_streams()
         return_streams(image_map)
         step = energy / whole_sum(product + prior_weight * prior)
@@ -963,7 +963,10 @@
     f32, i32 = jnp.float32, jnp.int32
     vmem, smem = pl.BlockSpec(memory_space=pltpu.VMEM), pl.BlockSpec(memory_space=pltpu.SMEM)
     anywhere = pl.BlockSpec(memory_space=pl.ANY)
-    params = pltpu.CompilerParams(vmem_limit_bytes=VMEM_BYTES)
+
+    def params(mebibytes):
+        return pltpu.CompilerParams(vmem_limit_bytes=mebibytes << 20)
+
     swap = [(0, 1), (1, 0)]
 
     def along_det(block):
@@ -988,7 +991,7 @@
         ],
         in_specs=[vmem] * 8,
         out_specs=[vmem] * 3,
-        compiler_params=params,
+        compiler_params=params(60),
         name="pack",
     )(
         psi[0], tod[0], point_row[0], hit_list[0, 0, 0], group_id, a_zero, band_coef[0].T,
@@ -1002,14 +1005,14 @@
     riders = jnp.concatenate([angles, tables.reshape(2 * reps, ROWS, LANES)])
     samples, riders = lax.optimization_barrier((samples, riders))
     samples = jnp.stack([samples, other_wafer(samples)])
-    blocks = along_det(riders)
+    samples, *blocks = lax.optimization_barrier((samples, *along_det(riders)))
+    samples = along_det(samples)
     tables = jnp.stack([block[tiles:] for block in blocks])
     angles = jnp.stack([block[:tiles] for block in blocks])
     tables = jnp.stack([tables, other_wafer(tables)])
     tables = tables.reshape(wafers, dets, reps, 2, ROWS, LANES)
-    samples, angles, tables = lax.optimization_barrier((samples, angles, tables))
+    angles, tables = lax.optimization_barrier((angles, tables))
     angles_across = other_wafer(angles)
-    samples = along_det(samples)
     table_rows = jax.ShapeDtypeStruct((devices, LANES), i32)
     lists = pl.pallas_call(
         functools.partial(list_kernel, shape),
@@ -1035,7 +1038,7 @@
             pltpu.VMEM((devices, LANES), i32),
             pltpu.SemaphoreType.DMA((devices,)),
         ],
-        compiler_params=params,
+        compiler_params=params(8),
         cost_estimate=pl.CostEstimate(flops=10**9, bytes_accessed=5 * 10**7, transcendentals=0),
         name="lists",
     )(*place_here[:2], tables)
@@ -1065,7 +1068,7 @@
             pltpu.SemaphoreType.DMA((devices,)),
             pltpu.SemaphoreType.DMA((devices,)),
         ] + [sky] * (3 * (3 + ITERS)) + [group_sums] * (2 * wafers * SUM_SETS),
-        compiler_params=params,
+        compiler_params=params(30),
         name="map_maker",
     )(
         *place_here, size, pair, group, moves, floats, whole, *angle_blocks,
@@ -1078,7 +1081,7 @@
         in_specs=[smem, vmem, vmem],
         out_specs=[anywhere] * 2,
         scratch_shapes=[buffers, buffers] + [pltpu.SemaphoreType.DMA((WRITES,))] * 2,
-        compiler_params=params,
+        compiler_params=params(16),
         name="write",
     )(start, columns, place)
     return x_turned.T, r_turned.T

time: 90.2 us -> 88.5 us (0.981); the launches traced: 89.6 us -> 88.9 us
  waiting for transfers between devices: 9.43 us -> 12.2 us
  starting transfers between devices: 15 us -> 13.3 us
    ppermute x6, waiting for transfers between devices: 1.72 us -> 6.41 us  [along_det(): lax.ppermute(block, 'det', [(i, (i + shift) % dets) for i in range(dets)])]
    ppermute x3, waiting for transfers between devices: 5.68 us -> 3.71 us  [other_wafer(): return lax.ppermute(here, 'wafer', swap)]
    pallas_call x1, Pallas kernels: 35.2 us -> 36.4 us  [whole_part(): pl.pallas_call(functools.partial(map_kernel, shape), out_shape=jax.ShapeD...]
    ppermute x6, starting transfers between devices: 9.84 us -> 8.69 us  [along_det(): lax.ppermute(block, 'det', [(i, (i + shift) % dets) for i in range(dets)])]
    pallas_call x1, Pallas kernels: 8.18 us -> 7.26 us  [whole_part(): pl.pallas_call(functools.partial(list_kernel, shape), out_shape=[jax.Shap...]
  transfers between devices with their start and end apart: 11 -> 11, of which waited for: 5 -> 6; matrix products, arithmetic and copies ran while one was open for 1% -> 1% of each run, Pallas kernels for 9% -> 8%
where the time goes in v5:
time: 88.5 us; the launch traced here: 88.9 us
  Pallas kernels  58.7 us (66%)
  starting transfers between devices  13.3 us (15%)
  waiting for transfers between devices  12.2 us (14%)
  blocking collectives  2.14 us (2%)
  other arithmetic  1.8 us (2%)
    pallas_call x1, Pallas kernels, whole_part(): pl.pallas_call(functools.partial(map_kernel, shape), out_shape=jax.ShapeD...  36.4 us
    pallas_call x1, Pallas kernels, whole_part(): pl.pallas_call(write_kernel, out_shape=[jax.ShapeDtypeStruct((height, own...  13.3 us
    ppermute x6, starting transfers between devices, along_det(): lax.ppermute(block, 'det', [(i, (i + shift) % dets) for i in range(dets)])  8.69 us
    pallas_call x1, Pallas kernels, whole_part(): pl.pallas_call(functools.partial(list_kernel, shape), out_shape=[jax.Shap...  7.26 us
    ppermute x6, waiting for transfers between devices, along_det(): lax.ppermute(block, 'det', [(i, (i + shift) % dets) for i in range(dets)])  6.41 us
    ppermute x3, starting transfers between devices, other_wafer(): return lax.ppermute(here, 'wafer', swap)  4.01 us
    ppermute x3, waiting for transfers between devices, other_wafer(): return lax.ppermute(here, 'wafer', swap)  3.71 us
    all_gather x1, blocking collectives, whole_part(): tables = lax.all_gather(tables, 'rep', axis=0, tiled=False)  2.14 us
  transfers between devices with their start and end apart: 11, of which 6 were waited for; matrix products, arithmetic and copies ran while one was open for 1% of the time, Pallas kernels for 8%

profile of v5, /device:TPU:0, one launch (start us, length us, event | category | flops | bytes accessed | tf_op | source)
XLA Modules:
  0.0 88.9 jit_solution(1580940139306616266)
XLA Ops:
  0.6 1.7 %pack.1 = (f32[2,8,128]{2,1,0:T(8,128)}, f32[8,16,128]{2,1,0:T(8,128)}, f32[8,16,128]{2,1,0:T(8,128)}) custom-call(f32[8,2048]{1,0:T(8,128)} %bitcast.52, f32[8,2048]{1,0:T(8,128)} %bitcast.53, s32[8,16]{1,0:T(8,128)} %bitcast.63, s32[8,32]{1,0:T(8,128)} %bitcast.64, s32[1,8]{1,0:T(1,128)} %group_ref.1, f32[1,8]{1,0:T(1,128)} %base_ref.1, f32[4,8]{1,0:T(4,128)} %bitcast.65, ...), custom_call_target="tpu_custom_call" | custom-call | tf_op jit(solution)/shard_map/pack/pallas_call | solution.py:985
  2.3 2.1 %all-gather = f32[4,8,128]{2,1,0:T(8,128)S(1)} all-gather(f32[2,8,128]{2,1,0:T(8,128)} %get-tuple-element.40), channel_id=2, replica_groups=mesh['groups'=2,'det'=4,'wafer'=2,'rep'=2] {'rep'}, dimensions={0}, use_global_device_ids=true | all-gather | bytes 24576 | tf_op jit(solution)/shard_map/all_gather | solution.py:1004
  4.5 0.8 pad_maximum_fusion.5
  5.3 2.8 %collective-permute-start = (f32[16,8,128]{2,1,0:T(8,128)}, f32[16,8,128]{2,1,0:T(8,128)S(1)}, u32[]{:S(2)}, u32[]{:S(2)}) collective-permute-start(f32[16,8,128]{2,1,0:T(8,128)} %bitcast.59), channel_id=1, source_target_pairs={{0,2},{2,0},{1,3},{3,1},{4,6},{6,4},{5,7},{7,5},{8,10},{10,8},{9,1... | collective-permute-start | bytes 196616 | tf_op jit(solution)/shard_map/ppermute | solution.py:980
  8.1 3.6 %collective-permute-start.3 = (f32[20,8,128]{2,1,0:T(8,128)S(1)}, f32[20,8,128]{2,1,0:T(8,128)S(1)}, u32[]{:S(2)}, u32[]{:S(2)}) collective-permute-start(f32[20,8,128]{2,1,0:T(8,128)S(1)} %pad_maximum_fusion.5), channel_id=1, source_target_pairs={{0,12},{4,0},{8,4},{12,8},{1,13},{5,1},{9,5},{13,9},{2,14},{6,2},{... | collective-permute-start | bytes 245768 | tf_op jit(solution)/shard_map/ppermute | solution.py:974
  11.7 1.0 %collective-permute-start.1 = (f32[20,8,128]{2,1,0:T(8,128)S(1)}, f32[20,8,128]{2,1,0:T(8,128)S(1)}, u32[]{:S(2)}, u32[]{:S(2)}) collective-permute-start(f32[20,8,128]{2,1,0:T(8,128)S(1)} %pad_maximum_fusion.5), channel_id=1, source_target_pairs={{0,4},{4,8},{8,12},{12,0},{1,5},{5,9},{9,13},{13,1},{2,6},{6,10},{... | collective-permute-start | bytes 245768 | tf_op jit(solution)/shard_map/ppermute | solution.py:974
  12.7 0.0 collective-permute-done
  12.7 0.8 pad_maximum_fusion.3
  13.6 1.0 %collective-permute-done.3 = f32[20,8,128]{2,1,0:T(8,128)S(1)} collective-permute-done((f32[20,8,128]{2,1,0:T(8,128)S(1)}, f32[20,8,128]{2,1,0:T(8,128)S(1)}, u32[]{:S(2)}, u32[]{:S(2)}) %collective-permute-start.3) | collective-permute-done | bytes 81952 | tf_op jit(solution)/shard_map/ppermute | solution.py:974
  14.6 4.8 %collective-permute-done.2 = f32[20,8,128]{2,1,0:T(8,128)S(1)} collective-permute-done((f32[20,8,128]{2,1,0:T(8,128)S(1)}, f32[20,8,128]{2,1,0:T(8,128)S(1)}, u32[]{:S(2)}, u32[]{:S(2)}) %collective-permute-start.2) | collective-permute-done | bytes 81952 | tf_op jit(solution)/shard_map/ppermute | solution.py:974
  19.4 0.6 collective-permute-start.4
  20.1 3.7 %collective-permute-done.4 = f32[4,4,8,128]{3,2,1,0:T(8,128)S(1)} collective-permute-done((f32[4,4,8,128]{3,2,1,0:T(8,128)S(1)}, f32[4,4,8,128]{3,2,1,0:T(8,128)S(1)}, u32[]{:S(2)}, u32[]{:S(2)}) %collective-permute-start.4) | collective-permute-done | bytes 65568 | tf_op jit(solution)/shard_map/ppermute | solution.py:980
  23.8 0.6 collective-permute-start.5
  24.4 2.5 %collective-permute-start.8 = (f32[2,16,8,128]{3,2,1,0:T(8,128)S(1)}, f32[2,16,8,128]{3,2,1,0:T(8,128)S(1)}, u32[]{:S(2)}, u32[]{:S(2)}) collective-permute-start(f32[2,16,8,128]{3,2,1,0:T(8,128)S(1)} %pad_maximum_fusion.3), channel_id=1, source_target_pairs={{0,12},{4,0},{8,4},{12,8},{1,13},{5,1},{9,5},{13,9},{2,14},{6,2},{... | collective-permute-start | bytes 393224 | tf_op jit(solution)/shard_map/ppermute | solution.py:974
  26.9 0.0 collective-permute-start.7
  26.9 1.6 %collective-permute-start.6 = (f32[2,16,8,128]{3,2,1,0:T(8,128)S(1)}, f32[2,16,8,128]{3,2,1,0:T(8,128)S(1)}, u32[]{:S(2)}, u32[]{:S(2)}) collective-permute-start(f32[2,16,8,128]{3,2,1,0:T(8,128)S(1)} %pad_maximum_fusion.3), channel_id=1, source_target_pairs={{0,4},{4,8},{8,12},{12,0},{1,5},{5,9},{9,13},{13,1},{2,6},{6,10},{... | collective-permute-start | bytes 393224 | tf_op jit(solution)/shard_map/ppermute | solution.py:974
  28.5 7.3 %lists.1 = (f32[16,128]{1,0:T(8,128)S(1)}, s32[16,128]{1,0:T(8,128)S(1)}, s32[256,128]{1,0:T(8,128)S(1)}, s32[8,256]{1,0:T(8,128)S(1)}, s32[16,128]{1,0:T(8,128)...) custom-call(s32[1]{0:T(128)} %bitcast.25.wafer_ref, s32[1]{0:T(128)} %bitcast.26.det_ref, ...), custom_call_target="tpu_custom_call" | custom-call | flops 1000000000 | bytes 50000000 | tf_op jit(solution)/shard_map/lists/pallas_call | solution.py:1017
  35.7 0.6 collective-permute-done.7
  36.4 0.1 collective-permute-start.9
  36.5 0.6 collective-permute-start.10
  37.1 1.3 %collective-permute-done.9.angle_other_ref = f32[2,4,16,8,128]{4,3,2,1,0:T(8,128)S(1)} collective-permute-done((f32[2,4,16,8,128]{4,3,2,1,0:T(8,128)S(1)}, f32[2,4,16,8,128]{4,3,2,1,0:T(8,128)S(1)}, u32[]{:S(2)}, u32[]{:S(2)}) %collective-permute-start.9) | collective-permute-done | bytes 524320 | tf_op jit(solution)/shard_map/ppermute | solution.py:983
  38.4 0.7 collective-permute-done.10.tod_other_ref
  39.2 36.4 %map_maker.1.column_ref = bf16[5,384,256]{2,1,0:T(8,128)(2,1)S(1)} custom-call(s32[1]{0:T(128)} %bitcast.25.wafer_ref, s32[1]{0:T(128)} %bitcast.26.det_ref, s32[1]{0:T(128)} %bitcast.27.rep_ref, s32[2]{0:T(128)S(1)} %get-tuple-element.59.size_ref, s32[2048]{0:T(1024)S(1)} %get-tuple-element.60.pair_ref, s32[2048]{0:T(1024)S(1)} %get-tuple-element.61.group_ref, ...), custom_call_target="tpu_custom_call" | custom-call | tf_op jit(solution)/shard_map/map_maker/pallas_call | solution.py:1055
  75.6 13.3 %write.1 = (f32[192,24576]{1,0:T(8,128)}, f32[192,24576]{1,0:T(8,128)}) custom-call(s32[8,256]{1,0:T(8,128)S(1)} %get-tuple-element.58.start_ref, bf16[5,384,256]{2,1,0:T(8,128)(2,1)S(1)} %map_maker.1.column_ref, s32[256,128]{1,0:T(8,128)S(1)} %get-tuple-element.71.place_ref), custom_call_target="tpu_custom_call" | custom-call | tf_op jit(solution)/shard_map/write/pallas_call | solution.py:1078
  (14 shorter events, 0.2 us)
Async XLA Ops:
  5.3 7.4 %collective-permute-start = (f32[16,8,128]{2,1,0:T(8,128)}, f32[16,8,128]{2,1,0:T(8,128)S(1)}, u32[]{:S(2)}, u32[]{:S(2)}) collective-permute-start(f32[16,8,128]{2,1,0:T(8,128)} %bitcast.59), channel_id=1, source_target_pairs={{0,2},{2,0},{1,3},{3,1},{4,6},{6,4},{5,7},{7,5},{8,10},{10,8},{9,1... | collective-permute-start | bytes 196616 | tf_op jit(solution)/shard_map/ppermute | solution.py:980
  8.1 6.4 %collective-permute-start.3 = (f32[20,8,128]{2,1,0:T(8,128)S(1)}, f32[20,8,128]{2,1,0:T(8,128)S(1)}, u32[]{:S(2)}, u32[]{:S(2)}) collective-permute-start(f32[20,8,128]{2,1,0:T(8,128)S(1)} %pad_maximum_fusion.5), channel_id=1, source_target_pairs={{0,12},{4,0},{8,4},{12,8},{1,13},{5,1},{9,5},{13,9},{2,14},{6,2},{... | collective-permute-start | bytes 245768 | tf_op jit(solution)/shard_map/ppermute | solution.py:974
  11.7 7.6 %collective-permute-start.2 = (f32[20,8,128]{2,1,0:T(8,128)S(1)}, f32[20,8,128]{2,1,0:T(8,128)S(1)}, u32[]{:S(2)}, u32[]{:S(2)}) collective-permute-start(f32[20,8,128]{2,1,0:T(8,128)S(1)} %pad_maximum_fusion.5), channel_id=1, source_target_pairs={{0,8},{4,12},{8,0},{12,4},{1,9},{5,13},{9,1},{13,5},{2,10},{6,14},... | collective-permute-start | bytes 245768 | tf_op jit(solution)/shard_map/ppermute | solution.py:974
  11.7 7.6 %collective-permute-start.1 = (f32[20,8,128]{2,1,0:T(8,128)S(1)}, f32[20,8,128]{2,1,0:T(8,128)S(1)}, u32[]{:S(2)}, u32[]{:S(2)}) collective-permute-start(f32[20,8,128]{2,1,0:T(8,128)S(1)} %pad_maximum_fusion.5), channel_id=1, source_target_pairs={{0,4},{4,8},{8,12},{12,0},{1,5},{5,9},{9,13},{13,1},{2,6},{6,10},{... | collective-permute-start | bytes 245768 | tf_op jit(solution)/shard_map/ppermute | solution.py:974
  19.4 4.3 %collective-permute-start.4 = (f32[4,4,8,128]{3,2,1,0:T(8,128)S(1)}, f32[4,4,8,128]{3,2,1,0:T(8,128)S(1)}, u32[]{:S(2)}, u32[]{:S(2)}) collective-permute-start(f32[4,4,8,128]{3,2,1,0:T(8,128)S(1)} %pad_maximum_fusion.6), channel_id=1, source_target_pairs={{0,2},{2,0},{1,3},{3,1},{4,6},{6,4},{5,7},{7,5},{8,10},{10,8},{9,1... | collective-permute-start | bytes 196616 | tf_op jit(solution)/shard_map/ppermute | solution.py:980
  23.8 12.6 %collective-permute-start.5 = (f32[4,16,8,128]{3,2,1,0:T(8,128)S(1)}, f32[4,16,8,128]{3,2,1,0:T(8,128)S(1)}, u32[]{:S(2)}, u32[]{:S(2)}) collective-permute-start(f32[4,16,8,128]{3,2,1,0:T(8,128)S(1)} %pad_maximum_fusion.2.angle_here_ref), channel_id=1, source_target_pairs={{0,2},{2,0},{1,3},{3,1},{4,6},{6,4},{5,7},{7,5},{8,10},{10,8},{9,1... | collective-permute-start | bytes 786440 | tf_op jit(solution)/shard_map/ppermute | solution.py:980
  24.4 11.3 %collective-permute-start.8 = (f32[2,16,8,128]{3,2,1,0:T(8,128)S(1)}, f32[2,16,8,128]{3,2,1,0:T(8,128)S(1)}, u32[]{:S(2)}, u32[]{:S(2)}) collective-permute-start(f32[2,16,8,128]{3,2,1,0:T(8,128)S(1)} %pad_maximum_fusion.3), channel_id=1, source_target_pairs={{0,12},{4,0},{8,4},{12,8},{1,13},{5,1},{9,5},{13,9},{2,14},{6,2},{... | collective-permute-start | bytes 393224 | tf_op jit(solution)/shard_map/ppermute | solution.py:974
  26.9 9.5 %collective-permute-start.7 = (f32[2,16,8,128]{3,2,1,0:T(8,128)S(1)}, f32[2,16,8,128]{3,2,1,0:T(8,128)S(1)}, u32[]{:S(2)}, u32[]{:S(2)}) collective-permute-start(f32[2,16,8,128]{3,2,1,0:T(8,128)S(1)} %pad_maximum_fusion.3), channel_id=1, source_target_pairs={{0,8},{4,12},{8,0},{12,4},{1,9},{5,13},{9,1},{13,5},{2,10},{6,14},... | collective-permute-start | bytes 393224 | tf_op jit(solution)/shard_map/ppermute | solution.py:974
  26.9 9.5 %collective-permute-start.6 = (f32[2,16,8,128]{3,2,1,0:T(8,128)S(1)}, f32[2,16,8,128]{3,2,1,0:T(8,128)S(1)}, u32[]{:S(2)}, u32[]{:S(2)}) collective-permute-start(f32[2,16,8,128]{3,2,1,0:T(8,128)S(1)} %pad_maximum_fusion.3), channel_id=1, source_target_pairs={{0,4},{4,8},{8,12},{12,0},{1,5},{5,9},{9,13},{13,1},{2,6},{6,10},{... | collective-permute-start | bytes 393224 | tf_op jit(solution)/shard_map/ppermute | solution.py:974
  36.4 2.0 %collective-permute-start.9 = (f32[2,4,16,8,128]{4,3,2,1,0:T(8,128)S(1)}, f32[2,4,16,8,128]{4,3,2,1,0:T(8,128)S(1)}, u32[]{:S(2)}, u32[]{:S(2)}) collective-permute-start(f32[2,4,16,8,128]{4,3,2,1,0:T(8,128)S(1)} %pad_maximum_fusion), channel_id=1, source_target_pairs={{0,1},{1,0},{2,3},{3,2},{4,5},{5,4},{6,7},{7,6},{8,9},{9,8},{10,11... | collective-permute-start | bytes 1572872 | tf_op jit(solution)/shard_map/ppermute | solution.py:983
  36.5 2.6 %collective-permute-start.10 = (f32[4,2,16,8,128]{4,3,2,1,0:T(8,128)S(1)}, f32[4,2,16,8,128]{4,3,2,1,0:T(8,128)S(1)}, u32[]{:S(2)}, u32[]{:S(2)}) collective-permute-start(f32[4,2,16,8,128]{4,3,2,1,0:T(8,128)S(1)} %pad_maximum_fusion.1.tod_here_ref), channel_id=1, source_target_pairs={{0,1},{1,0},{2,3},{3,2},{4,5},{5,4},{6,7},{7,6},{8,9},{9,8},{10,11... | collective-permute-start | bytes 1572872 | tf_op jit(solution)/shard_map/ppermute | solution.py:1051

commit v6 on v5

--- a/solution.py
+++ b/solution.py
@@ -159,8 +159,8 @@
 ROWS = 8
 OUT_TILES = 8
 PAIR_BATCH = 8
-WRITES = 6
-DET_BATCH = 16
+WRITES = 12
+DET_BATCH = 8
 SUM_SETS = 2
 MAP_BATCH = 8
 BIG = float(1 << 24)
@@ -468,9 +468,10 @@
 
 def map_kernel(
     shape, wafer_ref, det_ref, rep_ref, size_ref, pair_ref, group_ref, move_ref, float_smem, whole_smem,
-    angle_here_ref, angle_across_ref, angle_other_ref, tod_here_ref, tod_other_ref, column_ref,
+    start_ref, angle_here_ref, angle_across_ref, angle_other_ref, tod_here_ref, tod_other_ref,
+    place_ref, x_ref, r_ref,
     angle_ref, tod_ref, cos_ref, sin_ref, clean_ref, noise_ref, weight_ref,
-    share_ref, rows_ref, sorted_ref, angle_sem, tod_sem, *more_refs,
+    share_ref, rows_ref, sorted_ref, column_ref, write_ref, angle_sem, tod_sem, write_sem, *more_refs,
 ):
     wafers, dets, reps, tiles, owners, capacity, owner_rows, lag_count = shape
     devices = wafers * dets * reps
@@ -555,7 +556,7 @@
 
     def clear_sorted(n, carry):
         at = pl.ds(pl.multiple_of(n * ROWS, ROWS), ROWS)
-        sorted_ref[at, :] = jnp.zeros((ROWS, 6 * PBLOCK), jnp.float32)
+        sorted_ref[at, :] = jnp.zeros((ROWS, 2 * LANES), jnp.float32)
         return carry
 
     lax.fori_loop(0, sorted_ref.shape[0] // ROWS, clear_sorted, 0)
@@ -755,6 +756,91 @@
 
     factor = zero
     steps = []
+    width = OUT_TILES * LANES
+    out_steps = x_ref.shape[1] // width
+    depth = lax.broadcasted_iota(jnp.int32, (LANES, LANES), 0)
+
+    def solution_at(at):
+        result = []
+        for c in range(3):
+            value = steps[0] * d_maps[0][c][at]
+            for k in range(1, ITERS):
+                value = value + steps[k] * d_maps[k][c][at]
+            result.append(value)
+        return result
+
+    def copy_out(out_ref, block, slot):
+        to = pl.ds(pl.multiple_of(block * width, width), width)
+        return pltpu.make_async_copy(write_ref.at[slot], out_ref.at[:, to], write_sem.at[slot])
+
+    def write_map(out_ref, order, values_of):
+        def place_pixels(at, carry):
+            team = lax.rem(lax.div(at, reps * ROWS), dets)
+            turn = (3 * (team * ROWS + (at & (ROWS - 1)))) & (PBLOCK - 1)
+            inside = (lane & (PBLOCK - 1)) >= turn
+            left, right, third = values_of(at)
+            halves = jnp.where(low, left, turn_half(right)), jnp.where(low, turn_half(left), right)
+            for half, (value, other) in enumerate(zip(halves, unfold(third))):
+                value = jnp.where(
+                    inside, pltpu.roll(value, turn, 1), pltpu.roll(value, turn + PBLOCK, 1)
+                )
+                rows = pl.ds(pl.multiple_of((2 * at + half) * ROWS, ROWS), ROWS)
+                rows_ref[rows, 0:LANES] = value
+                rows_ref[rows, LANES : 2 * LANES] = pltpu.roll(other, turn, 1)
+            return carry
+
+        loop(count, place_pixels, 0, 16)
+
+        def pick(device, carry):
+            for c in range(capacity):
+                move = move_ref[device, c]
+                source, target = move & ((1 << 16) - 1), move >> 16
+                sorted_ref[pl.ds(target, 1), :] = rows_ref[pl.ds(source, 1), :]
+            return carry
+
+        lax.fori_loop(0, devices, pick, 0)
+        for tile in range(column_ref.shape[0]):
+            columns = sorted_ref[tile * LANES : (tile + 1) * LANES, :].T[0 : 3 * PBLOCK]
+            high = columns.astype(jnp.bfloat16)
+            column_ref[tile, :, 0:LANES] = high
+            column_ref[tile, :, LANES : 2 * LANES] = (columns - high.astype(jnp.float32)).astype(
+                jnp.bfloat16
+            )
+
+        def spread(group, tile):
+            chosen = []
+            for k in range(OUT_TILES):
+                place = jnp.broadcast_to(place_ref[pl.ds(group + k, 1), :], (LANES, LANES))
+                place = jnp.where(place == depth + tile * LANES, 1.0, 0.0)
+                chosen.append(place.astype(jnp.bfloat16))
+            chosen = jnp.concatenate(chosen, axis=1)
+            chosen = jnp.concatenate([chosen, chosen], axis=0)
+            return jnp.dot(column_ref[tile], chosen, preferred_element_type=jnp.float32)
+
+        def one_block(block, carry):
+            number = order * out_steps + block
+            slot = lax.rem(number, WRITES)
+
+            @pl.when(number >= WRITES)
+            def _():
+                copy_out(out_ref, block, slot).wait()
+
+            group = block * OUT_TILES
+            start, end = start_ref[0, group], start_ref[0, group + OUT_TILES]
+            first = lax.shift_right_logical(start, 7)
+            last = lax.shift_right_logical(jnp.maximum(end - 1, start), 7)
+            write_ref[slot] = spread(group, first)
+
+            def add_tile(tile, carry):
+                write_ref[slot] += spread(group, tile)
+                return carry
+
+            lax.fori_loop(first + 1, last + 1, add_tile, 0)
+            copy_out(out_ref, block, slot).start()
+            return carry
+
+        lax.fori_loop(0, out_steps, one_block, 0)
+
     for iteration, d_map in enumerate(d_maps):
         last = iteration == ITERS - 1
 
@@ -788,9 +874,11 @@
         if not iteration:
             energy = whole_sum(first_energy)
         product = filter_streams()
-        return_streams(image_map)
         step = energy / whole_sum(product + prior_weight * prior)
         steps.append(step)
+        if last:
+            write_map(x_ref, 0, solution_at)
+        return_streams(image_map)
 
         def new_residual(at, c):
             return r_map[c][at] - step * (image_map[c][at] + prior_weight * d_map[c][at])
@@ -816,107 +904,9 @@
             factor = next_energy / energy
             energy = next_energy
         else:
-
-            def place_pixels(at, carry):
-                team = lax.rem(lax.div(at, reps * ROWS), dets)
-                turn = (3 * (team * ROWS + (at & (ROWS - 1)))) & (PBLOCK - 1)
-                inside = (lane & (PBLOCK - 1)) >= turn
-                values = []
-                for c in range(3):
-                    value = steps[0] * d_maps[0][c][at]
-                    for k in range(1, ITERS):
-                        value = value + steps[k] * d_maps[k][c][at]
-                    values.append(value)
-                values += [new_residual(at, c) for c in range(3)]
-                for c in range(3):
-                    left, right = values[2 * c], values[2 * c + 1]
-                    halves = (
-                        jnp.where(low, left, turn_half(right)), jnp.where(low, turn_half(left), right)
-                    )
-                    for half, value in enumerate(halves):
-                        value = jnp.where(
-                            inside, pltpu.roll(value, turn, 1), pltpu.roll(value, turn + PBLOCK, 1)
-                        )
-                        rows = pl.ds(pl.multiple_of((2 * at + half) * ROWS, ROWS), ROWS)
-                        rows_ref[rows, c * LANES : (c + 1) * LANES] = value
-                return carry
-
-            loop(count, place_pixels, 0, 8)
-
-    def pick(device, carry):
-        for c in range(capacity):
-            move = move_ref[device, c]
-            source, target = move & ((1 << 16) - 1), move >> 16
-            sorted_ref[pl.ds(target, 1), :] = rows_ref[pl.ds(source, 1), :]
-        return carry
-
-    lax.fori_loop(0, devices, pick, 0)
-
-    def turn_tile(tile, carry):
-        columns = sorted_ref[pl.ds(pl.multiple_of(tile * LANES, LANES), LANES), :].T
-        high = columns.astype(jnp.bfloat16)
-        column_ref[tile, :, 0:LANES] = high
-        column_ref[tile, :, LANES : 2 * LANES] = (columns - high.astype(jnp.float32)).astype(
-            jnp.bfloat16
-        )
-        return carry
-
-    lax.fori_loop(0, column_ref.shape[0], turn_tile, 0)
-
-
-def write_kernel(start_ref, column_ref, place_ref, x_ref, r_ref, x_buffer, r_buffer, x_sem, r_sem):
-    height = 3 * PBLOCK
-    width = OUT_TILES * LANES
-    steps = x_ref.shape[1] // width
-    depth = lax.broadcasted_iota(jnp.int32, (LANES, LANES), 0)
-
-    def copies(step, slot):
-        to = pl.ds(pl.multiple_of(step * width, width), width)
-        return (
-            pltpu.make_async_copy(x_buffer.at[slot], x_ref.at[:, to], x_sem.at[slot]),
-            pltpu.make_async_copy(r_buffer.at[slot], r_ref.at[:, to], r_sem.at[slot]),
-        )
-
-    def spread(group, tile):
-        chosen = []
-        for k in range(OUT_TILES):
-            place = jnp.broadcast_to(place_ref[pl.ds(group + k, 1), :], (LANES, LANES))
-            chosen.append(jnp.where(place == depth + tile * LANES, 1.0, 0.0).astype(jnp.bfloat16))
-        chosen = jnp.concatenate(chosen, axis=1)
-        chosen = jnp.concatenate([chosen, chosen], axis=0)
-        return jnp.dot(column_ref[tile], chosen, preferred_element_type=jnp.float32)
-
-    def one_step(step, carry):
-        slot = lax.rem(step, WRITES)
-
-        @pl.when(step >= WRITES)
-        def _():
-            for copy in copies(step - WRITES, slot):
-                copy.wait()
-
-        group = step * OUT_TILES
-        start, end = start_ref[0, group], start_ref[0, group + OUT_TILES]
-        first = lax.shift_right_logical(start, 7)
-        last = lax.shift_right_logical(jnp.maximum(end - 1, start), 7)
-        values = spread(group, first)
-        x_buffer[slot] = values[:height]
-        r_buffer[slot] = values[height:]
-
-        def add_tile(tile, carry):
-            values = spread(group, tile)
-            x_buffer[slot] += values[:height]
-            r_buffer[slot] += values[height:]
-            return carry
-
-        lax.fori_loop(first + 1, last + 1, add_tile, 0)
-        for copy in copies(step, slot):
-            copy.start()
-        return carry
-
-    lax.fori_loop(0, steps, one_step, 0)
-    for step in range(steps - WRITES, steps):
-        for copy in copies(step, step % WRITES):
-            copy.wait()
+            write_map(r_ref, 1, lambda at: [new_residual(at, c) for c in range(3)])
+    for block in range(WRITES):
+        copy_out(r_ref, out_steps - WRITES + block, (2 * out_steps - WRITES + block) % WRITES).wait()
 
 
 def part_shape(sizes, tod, hit_list, band_lag):
@@ -1005,7 +995,7 @@
     riders = jnp.concatenate([angles, tables.reshape(2 * reps, ROWS, LANES)])
     samples, riders = lax.optimization_barrier((samples, riders))
     samples = jnp.stack([samples, other_wafer(samples)])
-    samples, *blocks = lax.optimization_barrier((samples, *along_det(riders)))
+    blocks = along_det(riders)
     samples = along_det(samples)
     tables = jnp.stack([block[tiles:] for block in blocks])
     angles = jnp.stack([block[:tiles] for block in blocks])
@@ -1039,7 +1029,7 @@
             pltpu.SemaphoreType.DMA((devices,)),
         ],
         compiler_params=params(8),
-        cost_estimate=pl.CostEstimate(flops=10**9, bytes_accessed=5 * 10**7, transcendentals=0),
+        cost_estimate=pl.CostEstimate(flops=10**6, bytes_accessed=10**6, transcendentals=0),
         name="lists",
     )(*place_here[:2], tables)
     angles, angles_across, samples, lists = lax.optimization_barrier(
@@ -1052,38 +1042,31 @@
     stream = pltpu.VMEM((count, ROWS, LANES), f32)
     sky = pltpu.VMEM((devices * ROWS + 1, ROWS, LANES), f32)
     group_sums = pltpu.VMEM((NSUB, octets * ROWS, LANES), f32)
-    columns = pl.pallas_call(
+    x_turned, r_turned = pl.pallas_call(
         functools.partial(map_kernel, shape),
-        out_shape=jax.ShapeDtypeStruct((slots // LANES + 1, 2 * height, 2 * LANES), jnp.bfloat16),
-        in_specs=[smem] * 9 + [anywhere] * 5,
-        out_specs=vmem,
+        out_shape=[jax.ShapeDtypeStruct((height, owner_rows), f32)] * 2,
+        in_specs=[smem] * 10 + [anywhere] * 5 + [vmem],
+        out_specs=[anywhere] * 2,
         scratch_shapes=[
             stream, stream, stream, stream,
             pltpu.VMEM((detectors, octets * ROWS, LANES), f32),
             pltpu.VMEM((detectors, octets * ROWS, LANES), f32),
             sky,
             pltpu.VMEM((wafers * NSUB, ROWS, LANES), f32),
-            pltpu.VMEM((total, 2 * height), f32),
-            pltpu.VMEM((slots + LANES + ROWS, 2 * height), f32),
+            pltpu.VMEM((total, 2 * LANES), f32),
+            pltpu.VMEM((slots + LANES + ROWS, 2 * LANES), f32),
+            pltpu.VMEM((slots // LANES + 1, height, 2 * LANES), jnp.bfloat16),
+            pltpu.VMEM((WRITES, height, OUT_TILES * LANES), f32),
             pltpu.SemaphoreType.DMA((devices,)),
             pltpu.SemaphoreType.DMA((devices,)),
+            pltpu.SemaphoreType.DMA((WRITES,)),
         ] + [sky] * (3 * (3 + ITERS)) + [group_sums] * (2 * wafers * SUM_SETS),
-        compiler_params=params(30),
+        compiler_params=params(40),
         name="map_maker",
     )(
-        *place_here, size, pair, group, moves, floats, whole, *angle_blocks,
-        *sample_blocks,
+        *place_here, size, pair, group, moves, floats, whole, start, *angle_blocks,
+        *sample_blocks, place,
     )
-    buffers = pltpu.VMEM((WRITES, height, OUT_TILES * LANES), f32)
-    x_turned, r_turned = pl.pallas_call(
-        write_kernel,
-        out_shape=[jax.ShapeDtypeStruct((height, owner_rows), f32)] * 2,
-        in_specs=[smem, vmem, vmem],
-        out_specs=[anywhere] * 2,
-        scratch_shapes=[buffers, buffers] + [pltpu.SemaphoreType.DMA((WRITES,))] * 2,
-        compiler_params=params(16),
-        name="write",
-    )(start, columns, place)
     return x_turned.T, r_turned.T
 
 

time: 88.5 us -> 94.3 us (1.066)
  Pallas kernels: 58.7 us -> 63.2 us
  starting transfers between devices: 13.3 us -> 15.1 us
  waiting for transfers between devices: 12.2 us -> 11 us
    pallas_call x2 -> x1, Pallas kernels: 49.7 us -> 54.1 us  [whole_part(): pl.pallas_call(functools.partial(map_kernel, shape), out_shape=[jax.Shape...]
    ppermute x6, starting transfers between devices: 8.69 us -> 9.89 us  [along_det(): lax.ppermute(block, 'det', [(i, (i + shift) % dets) for i in range(dets)])]
    ppermute x3, waiting for transfers between devices: 3.71 us -> 2.72 us  [other_wafer(): return lax.ppermute(here, 'wafer', swap)]
where the time goes in v6:
time: 94.3 us; the launch traced here: 94 us
  Pallas kernels  63.2 us (67%)
  starting transfers between devices  15.1 us (16%)
  waiting for transfers between devices  11 us (12%)
  blocking collectives  2.14 us (2%)
  other arithmetic  1.8 us (2%)
    pallas_call x1, Pallas kernels, whole_part(): pl.pallas_call(functools.partial(map_kernel, shape), out_shape=[jax.Shape...  54.1 us
    ppermute x6, starting transfers between devices, along_det(): lax.ppermute(block, 'det', [(i, (i + shift) % dets) for i in range(dets)])  9.89 us
    pallas_call x1, Pallas kernels, whole_part(): pl.pallas_call(functools.partial(list_kernel, shape), out_shape=[jax.Shap...  7.38 us
    ppermute x6, waiting for transfers between devices, along_det(): lax.ppermute(block, 'det', [(i, (i + shift) % dets) for i in range(dets)])  6.26 us
    ppermute x3, starting transfers between devices, other_wafer(): return lax.ppermute(here, 'wafer', swap)  4.6 us
    ppermute x3, waiting for transfers between devices, other_wafer(): return lax.ppermute(here, 'wafer', swap)  2.72 us
    all_gather x1, blocking collectives, whole_part(): tables = lax.all_gather(tables, 'rep', axis=0, tiled=False)  2.14 us
  transfers between devices with their start and end apart: 11, of which 6 were waited for; matrix products, arithmetic and copies ran while one was open for 1% of the time, Pallas kernels for 8%

profile of v6, /device:TPU:0, one launch (start us, length us, event | category | flops | bytes accessed | tf_op | source)
XLA Modules:
  0.0 94.0 jit_solution(3812567706825126488)
XLA Ops:
  0.6 1.7 %pack.1 = (f32[2,8,128]{2,1,0:T(8,128)}, f32[8,16,128]{2,1,0:T(8,128)}, f32[8,16,128]{2,1,0:T(8,128)}) custom-call(f32[8,2048]{1,0:T(8,128)} %bitcast.56, f32[8,2048]{1,0:T(8,128)} %bitcast.57, s32[8,16]{1,0:T(8,128)} %bitcast.63, s32[8,32]{1,0:T(8,128)} %bitcast.64, s32[1,8]{1,0:T(1,128)} %group_ref.1, f32[1,8]{1,0:T(1,128)} %base_ref.1, f32[4,8]{1,0:T(4,128)} %bitcast.65, ...), custom_call_target="tpu_custom_call" | custom-call | tf_op jit(solution)/shard_map/pack/pallas_call | solution.py:975
  2.3 2.1 %all-gather = f32[4,8,128]{2,1,0:T(8,128)S(1)} all-gather(f32[2,8,128]{2,1,0:T(8,128)} %get-tuple-element.35), channel_id=2, replica_groups=mesh['groups'=2,'det'=4,'wafer'=2,'rep'=2] {'rep'}, dimensions={0}, use_global_device_ids=true | all-gather | bytes 24576 | tf_op jit(solution)/shard_map/all_gather | solution.py:994
  4.5 0.8 pad_maximum_fusion.5
  5.3 4.9 %collective-permute-start.2 = (f32[20,8,128]{2,1,0:T(8,128)S(1)}, f32[20,8,128]{2,1,0:T(8,128)S(1)}, u32[]{:S(2)}, u32[]{:S(2)}) collective-permute-start(f32[20,8,128]{2,1,0:T(8,128)S(1)} %pad_maximum_fusion.5), channel_id=1, source_target_pairs={{0,12},{4,0},{8,4},{12,8},{1,13},{5,1},{9,5},{13,9},{2,14},{6,2},{... | collective-permute-start | bytes 245768 | tf_op jit(solution)/shard_map/ppermute | solution.py:964
  10.2 0.0 collective-permute-start.1
  10.2 1.0 %collective-permute-start = (f32[20,8,128]{2,1,0:T(8,128)S(1)}, f32[20,8,128]{2,1,0:T(8,128)S(1)}, u32[]{:S(2)}, u32[]{:S(2)}) collective-permute-start(f32[20,8,128]{2,1,0:T(8,128)S(1)} %pad_maximum_fusion.5), channel_id=1, source_target_pairs={{0,4},{4,8},{8,12},{12,0},{1,5},{5,9},{9,13},{13,1},{2,6},{6,10},{... | collective-permute-start | bytes 245768 | tf_op jit(solution)/shard_map/ppermute | solution.py:964
  11.2 1.5 %collective-permute-start.5 = (f32[16,8,128]{2,1,0:T(8,128)}, f32[16,8,128]{2,1,0:T(8,128)S(1)}, u32[]{:S(2)}, u32[]{:S(2)}) collective-permute-start(f32[16,8,128]{2,1,0:T(8,128)} %bitcast.59), channel_id=1, source_target_pairs={{0,2},{2,0},{1,3},{3,1},{4,6},{6,4},{5,7},{7,5},{8,10},{10,8},{9,1... | collective-permute-start | bytes 196616 | tf_op jit(solution)/shard_map/ppermute | solution.py:970
  12.8 0.3 collective-permute-done.2
  13.1 5.2 %collective-permute-done.1 = f32[20,8,128]{2,1,0:T(8,128)S(1)} collective-permute-done((f32[20,8,128]{2,1,0:T(8,128)S(1)}, f32[20,8,128]{2,1,0:T(8,128)S(1)}, u32[]{:S(2)}, u32[]{:S(2)}) %collective-permute-start.1) | collective-permute-done | bytes 81952 | tf_op jit(solution)/shard_map/ppermute | solution.py:964
  18.3 1.6 %collective-permute-start.3 = (f32[4,4,8,128]{3,2,1,0:T(8,128)S(1)}, f32[4,4,8,128]{3,2,1,0:T(8,128)S(1)}, u32[]{:S(2)}, u32[]{:S(2)}) collective-permute-start(f32[4,4,8,128]{3,2,1,0:T(8,128)S(1)} %pad_maximum_fusion.6), channel_id=1, source_target_pairs={{0,2},{2,0},{1,3},{3,1},{4,6},{6,4},{5,7},{7,5},{8,10},{10,8},{9,1... | collective-permute-start | bytes 196616 | tf_op jit(solution)/shard_map/ppermute | solution.py:970
  20.0 2.7 %collective-permute-done.3 = f32[4,4,8,128]{3,2,1,0:T(8,128)S(1)} collective-permute-done((f32[4,4,8,128]{3,2,1,0:T(8,128)S(1)}, f32[4,4,8,128]{3,2,1,0:T(8,128)S(1)}, u32[]{:S(2)}, u32[]{:S(2)}) %collective-permute-start.3) | collective-permute-done | bytes 65568 | tf_op jit(solution)/shard_map/ppermute | solution.py:970
  22.7 1.6 %collective-permute-start.4 = (f32[4,16,8,128]{3,2,1,0:T(8,128)S(1)}, f32[4,16,8,128]{3,2,1,0:T(8,128)S(1)}, u32[]{:S(2)}, u32[]{:S(2)}) collective-permute-start(f32[4,16,8,128]{3,2,1,0:T(8,128)S(1)} %pad_maximum_fusion.2.angle_here_ref), channel_id=1, source_target_pairs={{0,2},{2,0},{1,3},{3,1},{4,6},{6,4},{5,7},{7,5},{8,10},{10,8},{9,1... | collective-permute-start | bytes 786440 | tf_op jit(solution)/shard_map/ppermute | solution.py:970
  24.2 0.0 collective-permute-done.5
  24.2 0.8 pad_maximum_fusion.4
  25.1 1.9 %collective-permute-start.8 = (f32[2,16,8,128]{3,2,1,0:T(8,128)S(1)}, f32[2,16,8,128]{3,2,1,0:T(8,128)S(1)}, u32[]{:S(2)}, u32[]{:S(2)}) collective-permute-start(f32[2,16,8,128]{3,2,1,0:T(8,128)S(1)} %pad_maximum_fusion.4), channel_id=1, source_target_pairs={{0,12},{4,0},{8,4},{12,8},{1,13},{5,1},{9,5},{13,9},{2,14},{6,2},{... | collective-permute-start | bytes 393224 | tf_op jit(solution)/shard_map/ppermute | solution.py:964
  27.0 0.1 collective-permute-start.7
  27.1 1.9 %collective-permute-start.6 = (f32[2,16,8,128]{3,2,1,0:T(8,128)S(1)}, f32[2,16,8,128]{3,2,1,0:T(8,128)S(1)}, u32[]{:S(2)}, u32[]{:S(2)}) collective-permute-start(f32[2,16,8,128]{3,2,1,0:T(8,128)S(1)} %pad_maximum_fusion.4), channel_id=1, source_target_pairs={{0,4},{4,8},{8,12},{12,0},{1,5},{5,9},{9,13},{13,1},{2,6},{6,10},{... | collective-permute-start | bytes 393224 | tf_op jit(solution)/shard_map/ppermute | solution.py:964
  29.1 7.4 %lists.1 = (f32[16,128]{1,0:T(8,128)S(1)}, s32[16,128]{1,0:T(8,128)S(1)}, s32[256,128]{1,0:T(8,128)S(1)}, s32[8,256]{1,0:T(8,128)S(1)}, s32[16,128]{1,0:T(8,128)...) custom-call(s32[1]{0:T(128)} %bitcast.wafer_ref, s32[1]{0:T(128)} %bitcast.1.det_ref, ...), custom_call_target="tpu_custom_call" | custom-call | flops 1000000 | bytes 1000000 | tf_op jit(solution)/shard_map/lists/pallas_call | solution.py:1007
  36.5 0.7 collective-permute-done.7
  37.2 0.1 collective-permute-start.9
  37.3 0.6 collective-permute-start.10
  37.9 1.3 %collective-permute-done.9.angle_other_ref = f32[2,4,16,8,128]{4,3,2,1,0:T(8,128)S(1)} collective-permute-done((f32[2,4,16,8,128]{4,3,2,1,0:T(8,128)S(1)}, f32[2,4,16,8,128]{4,3,2,1,0:T(8,128)S(1)}, u32[]{:S(2)}, u32[]{:S(2)}) %collective-permute-start.9) | collective-permute-done | bytes 524320 | tf_op jit(solution)/shard_map/ppermute | solution.py:973
  39.2 0.7 collective-permute-done.10.tod_other_ref
  39.9 54.1 %map_maker.1 = (f32[192,24576]{1,0:T(8,128)}, f32[192,24576]{1,0:T(8,128)}) custom-call(s32[1]{0:T(128)} %bitcast.wafer_ref, s32[1]{0:T(128)} %bitcast.1.det_ref, s32[1]{0:T(128)} %bitcast.2.rep_ref, s32[2]{0:T(128)S(1)} %get-tuple-element.48.size_ref, s32[2048]{0:T(1024)S(1)} %get-tuple-element.49.pair_ref, s32[2048]{0:T(1024)S(1)} %get-tuple-element.50.group_ref, ...), custom_call_target="tpu_custom_call" | custom-call | tf_op jit(solution)/shard_map/map_maker/pallas_call | solution.py:1045
  (17 shorter events, 0.2 us)
Async XLA Ops:
  5.3 7.8 %collective-permute-start.2 = (f32[20,8,128]{2,1,0:T(8,128)S(1)}, f32[20,8,128]{2,1,0:T(8,128)S(1)}, u32[]{:S(2)}, u32[]{:S(2)}) collective-permute-start(f32[20,8,128]{2,1,0:T(8,128)S(1)} %pad_maximum_fusion.5), channel_id=1, source_target_pairs={{0,12},{4,0},{8,4},{12,8},{1,13},{5,1},{9,5},{13,9},{2,14},{6,2},{... | collective-permute-start | bytes 245768 | tf_op jit(solution)/shard_map/ppermute | solution.py:964
  10.2 8.1 %collective-permute-start.1 = (f32[20,8,128]{2,1,0:T(8,128)S(1)}, f32[20,8,128]{2,1,0:T(8,128)S(1)}, u32[]{:S(2)}, u32[]{:S(2)}) collective-permute-start(f32[20,8,128]{2,1,0:T(8,128)S(1)} %pad_maximum_fusion.5), channel_id=1, source_target_pairs={{0,8},{4,12},{8,0},{12,4},{1,9},{5,13},{9,1},{13,5},{2,10},{6,14},... | collective-permute-start | bytes 245768 | tf_op jit(solution)/shard_map/ppermute | solution.py:964
  10.2 8.1 %collective-permute-start = (f32[20,8,128]{2,1,0:T(8,128)S(1)}, f32[20,8,128]{2,1,0:T(8,128)S(1)}, u32[]{:S(2)}, u32[]{:S(2)}) collective-permute-start(f32[20,8,128]{2,1,0:T(8,128)S(1)} %pad_maximum_fusion.5), channel_id=1, source_target_pairs={{0,4},{4,8},{8,12},{12,0},{1,5},{5,9},{9,13},{13,1},{2,6},{6,10},{... | collective-permute-start | bytes 245768 | tf_op jit(solution)/shard_map/ppermute | solution.py:964
  11.2 13.0 %collective-permute-start.5 = (f32[16,8,128]{2,1,0:T(8,128)}, f32[16,8,128]{2,1,0:T(8,128)S(1)}, u32[]{:S(2)}, u32[]{:S(2)}) collective-permute-start(f32[16,8,128]{2,1,0:T(8,128)} %bitcast.59), channel_id=1, source_target_pairs={{0,2},{2,0},{1,3},{3,1},{4,6},{6,4},{5,7},{7,5},{8,10},{10,8},{9,1... | collective-permute-start | bytes 196616 | tf_op jit(solution)/shard_map/ppermute | solution.py:970
  18.3 4.3 %collective-permute-start.3 = (f32[4,4,8,128]{3,2,1,0:T(8,128)S(1)}, f32[4,4,8,128]{3,2,1,0:T(8,128)S(1)}, u32[]{:S(2)}, u32[]{:S(2)}) collective-permute-start(f32[4,4,8,128]{3,2,1,0:T(8,128)S(1)} %pad_maximum_fusion.6), channel_id=1, source_target_pairs={{0,2},{2,0},{1,3},{3,1},{4,6},{6,4},{5,7},{7,5},{8,10},{10,8},{9,1... | collective-permute-start | bytes 196616 | tf_op jit(solution)/shard_map/ppermute | solution.py:970
  22.7 14.5 %collective-permute-start.4 = (f32[4,16,8,128]{3,2,1,0:T(8,128)S(1)}, f32[4,16,8,128]{3,2,1,0:T(8,128)S(1)}, u32[]{:S(2)}, u32[]{:S(2)}) collective-permute-start(f32[4,16,8,128]{3,2,1,0:T(8,128)S(1)} %pad_maximum_fusion.2.angle_here_ref), channel_id=1, source_target_pairs={{0,2},{2,0},{1,3},{3,1},{4,6},{6,4},{5,7},{7,5},{8,10},{10,8},{9,1... | collective-permute-start | bytes 786440 | tf_op jit(solution)/shard_map/ppermute | solution.py:970
  25.1 11.4 %collective-permute-start.8 = (f32[2,16,8,128]{3,2,1,0:T(8,128)S(1)}, f32[2,16,8,128]{3,2,1,0:T(8,128)S(1)}, u32[]{:S(2)}, u32[]{:S(2)}) collective-permute-start(f32[2,16,8,128]{3,2,1,0:T(8,128)S(1)} %pad_maximum_fusion.4), channel_id=1, source_target_pairs={{0,12},{4,0},{8,4},{12,8},{1,13},{5,1},{9,5},{13,9},{2,14},{6,2},{... | collective-permute-start | bytes 393224 | tf_op jit(solution)/shard_map/ppermute | solution.py:964
  27.0 10.1 %collective-permute-start.7 = (f32[2,16,8,128]{3,2,1,0:T(8,128)S(1)}, f32[2,16,8,128]{3,2,1,0:T(8,128)S(1)}, u32[]{:S(2)}, u32[]{:S(2)}) collective-permute-start(f32[2,16,8,128]{3,2,1,0:T(8,128)S(1)} %pad_maximum_fusion.4), channel_id=1, source_target_pairs={{0,8},{4,12},{8,0},{12,4},{1,9},{5,13},{9,1},{13,5},{2,10},{6,14},... | collective-permute-start | bytes 393224 | tf_op jit(solution)/shard_map/ppermute | solution.py:964
  27.1 10.0 %collective-permute-start.6 = (f32[2,16,8,128]{3,2,1,0:T(8,128)S(1)}, f32[2,16,8,128]{3,2,1,0:T(8,128)S(1)}, u32[]{:S(2)}, u32[]{:S(2)}) collective-permute-start(f32[2,16,8,128]{3,2,1,0:T(8,128)S(1)} %pad_maximum_fusion.4), channel_id=1, source_target_pairs={{0,4},{4,8},{8,12},{12,0},{1,5},{5,9},{9,13},{13,1},{2,6},{6,10},{... | collective-permute-start | bytes 393224 | tf_op jit(solution)/shard_map/ppermute | solution.py:964
  37.2 2.0 %collective-permute-start.9 = (f32[2,4,16,8,128]{4,3,2,1,0:T(8,128)S(1)}, f32[2,4,16,8,128]{4,3,2,1,0:T(8,128)S(1)}, u32[]{:S(2)}, u32[]{:S(2)}) collective-permute-start(f32[2,4,16,8,128]{4,3,2,1,0:T(8,128)S(1)} %pad_maximum_fusion), channel_id=1, source_target_pairs={{0,1},{1,0},{2,3},{3,2},{4,5},{5,4},{6,7},{7,6},{8,9},{9,8},{10,11... | collective-permute-start | bytes 1572872 | tf_op jit(solution)/shard_map/ppermute | solution.py:973
  37.3 2.6 %collective-permute-start.10 = (f32[4,2,16,8,128]{4,3,2,1,0:T(8,128)S(1)}, f32[4,2,16,8,128]{4,3,2,1,0:T(8,128)S(1)}, u32[]{:S(2)}, u32[]{:S(2)}) collective-permute-start(f32[4,2,16,8,128]{4,3,2,1,0:T(8,128)S(1)} %pad_maximum_fusion.1.tod_here_ref), channel_id=1, source_target_pairs={{0,1},{1,0},{2,3},{3,2},{4,5},{5,4},{6,7},{7,6},{8,9},{9,8},{10,11... | collective-permute-start | bytes 1572872 | tf_op jit(solution)/shard_map/ppermute | solution.py:1041

commit v7 on v5

--- a/solution.py
+++ b/solution.py
@@ -160,7 +160,7 @@
 OUT_TILES = 8
 PAIR_BATCH = 8
 WRITES = 6
-DET_BATCH = 16
+DET_BATCH = 8
 SUM_SETS = 2
 MAP_BATCH = 8
 BIG = float(1 << 24)
@@ -259,7 +259,7 @@
             device = ((self_ref[0] ^ swap_wafer) * dets + det) * reps
             copies.append(
                 pltpu.make_async_copy(
-                    source_ref.at[swap_wafer, shift], part_ref.at[pl.ds(device, reps)],
+                    source_ref.at[shift, swap_wafer], part_ref.at[pl.ds(device, reps)],
                     sem.at[len(copies)],
                 )
             )
@@ -1002,17 +1002,16 @@
         lax.axis_index(axis).astype(i32).reshape(1) for axis in ("wafer", "det", "rep")
     ]
     tables = lax.all_gather(tables, "rep", axis=0, tiled=False)
-    riders = jnp.concatenate([angles, tables.reshape(2 * reps, ROWS, LANES)])
-    samples, riders = lax.optimization_barrier((samples, riders))
-    samples = jnp.stack([samples, other_wafer(samples)])
-    samples, *blocks = lax.optimization_barrier((samples, *along_det(riders)))
-    samples = along_det(samples)
-    tables = jnp.stack([block[tiles:] for block in blocks])
-    angles = jnp.stack([block[:tiles] for block in blocks])
-    tables = jnp.stack([tables, other_wafer(tables)])
-    tables = tables.reshape(wafers, dets, reps, 2, ROWS, LANES)
     angles, tables = lax.optimization_barrier((angles, tables))
-    angles_across = other_wafer(angles)
+    riders = jnp.concatenate([samples, tables.reshape(2 * reps, ROWS, LANES)])
+    riders = jnp.stack([riders, other_wafer(riders)])
+    angles = jnp.stack(along_det(angles))
+    blocks = along_det(riders)
+    tables = jnp.stack([block[:, tiles:] for block in blocks])
+    tables = tables.reshape(dets, wafers, reps, 2, ROWS, LANES)
+    samples = jnp.stack([block[:, :tiles] for block in blocks])
+    angle_blocks = other_rep(angles, other_wafer(angles))
+    sample_blocks = samples, lax.ppermute(samples, "rep", swap)
     table_rows = jax.ShapeDtypeStruct((devices, LANES), i32)
     lists = pl.pallas_call(
         functools.partial(list_kernel, shape),
@@ -1042,13 +1041,7 @@
         cost_estimate=pl.CostEstimate(flops=10**9, bytes_accessed=5 * 10**7, transcendentals=0),
         name="lists",
     )(*place_here[:2], tables)
-    angles, angles_across, samples, lists = lax.optimization_barrier(
-        (angles, angles_across, samples, lists)
-    )
     floats, whole, place, start, moves, size, pair, group = lists
-    angle_blocks = other_rep(angles, angles_across)
-    samples = jnp.stack(samples)
-    sample_blocks = samples, lax.ppermute(samples, "rep", swap)
     stream = pltpu.VMEM((count, ROWS, LANES), f32)
     sky = pltpu.VMEM((devices * ROWS + 1, ROWS, LANES), f32)
     group_sums = pltpu.VMEM((NSUB, octets * ROWS, LANES), f32)

time: 88.5 us -> 91.3 us (1.032)
  starting transfers between devices: 13.3 us -> 14.5 us
    ppermute x6, waiting for transfers between devices: 6.41 us -> 12.7 us  [along_det(): lax.ppermute(block, 'det', [(i, (i + shift) % dets) for i in range(dets)])]
    ppermute x3 -> x2, waiting for transfers between devices: 3.71 us -> 0.01 us  [other_wafer(): return lax.ppermute(here, 'wafer', swap)]
    ppermute x6, starting transfers between devices: 8.69 us -> 10.4 us  [along_det(): lax.ppermute(block, 'det', [(i, (i + shift) % dets) for i in range(dets)])]
    ppermute x1, waiting for transfers between devices: 1.3 us -> 0.01 us  [other_rep(): return (here, across, lax.ppermute(jnp.stack([here, across]), 'rep', swap))]
    ppermute x3 -> x2, starting transfers between devices: 4.01 us -> 3.47 us  [other_wafer(): return lax.ppermute(here, 'wafer', swap)]
  transfers between devices with their start and end apart: 11 -> 10, of which waited for: 6 -> 3; matrix products, arithmetic and copies ran while one was open for 1% -> 1% of each run, Pallas kernels for 8% -> 9%
where the time goes in v7:
time: 91.3 us; the launch traced here: 91.5 us
  Pallas kernels  59.5 us (65%)
  starting transfers between devices  14.5 us (16%)
  waiting for transfers between devices  12.7 us (14%)
  blocking collectives  2.14 us (2%)
  other arithmetic  1.83 us (2%)
    pallas_call x1, Pallas kernels, whole_part(): pl.pallas_call(functools.partial(map_kernel, shape), out_shape=jax.ShapeD...  36.6 us
    pallas_call x1, Pallas kernels, whole_part(): pl.pallas_call(write_kernel, out_shape=[jax.ShapeDtypeStruct((height, own...  13.3 us
    ppermute x6, waiting for transfers between devices, along_det(): lax.ppermute(block, 'det', [(i, (i + shift) % dets) for i in range(dets)])  12.7 us
    ppermute x6, starting transfers between devices, along_det(): lax.ppermute(block, 'det', [(i, (i + shift) % dets) for i in range(dets)])  10.4 us
    pallas_call x1, Pallas kernels, whole_part(): pl.pallas_call(functools.partial(list_kernel, shape), out_shape=[jax.Shap...  7.94 us
    ppermute x2, starting transfers between devices, other_wafer(): return lax.ppermute(here, 'wafer', swap)  3.47 us
    all_gather x1, blocking collectives, whole_part(): tables = lax.all_gather(tables, 'rep', axis=0, tiled=False)  2.14 us
  transfers between devices with their start and end apart: 10, of which 3 were waited for; matrix products, arithmetic and copies ran while one was open for 1% of the time, Pallas kernels for 9%

profile of v7, /device:TPU:0, one launch (start us, length us, event | category | flops | bytes accessed | tf_op | source)
XLA Modules:
  0.0 91.5 jit_solution(8307555931476195266)
XLA Ops:
  0.6 1.7 %pack.1 = (f32[2,8,128]{2,1,0:T(8,128)}, f32[8,16,128]{2,1,0:T(8,128)}, f32[8,16,128]{2,1,0:T(8,128)}) custom-call(f32[8,2048]{1,0:T(8,128)} %bitcast.56, f32[8,2048]{1,0:T(8,128)} %bitcast.57, s32[8,16]{1,0:T(8,128)} %bitcast.59, s32[8,32]{1,0:T(8,128)} %bitcast.60, s32[1,8]{1,0:T(1,128)} %group_ref.1, f32[1,8]{1,0:T(1,128)} %base_ref.1, f32[4,8]{1,0:T(4,128)} %bitcast.61, ...), custom_call_target="tpu_custom_call" | custom-call | tf_op jit(solution)/shard_map/pack/pallas_call | solution.py:985
  2.3 2.1 %all-gather = f32[4,8,128]{2,1,0:T(8,128)S(1)} all-gather(f32[2,8,128]{2,1,0:T(8,128)} %get-tuple-element.19), channel_id=2, replica_groups=mesh['groups'=2,'det'=4,'wafer'=2,'rep'=2] {'rep'}, dimensions={0}, use_global_device_ids=true | all-gather | bytes 24576 | tf_op jit(solution)/shard_map/all_gather | solution.py:1004
  4.5 0.9 fusion.3
  5.3 2.9 %collective-permute-start = (f32[20,8,128]{2,1,0:T(8,128)S(1)}, f32[20,8,128]{2,1,0:T(8,128)S(1)}, u32[]{:S(2)}, u32[]{:S(2)}) collective-permute-start(f32[20,8,128]{2,1,0:T(8,128)S(1)} %get-tuple-element.35), channel_id=1, source_target_pairs={{0,2},{2,0},{1,3},{3,1},{4,6},{6,4},{5,7},{7,5},{8,10},{10,8},{9,1... | collective-permute-start | bytes 245768 | tf_op jit(solution)/shard_map/ppermute | solution.py:980
  8.2 3.6 %collective-permute-start.6 = (f32[16,8,128]{2,1,0:T(8,128)}, f32[16,8,128]{2,1,0:T(8,128)S(1)}, u32[]{:S(2)}, u32[]{:S(2)}) collective-permute-start(f32[16,8,128]{2,1,0:T(8,128)} %bitcast.49), channel_id=1, source_target_pairs={{0,12},{4,0},{8,4},{12,8},{1,13},{5,1},{9,5},{13,9},{2,14},{6,2},{... | collective-permute-start | bytes 196616 | tf_op jit(solution)/shard_map/ppermute | solution.py:974
  11.8 0.0 collective-permute-start.5
  11.8 1.0 %collective-permute-start.4 = (f32[16,8,128]{2,1,0:T(8,128)}, f32[16,8,128]{2,1,0:T(8,128)S(1)}, u32[]{:S(2)}, u32[]{:S(2)}) collective-permute-start(f32[16,8,128]{2,1,0:T(8,128)} %bitcast.51), channel_id=1, source_target_pairs={{0,4},{4,8},{8,12},{12,0},{1,5},{5,9},{9,13},{13,1},{2,6},{6,10},{... | collective-permute-start | bytes 196616 | tf_op jit(solution)/shard_map/ppermute | solution.py:974
  12.8 0.0 collective-permute-done
  12.8 2.0 %collective-permute-start.2 = (f32[2,20,8,128]{3,2,1,0:T(8,128)S(1)}, f32[2,20,8,128]{3,2,1,0:T(8,128)S(1)}, u32[]{:S(2)}, u32[]{:S(2)}) collective-permute-start(f32[2,20,8,128]{3,2,1,0:T(8,128)S(1)} %pad_maximum_fusion.3), channel_id=1, source_target_pairs={{0,8},{4,12},{8,0},{12,4},{1,9},{5,13},{9,1},{13,5},{2,10},{6,14},... | collective-permute-start | bytes 491528 | tf_op jit(solution)/shard_map/ppermute | solution.py:974
  14.8 0.0 collective-permute-done.6
  14.8 7.5 %collective-permute-done.5 = f32[16,8,128]{2,1,0:T(8,128)S(1)} collective-permute-done((f32[16,8,128]{2,1,0:T(8,128)}, f32[16,8,128]{2,1,0:T(8,128)S(1)}, u32[]{:S(2)}, u32[]{:S(2)}) %collective-permute-start.5) | collective-permute-done | bytes 65568 | tf_op jit(solution)/shard_map/ppermute | solution.py:974
  22.3 0.0 collective-permute-done.4
  22.4 0.9 fusion.4
  23.2 0.6 collective-permute-start.7
  23.8 0.3 collective-permute-start.1
  24.1 3.5 %collective-permute-start.3 = (f32[2,20,8,128]{3,2,1,0:T(8,128)S(1)}, f32[2,20,8,128]{3,2,1,0:T(8,128)S(1)}, u32[]{:S(2)}, u32[]{:S(2)}) collective-permute-start(f32[2,20,8,128]{3,2,1,0:T(8,128)S(1)} %pad_maximum_fusion.3), channel_id=1, source_target_pairs={{0,12},{4,0},{8,4},{12,8},{1,13},{5,1},{9,5},{13,9},{2,14},{6,2},{... | collective-permute-start | bytes 491528 | tf_op jit(solution)/shard_map/ppermute | solution.py:974
  27.7 5.1 %collective-permute-done.1 = f32[2,20,8,128]{3,2,1,0:T(8,128)S(1)} collective-permute-done((f32[2,20,8,128]{3,2,1,0:T(8,128)S(1)}, f32[2,20,8,128]{3,2,1,0:T(8,128)S(1)}, u32[]{:S(2)}, u32[]{:S(2)}) %collective-permute-start.1) | collective-permute-done | bytes 163872 | tf_op jit(solution)/shard_map/ppermute | solution.py:974
  32.8 0.1 collective-permute-done.3
  32.9 0.1 collective-permute-start.9
  33.0 0.0 collective-permute-done.7.angle_across_ref
  33.0 0.5 collective-permute-start.8
  33.6 7.9 %lists.1 = (f32[16,128]{1,0:T(8,128)S(1)}, s32[16,128]{1,0:T(8,128)S(1)}, s32[256,128]{1,0:T(8,128)S(1)}, s32[8,256]{1,0:T(8,128)S(1)}, s32[16,128]{1,0:T(8,128)...) custom-call(s32[1]{0:T(128)} %bitcast.wafer_ref, s32[1]{0:T(128)} %bitcast.1.det_ref, ...), custom_call_target="tpu_custom_call" | custom-call | flops 1000000000 | bytes 50000000 | tf_op jit(solution)/shard_map/lists/pallas_call | solution.py:1016
  41.6 36.6 %map_maker.1.column_ref = bf16[5,384,256]{2,1,0:T(8,128)(2,1)S(1)} custom-call(s32[1]{0:T(128)} %bitcast.wafer_ref, s32[1]{0:T(128)} %bitcast.1.det_ref, s32[1]{0:T(128)} %bitcast.20.rep_ref, s32[2]{0:T(128)S(1)} %get-tuple-element.22.size_ref, s32[2048]{0:T(1024)S(1)} %get-tuple-element.23.pair_ref, s32[2048]{0:T(1024)S(1)} %get-tuple-element.24.group_ref, ...), custom_call_target="tpu_custom_call" | custom-call | tf_op jit(solution)/shard_map/map_maker/pallas_call | solution.py:1048
  78.2 13.3 %write.1 = (f32[192,24576]{1,0:T(8,128)}, f32[192,24576]{1,0:T(8,128)}) custom-call(s32[8,256]{1,0:T(8,128)S(1)} %get-tuple-element.21.start_ref, bf16[5,384,256]{2,1,0:T(8,128)(2,1)S(1)} %map_maker.1.column_ref, s32[256,128]{1,0:T(8,128)S(1)} %get-tuple-element.29.place_ref), custom_call_target="tpu_custom_call" | custom-call | tf_op jit(solution)/shard_map/write/pallas_call | solution.py:1071
  (15 shorter events, 0.2 us)
Async XLA Ops:
  5.3 7.5 %collective-permute-start = (f32[20,8,128]{2,1,0:T(8,128)S(1)}, f32[20,8,128]{2,1,0:T(8,128)S(1)}, u32[]{:S(2)}, u32[]{:S(2)}) collective-permute-start(f32[20,8,128]{2,1,0:T(8,128)S(1)} %get-tuple-element.35), channel_id=1, source_target_pairs={{0,2},{2,0},{1,3},{3,1},{4,6},{6,4},{5,7},{7,5},{8,10},{10,8},{9,1... | collective-permute-start | bytes 245768 | tf_op jit(solution)/shard_map/ppermute | solution.py:980
  8.2 6.6 %collective-permute-start.6 = (f32[16,8,128]{2,1,0:T(8,128)}, f32[16,8,128]{2,1,0:T(8,128)S(1)}, u32[]{:S(2)}, u32[]{:S(2)}) collective-permute-start(f32[16,8,128]{2,1,0:T(8,128)} %bitcast.49), channel_id=1, source_target_pairs={{0,12},{4,0},{8,4},{12,8},{1,13},{5,1},{9,5},{13,9},{2,14},{6,2},{... | collective-permute-start | bytes 196616 | tf_op jit(solution)/shard_map/ppermute | solution.py:974
  11.8 10.5 %collective-permute-start.5 = (f32[16,8,128]{2,1,0:T(8,128)}, f32[16,8,128]{2,1,0:T(8,128)S(1)}, u32[]{:S(2)}, u32[]{:S(2)}) collective-permute-start(f32[16,8,128]{2,1,0:T(8,128)} %bitcast.50), channel_id=1, source_target_pairs={{0,8},{4,12},{8,0},{12,4},{1,9},{5,13},{9,1},{13,5},{2,10},{6,14},... | collective-permute-start | bytes 196616 | tf_op jit(solution)/shard_map/ppermute | solution.py:974
  11.8 10.5 %collective-permute-start.4 = (f32[16,8,128]{2,1,0:T(8,128)}, f32[16,8,128]{2,1,0:T(8,128)S(1)}, u32[]{:S(2)}, u32[]{:S(2)}) collective-permute-start(f32[16,8,128]{2,1,0:T(8,128)} %bitcast.51), channel_id=1, source_target_pairs={{0,4},{4,8},{8,12},{12,0},{1,5},{5,9},{9,13},{13,1},{2,6},{6,10},{... | collective-permute-start | bytes 196616 | tf_op jit(solution)/shard_map/ppermute | solution.py:974
  12.8 14.8 %collective-permute-start.2 = (f32[2,20,8,128]{3,2,1,0:T(8,128)S(1)}, f32[2,20,8,128]{3,2,1,0:T(8,128)S(1)}, u32[]{:S(2)}, u32[]{:S(2)}) collective-permute-start(f32[2,20,8,128]{3,2,1,0:T(8,128)S(1)} %pad_maximum_fusion.3), channel_id=1, source_target_pairs={{0,8},{4,12},{8,0},{12,4},{1,9},{5,13},{9,1},{13,5},{2,10},{6,14},... | collective-permute-start | bytes 491528 | tf_op jit(solution)/shard_map/ppermute | solution.py:974
  23.2 9.8 %collective-permute-start.7 = (f32[4,16,8,128]{3,2,1,0:T(8,128)S(1)}, f32[4,16,8,128]{3,2,1,0:T(8,128)S(1)}, u32[]{:S(2)}, u32[]{:S(2)}) collective-permute-start(f32[4,16,8,128]{3,2,1,0:T(8,128)S(1)} %get-tuple-element.33.angle_here_ref), channel_id=1, source_target_pairs={{0,2},{2,0},{1,3},{3,1},{4,6},{6,4},{5,7},{7,5},{8,10},{10,8},{9,1... | collective-permute-start | bytes 786440 | tf_op jit(solution)/shard_map/ppermute | solution.py:980
  23.8 8.9 %collective-permute-start.1 = (f32[2,20,8,128]{3,2,1,0:T(8,128)S(1)}, f32[2,20,8,128]{3,2,1,0:T(8,128)S(1)}, u32[]{:S(2)}, u32[]{:S(2)}) collective-permute-start(f32[2,20,8,128]{3,2,1,0:T(8,128)S(1)} %pad_maximum_fusion.3), channel_id=1, source_target_pairs={{0,4},{4,8},{8,12},{12,0},{1,5},{5,9},{9,13},{13,1},{2,6},{6,10},{... | collective-permute-start | bytes 491528 | tf_op jit(solution)/shard_map/ppermute | solution.py:974
  24.1 8.7 %collective-permute-start.3 = (f32[2,20,8,128]{3,2,1,0:T(8,128)S(1)}, f32[2,20,8,128]{3,2,1,0:T(8,128)S(1)}, u32[]{:S(2)}, u32[]{:S(2)}) collective-permute-start(f32[2,20,8,128]{3,2,1,0:T(8,128)S(1)} %pad_maximum_fusion.3), channel_id=1, source_target_pairs={{0,12},{4,0},{8,4},{12,8},{1,13},{5,1},{9,5},{13,9},{2,14},{6,2},{... | collective-permute-start | bytes 491528 | tf_op jit(solution)/shard_map/ppermute | solution.py:974
  32.9 8.7 %collective-permute-start.9 = (f32[4,2,16,8,128]{4,3,2,1,0:T(8,128)S(1)}, f32[4,2,16,8,128]{4,3,2,1,0:T(8,128)S(1)}, u32[]{:S(2)}, u32[]{:S(2)}) collective-permute-start(f32[4,2,16,8,128]{4,3,2,1,0:T(8,128)S(1)} %pad_maximum_fusion.1.tod_here_ref), channel_id=1, source_target_pairs={{0,1},{1,0},{2,3},{3,2},{4,5},{5,4},{6,7},{7,6},{8,9},{9,8},{10,11... | collective-permute-start | bytes 1572872 | tf_op jit(solution)/shard_map/ppermute | solution.py:1014
  33.0 8.6 %collective-permute-start.8 = (f32[2,4,16,8,128]{4,3,2,1,0:T(8,128)S(1)}, f32[2,4,16,8,128]{4,3,2,1,0:T(8,128)S(1)}, u32[]{:S(2)}, u32[]{:S(2)}) collective-permute-start(f32[2,4,16,8,128]{4,3,2,1,0:T(8,128)S(1)} %pad_maximum_fusion), channel_id=1, source_target_pairs={{0,1},{1,0},{2,3},{3,2},{4,5},{5,4},{6,7},{7,6},{8,9},{9,8},{10,11... | collective-permute-start | bytes 1572872 | tf_op jit(solution)/shard_map/ppermute | solution.py:983

commit v8 on v5

--- a/solution.py
+++ b/solution.py
@@ -197,7 +197,7 @@
 
 def pack_kernel(
     shape, angle_ref, tod_ref, row_ref, hit_ref, group_ref, base_ref, coef_ref, lag_ref,
-    table_ref, angle_rows_ref, tod_rows_ref,
+    angle_rows_ref, tod_rows_ref,
 ):
     wafers, dets, reps, tiles, owners, capacity, owner_rows, lag_count = shape
     lane, sub = tile_iotas()
@@ -224,10 +224,10 @@
         lag = lag_ref[j : j + 1, :].astype(jnp.float32)
         whole = whole + pltpu.roll(spread(lag, ROWS), at, 1)
     table = jnp.where(sub == 0, wide(ids), jnp.where(sub == 1, wide(floats), wide(whole)))
-    table_ref[0] = table
-    table_ref[1] = spread(lists.astype(jnp.float32), capacity)
+    angle_rows_ref[ROWS, 0:ROWS, :] = table
+    angle_rows_ref[ROWS, ROWS : 2 * ROWS, :] = spread(lists.astype(jnp.float32), capacity)
     for b in range(tiles):
-        angle_rows_ref[:, b, :] = angle_ref[:, b * LANES : (b + 1) * LANES]
+        angle_rows_ref[0:ROWS, b, :] = angle_ref[:, b * LANES : (b + 1) * LANES]
         tod_rows_ref[:, b, :] = tod_ref[:, b * LANES : (b + 1) * LANES]
 
 
@@ -252,17 +252,18 @@
 def table_copies(shape, self_ref, source_ref, part_ref, sem):
     wafers, dets, reps = shape[:3]
     copies = []
-    for swap_wafer in range(wafers):
-        for shift in range(dets):
-            det = self_ref[1] - shift
-            det = jnp.where(det < 0, det + dets, det)
-            device = ((self_ref[0] ^ swap_wafer) * dets + det) * reps
-            copies.append(
-                pltpu.make_async_copy(
-                    source_ref.at[swap_wafer, shift], part_ref.at[pl.ds(device, reps)],
-                    sem.at[len(copies)],
+    for rep in range(reps):
+        for swap_wafer in range(wafers):
+            for shift in range(dets):
+                det = self_ref[1] - shift
+                det = jnp.where(det < 0, det + dets, det)
+                device = ((self_ref[0] ^ swap_wafer) * dets + det) * reps + rep
+                copies.append(
+                    pltpu.make_async_copy(
+                        source_ref.at[rep, swap_wafer, shift], part_ref.at[device],
+                        sem.at[len(copies)],
+                    )
                 )
-            )
     for copy in copies:
         copy.start()
     for copy in copies:
@@ -982,36 +983,33 @@
     def other_rep(here, across):
         return here, across, lax.ppermute(jnp.stack([here, across]), "rep", swap)
 
-    tables, angles, samples = pl.pallas_call(
+    angles, samples = pl.pallas_call(
         functools.partial(pack_kernel, shape),
         out_shape=[
-            jax.ShapeDtypeStruct((2, ROWS, LANES), f32),
-            jax.ShapeDtypeStruct((ROWS, tiles, LANES), f32),
+            jax.ShapeDtypeStruct((ROWS + 1, tiles, LANES), f32),
             jax.ShapeDtypeStruct((ROWS, tiles, LANES), f32),
         ],
         in_specs=[vmem] * 8,
-        out_specs=[vmem] * 3,
+        out_specs=[vmem] * 2,
         compiler_params=params(60),
         name="pack",
     )(
         psi[0], tod[0], point_row[0], hit_list[0, 0, 0], group_id, a_zero, band_coef[0].T,
         band_lag[0].T,
     )
-    angles, samples = (stream.reshape(tiles, ROWS, LANES) for stream in (angles, samples))
+    riders = angles.reshape(tiles + 2, ROWS, LANES)
+    samples = samples.reshape(tiles, ROWS, LANES)
     place_here = [
         lax.axis_index(axis).astype(i32).reshape(1) for axis in ("wafer", "det", "rep")
     ]
-    tables = lax.all_gather(tables, "rep", axis=0, tiled=False)
-    riders = jnp.concatenate([angles, tables.reshape(2 * reps, ROWS, LANES)])
-    samples, riders = lax.optimization_barrier((samples, riders))
     samples = jnp.stack([samples, other_wafer(samples)])
-    samples, *blocks = lax.optimization_barrier((samples, *along_det(riders)))
-    samples = along_det(samples)
+    blocks = along_det(riders)
     tables = jnp.stack([block[tiles:] for block in blocks])
     angles = jnp.stack([block[:tiles] for block in blocks])
     tables = jnp.stack([tables, other_wafer(tables)])
-    tables = tables.reshape(wafers, dets, reps, 2, ROWS, LANES)
-    angles, tables = lax.optimization_barrier((angles, tables))
+    tables = lax.all_gather(tables, "rep", axis=0, tiled=False)
+    samples, angles, tables = lax.optimization_barrier((samples, angles, tables))
+    samples = along_det(samples)
     angles_across = other_wafer(angles)
     table_rows = jax.ShapeDtypeStruct((devices, LANES), i32)
     lists = pl.pallas_call(

time: 88.5 us -> 88.8 us (level)
  waiting for transfers between devices: 12.2 us -> 9.23 us
  starting transfers between devices: 13.3 us -> 15.2 us
  local copies, waits for them, and re-layouts: 0.04 us -> 1.56 us
    ppermute x6, waiting for transfers between devices: 6.41 us -> 3.37 us  [along_det(): lax.ppermute(block, 'det', [(i, (i + shift) % dets) for i in range(dets)])]
    ppermute x6, starting transfers between devices: 8.69 us -> 10 us  [along_det(): lax.ppermute(block, 'det', [(i, (i + shift) % dets) for i in range(dets)])]
    pallas_call x1, Pallas kernels: 7.26 us -> 8.34 us  [whole_part(): pl.pallas_call(functools.partial(list_kernel, shape), out_shape=[jax.Shap...]
  transfers between devices with their start and end apart: 11 -> 11, of which waited for: 6 -> 6; matrix products, arithmetic and copies ran while one was open for 1% -> 3% of each run, Pallas kernels for 8% -> 9%
where the time goes in v8:
time: 88.8 us; the launch traced here: 89 us
  Pallas kernels  59.5 us (67%)
  starting transfers between devices  15.2 us (17%)
  waiting for transfers between devices  9.23 us (10%)
  blocking collectives  1.89 us (2%)
  local copies, waits for them, and re-layouts  1.56 us (2%)
  other arithmetic  0.95 us (1%)
    pallas_call x1, Pallas kernels, whole_part(): pl.pallas_call(functools.partial(map_kernel, shape), out_shape=jax.ShapeD...  36.2 us
    pallas_call x1, Pallas kernels, whole_part(): pl.pallas_call(write_kernel, out_shape=[jax.ShapeDtypeStruct((height, own...  13.3 us
    ppermute x6, starting transfers between devices, along_det(): lax.ppermute(block, 'det', [(i, (i + shift) % dets) for i in range(dets)])  10 us
    pallas_call x1, Pallas kernels, whole_part(): pl.pallas_call(functools.partial(list_kernel, shape), out_shape=[jax.Shap...  8.34 us
    ppermute x3, starting transfers between devices, other_wafer(): return lax.ppermute(here, 'wafer', swap)  4.54 us
    ppermute x3, waiting for transfers between devices, other_wafer(): return lax.ppermute(here, 'wafer', swap)  3.81 us
    ppermute x6, waiting for transfers between devices, along_det(): lax.ppermute(block, 'det', [(i, (i + shift) % dets) for i in range(dets)])  3.37 us
    all_gather x1, blocking collectives, whole_part(): tables = lax.all_gather(tables, 'rep', axis=0, tiled=False)  1.89 us
  transfers between devices with their start and end apart: 11, of which 6 were waited for; matrix products, arithmetic and copies ran while one was open for 3% of the time, Pallas kernels for 9%

profile of v8, /device:TPU:0, one launch (start us, length us, event | category | flops | bytes accessed | tf_op | source)
XLA Modules:
  0.0 89.0 jit_solution(16274838225876695204)
XLA Ops:
  0.6 1.7 %pack.1 = (f32[9,16,128]{2,1,0:T(8,128)}, f32[8,16,128]{2,1,0:T(8,128)}) custom-call(f32[8,2048]{1,0:T(8,128)} %bitcast.55, f32[8,2048]{1,0:T(8,128)} %bitcast.56, s32[8,16]{1,0:T(8,128)} %bitcast.61, s32[8,32]{1,0:T(8,128)} %bitcast.62, s32[1,8]{1,0:T(1,128)} %group_ref.1, f32[1,8]{1,0:T(1,128)} %base_ref.1, f32[4,8]{1,0:T(4,128)} %bitcast.63, s32[4,8]{1,0:T(4,128)} %bitcast.64), custom_call_target="tpu_custom_call" | custom-call | tf_op jit(solution)/shard_map/pack/pallas_call | solution.py:986
  2.3 5.0 %collective-permute-start.3 = (f32[18,8,128]{2,1,0:T(8,128)}, f32[18,8,128]{2,1,0:T(8,128)S(1)}, u32[]{:S(2)}, u32[]{:S(2)}) collective-permute-start(f32[18,8,128]{2,1,0:T(8,128)} %bitcast.52), channel_id=1, source_target_pairs={{0,12},{4,0},{8,4},{12,8},{1,13},{5,1},{9,5},{13,9},{2,14},{6,2},{... | collective-permute-start | bytes 221192 | tf_op jit(solution)/shard_map/ppermute | solution.py:975
  7.4 1.0 %collective-permute-start.1 = (f32[18,8,128]{2,1,0:T(8,128)}, f32[18,8,128]{2,1,0:T(8,128)S(1)}, u32[]{:S(2)}, u32[]{:S(2)}) collective-permute-start(f32[18,8,128]{2,1,0:T(8,128)} %bitcast.54), channel_id=1, source_target_pairs={{0,4},{4,8},{8,12},{12,0},{1,5},{5,9},{9,13},{13,1},{2,6},{6,10},{... | collective-permute-start | bytes 221192 | tf_op jit(solution)/shard_map/ppermute | solution.py:975
  8.4 1.5 %collective-permute-start = (f32[16,8,128]{2,1,0:T(8,128)}, f32[16,8,128]{2,1,0:T(8,128)S(1)}, u32[]{:S(2)}, u32[]{:S(2)}) collective-permute-start(f32[16,8,128]{2,1,0:T(8,128)} %bitcast.57), channel_id=1, source_target_pairs={{0,2},{2,0},{1,3},{3,1},{4,6},{6,4},{5,7},{7,5},{8,10},{10,8},{9,1... | collective-permute-start | bytes 196616 | tf_op jit(solution)/shard_map/ppermute | solution.py:981
  9.9 0.7 slice_bitcast_fusion.6
  10.6 0.8 slice.26
  11.4 1.4 %collective-permute-done = f32[16,8,128]{2,1,0:T(8,128)S(1)} collective-permute-done((f32[16,8,128]{2,1,0:T(8,128)}, f32[16,8,128]{2,1,0:T(8,128)S(1)}, u32[]{:S(2)}, u32[]{:S(2)}) %collective-permute-start) | collective-permute-done | bytes 65568 | tf_op jit(solution)/shard_map/ppermute | solution.py:981
  12.9 0.8 pad_maximum_fusion.3
  13.7 0.8 collective-permute-done.2
  14.6 1.6 %collective-permute-start.4 = (f32[4,2,8,128]{3,2,1,0:T(8,128)S(1)}, f32[4,2,8,128]{3,2,1,0:T(8,128)S(1)}, u32[]{:S(2)}, u32[]{:S(2)}) collective-permute-start(f32[4,2,8,128]{3,2,1,0:T(8,128)S(1)} %get-tuple-element.61), channel_id=1, source_target_pairs={{0,2},{2,0},{1,3},{3,1},{4,6},{6,4},{5,7},{7,5},{8,10},{10,8},{9,1... | collective-permute-start | bytes 98312 | tf_op jit(solution)/shard_map/ppermute | solution.py:981
  16.2 2.4 %collective-permute-done.4 = f32[4,2,8,128]{3,2,1,0:T(8,128)S(1)} collective-permute-done((f32[4,2,8,128]{3,2,1,0:T(8,128)S(1)}, f32[4,2,8,128]{3,2,1,0:T(8,128)S(1)}, u32[]{:S(2)}, u32[]{:S(2)}) %collective-permute-start.4) | collective-permute-done | bytes 32800 | tf_op jit(solution)/shard_map/ppermute | solution.py:981
  18.6 1.9 %all-gather = f32[4,4,2,8,128]{4,3,2,1,0:T(8,128)S(1)} all-gather(f32[2,4,2,8,128]{4,3,2,1,0:T(8,128)S(1)} %pad_maximum_fusion.4), channel_id=2, replica_groups=mesh['groups'=2,'det'=4,'wafer'=2,'rep'=2] {'rep'}, dimensions={0}, use_global_device_ids=true | all-gather | bytes 196608 | tf_op jit(solution)/shard_map/all_gather | solution.py:1010
  20.5 1.5 %collective-permute-start.5 = (f32[4,16,8,128]{3,2,1,0:T(8,128)S(1)}, f32[4,16,8,128]{3,2,1,0:T(8,128)S(1)}, u32[]{:S(2)}, u32[]{:S(2)}) collective-permute-start(f32[4,16,8,128]{3,2,1,0:T(8,128)S(1)} %pad_maximum_fusion.2.angle_here_ref), channel_id=1, source_target_pairs={{0,2},{2,0},{1,3},{3,1},{4,6},{6,4},{5,7},{7,5},{8,10},{10,8},{9,1... | collective-permute-start | bytes 786440 | tf_op jit(solution)/shard_map/ppermute | solution.py:981
  22.0 2.0 %collective-permute-start.8 = (f32[2,16,8,128]{3,2,1,0:T(8,128)S(1)}, f32[2,16,8,128]{3,2,1,0:T(8,128)S(1)}, u32[]{:S(2)}, u32[]{:S(2)}) collective-permute-start(f32[2,16,8,128]{3,2,1,0:T(8,128)S(1)} %pad_maximum_fusion.3), channel_id=1, source_target_pairs={{0,12},{4,0},{8,4},{12,8},{1,13},{5,1},{9,5},{13,9},{2,14},{6,2},{... | collective-permute-start | bytes 393224 | tf_op jit(solution)/shard_map/ppermute | solution.py:975
  24.0 1.1 %collective-permute-start.7 = (f32[2,16,8,128]{3,2,1,0:T(8,128)S(1)}, f32[2,16,8,128]{3,2,1,0:T(8,128)S(1)}, u32[]{:S(2)}, u32[]{:S(2)}) collective-permute-start(f32[2,16,8,128]{3,2,1,0:T(8,128)S(1)} %pad_maximum_fusion.3), channel_id=1, source_target_pairs={{0,8},{4,12},{8,0},{12,4},{1,9},{5,13},{9,1},{13,5},{2,10},{6,14},... | collective-permute-start | bytes 393224 | tf_op jit(solution)/shard_map/ppermute | solution.py:975
  25.1 0.8 collective-permute-start.6
  25.9 8.3 %lists.1 = (f32[16,128]{1,0:T(8,128)S(1)}, s32[16,128]{1,0:T(8,128)S(1)}, s32[256,128]{1,0:T(8,128)S(1)}, s32[8,256]{1,0:T(8,128)S(1)}, s32[16,128]{1,0:T(8,128)...) custom-call(s32[1]{0:T(128)} %bitcast.23.wafer_ref, s32[1]{0:T(128)} %bitcast.24.det_ref, ...), custom_call_target="tpu_custom_call" | custom-call | flops 1000000000 | bytes 50000000 | tf_op jit(solution)/shard_map/lists/pallas_call | solution.py:1015
  34.3 2.5 %collective-permute-done.7 = f32[2,16,8,128]{3,2,1,0:T(8,128)S(1)} collective-permute-done((f32[2,16,8,128]{3,2,1,0:T(8,128)S(1)}, f32[2,16,8,128]{3,2,1,0:T(8,128)S(1)}, u32[]{:S(2)}, u32[]{:S(2)}) %collective-permute-start.7) | collective-permute-done | bytes 131104 | tf_op jit(solution)/shard_map/ppermute | solution.py:975
  36.8 0.1 collective-permute-start.9
  37.0 0.6 collective-permute-start.10
  37.5 1.3 %collective-permute-done.9.angle_other_ref = f32[2,4,16,8,128]{4,3,2,1,0:T(8,128)S(1)} collective-permute-done((f32[2,4,16,8,128]{4,3,2,1,0:T(8,128)S(1)}, f32[2,4,16,8,128]{4,3,2,1,0:T(8,128)S(1)}, u32[]{:S(2)}, u32[]{:S(2)}) %collective-permute-start.9) | collective-permute-done | bytes 524320 | tf_op jit(solution)/shard_map/ppermute | solution.py:984
  38.8 0.7 collective-permute-done.10.tod_other_ref
  39.6 36.2 %map_maker.1.column_ref = bf16[5,384,256]{2,1,0:T(8,128)(2,1)S(1)} custom-call(s32[1]{0:T(128)} %bitcast.23.wafer_ref, s32[1]{0:T(128)} %bitcast.24.det_ref, s32[1]{0:T(128)} %bitcast.25.rep_ref, s32[2]{0:T(128)S(1)} %get-tuple-element.45.size_ref, s32[2048]{0:T(1024)S(1)} %get-tuple-element.46.pair_ref, s32[2048]{0:T(1024)S(1)} %get-tuple-element.47.group_ref, ...), custom_call_target="tpu_custom_call" | custom-call | tf_op jit(solution)/shard_map/map_maker/pallas_call | solution.py:1053
  75.7 13.3 %write.1 = (f32[192,24576]{1,0:T(8,128)}, f32[192,24576]{1,0:T(8,128)}) custom-call(s32[8,256]{1,0:T(8,128)S(1)} %get-tuple-element.44.start_ref, bf16[5,384,256]{2,1,0:T(8,128)(2,1)S(1)} %map_maker.1.column_ref, s32[256,128]{1,0:T(8,128)S(1)} %get-tuple-element.57.place_ref), custom_call_target="tpu_custom_call" | custom-call | tf_op jit(solution)/shard_map/write/pallas_call | solution.py:1076
  (17 shorter events, 0.1 us)
Async XLA Ops:
  2.3 11.4 %collective-permute-start.3 = (f32[18,8,128]{2,1,0:T(8,128)}, f32[18,8,128]{2,1,0:T(8,128)S(1)}, u32[]{:S(2)}, u32[]{:S(2)}) collective-permute-start(f32[18,8,128]{2,1,0:T(8,128)} %bitcast.52), channel_id=1, source_target_pairs={{0,12},{4,0},{8,4},{12,8},{1,13},{5,1},{9,5},{13,9},{2,14},{6,2},{... | collective-permute-start | bytes 221192 | tf_op jit(solution)/shard_map/ppermute | solution.py:975
  7.4 7.2 %collective-permute-start.2 = (f32[18,8,128]{2,1,0:T(8,128)}, f32[18,8,128]{2,1,0:T(8,128)S(1)}, u32[]{:S(2)}, u32[]{:S(2)}) collective-permute-start(f32[18,8,128]{2,1,0:T(8,128)} %bitcast.53), channel_id=1, source_target_pairs={{0,8},{4,12},{8,0},{12,4},{1,9},{5,13},{9,1},{13,5},{2,10},{6,14},... | collective-permute-start | bytes 221192 | tf_op jit(solution)/shard_map/ppermute | solution.py:975
  7.4 7.2 %collective-permute-start.1 = (f32[18,8,128]{2,1,0:T(8,128)}, f32[18,8,128]{2,1,0:T(8,128)S(1)}, u32[]{:S(2)}, u32[]{:S(2)}) collective-permute-start(f32[18,8,128]{2,1,0:T(8,128)} %bitcast.54), channel_id=1, source_target_pairs={{0,4},{4,8},{8,12},{12,0},{1,5},{5,9},{9,13},{13,1},{2,6},{6,10},{... | collective-permute-start | bytes 221192 | tf_op jit(solution)/shard_map/ppermute | solution.py:975
  8.4 4.5 %collective-permute-start = (f32[16,8,128]{2,1,0:T(8,128)}, f32[16,8,128]{2,1,0:T(8,128)S(1)}, u32[]{:S(2)}, u32[]{:S(2)}) collective-permute-start(f32[16,8,128]{2,1,0:T(8,128)} %bitcast.57), channel_id=1, source_target_pairs={{0,2},{2,0},{1,3},{3,1},{4,6},{6,4},{5,7},{7,5},{8,10},{10,8},{9,1... | collective-permute-start | bytes 196616 | tf_op jit(solution)/shard_map/ppermute | solution.py:981
  14.6 4.0 %collective-permute-start.4 = (f32[4,2,8,128]{3,2,1,0:T(8,128)S(1)}, f32[4,2,8,128]{3,2,1,0:T(8,128)S(1)}, u32[]{:S(2)}, u32[]{:S(2)}) collective-permute-start(f32[4,2,8,128]{3,2,1,0:T(8,128)S(1)} %get-tuple-element.61), channel_id=1, source_target_pairs={{0,2},{2,0},{1,3},{3,1},{4,6},{6,4},{5,7},{7,5},{8,10},{10,8},{9,1... | collective-permute-start | bytes 98312 | tf_op jit(solution)/shard_map/ppermute | solution.py:981
  20.5 16.3 %collective-permute-start.5 = (f32[4,16,8,128]{3,2,1,0:T(8,128)S(1)}, f32[4,16,8,128]{3,2,1,0:T(8,128)S(1)}, u32[]{:S(2)}, u32[]{:S(2)}) collective-permute-start(f32[4,16,8,128]{3,2,1,0:T(8,128)S(1)} %pad_maximum_fusion.2.angle_here_ref), channel_id=1, source_target_pairs={{0,2},{2,0},{1,3},{3,1},{4,6},{6,4},{5,7},{7,5},{8,10},{10,8},{9,1... | collective-permute-start | bytes 786440 | tf_op jit(solution)/shard_map/ppermute | solution.py:981
  22.0 12.3 %collective-permute-start.8 = (f32[2,16,8,128]{3,2,1,0:T(8,128)S(1)}, f32[2,16,8,128]{3,2,1,0:T(8,128)S(1)}, u32[]{:S(2)}, u32[]{:S(2)}) collective-permute-start(f32[2,16,8,128]{3,2,1,0:T(8,128)S(1)} %pad_maximum_fusion.3), channel_id=1, source_target_pairs={{0,12},{4,0},{8,4},{12,8},{1,13},{5,1},{9,5},{13,9},{2,14},{6,2},{... | collective-permute-start | bytes 393224 | tf_op jit(solution)/shard_map/ppermute | solution.py:975
  24.0 12.8 %collective-permute-start.7 = (f32[2,16,8,128]{3,2,1,0:T(8,128)S(1)}, f32[2,16,8,128]{3,2,1,0:T(8,128)S(1)}, u32[]{:S(2)}, u32[]{:S(2)}) collective-permute-start(f32[2,16,8,128]{3,2,1,0:T(8,128)S(1)} %pad_maximum_fusion.3), channel_id=1, source_target_pairs={{0,8},{4,12},{8,0},{12,4},{1,9},{5,13},{9,1},{13,5},{2,10},{6,14},... | collective-permute-start | bytes 393224 | tf_op jit(solution)/shard_map/ppermute | solution.py:975
  25.1 11.7 %collective-permute-start.6 = (f32[2,16,8,128]{3,2,1,0:T(8,128)S(1)}, f32[2,16,8,128]{3,2,1,0:T(8,128)S(1)}, u32[]{:S(2)}, u32[]{:S(2)}) collective-permute-start(f32[2,16,8,128]{3,2,1,0:T(8,128)S(1)} %pad_maximum_fusion.3), channel_id=1, source_target_pairs={{0,4},{4,8},{8,12},{12,0},{1,5},{5,9},{9,13},{13,1},{2,6},{6,10},{... | collective-permute-start | bytes 393224 | tf_op jit(solution)/shard_map/ppermute | solution.py:975
  36.8 2.0 %collective-permute-start.9 = (f32[2,4,16,8,128]{4,3,2,1,0:T(8,128)S(1)}, f32[2,4,16,8,128]{4,3,2,1,0:T(8,128)S(1)}, u32[]{:S(2)}, u32[]{:S(2)}) collective-permute-start(f32[2,4,16,8,128]{4,3,2,1,0:T(8,128)S(1)} %pad_maximum_fusion), channel_id=1, source_target_pairs={{0,1},{1,0},{2,3},{3,2},{4,5},{5,4},{6,7},{7,6},{8,9},{9,8},{10,11... | collective-permute-start | bytes 1572872 | tf_op jit(solution)/shard_map/ppermute | solution.py:984
  37.0 2.6 %collective-permute-start.10 = (f32[4,2,16,8,128]{4,3,2,1,0:T(8,128)S(1)}, f32[4,2,16,8,128]{4,3,2,1,0:T(8,128)S(1)}, u32[]{:S(2)}, u32[]{:S(2)}) collective-permute-start(f32[4,2,16,8,128]{4,3,2,1,0:T(8,128)S(1)} %pad_maximum_fusion.1.tod_here_ref), channel_id=1, source_target_pairs={{0,1},{1,0},{2,3},{3,2},{4,5},{5,4},{6,7},{7,6},{8,9},{9,8},{10,11... | collective-permute-start | bytes 1572872 | tf_op jit(solution)/shard_map/ppermute | solution.py:1049

commit v9 on v5

--- a/solution.py
+++ b/solution.py
@@ -177,22 +177,23 @@
 
 
 def cosine_sine_double(angle):
-    turns = jnp.floor(angle * 1.2732395447351628 + 0.5)
-    reduced = 2.0 * angle - turns * 1.5703125
-    reduced = reduced - turns * 4.837512969970703125e-4
-    reduced = reduced - turns * 7.54978995489188216e-8
+    turns = jnp.floor(angle * 0.3183098861837907 + 0.5)
+    reduced = angle - turns * 3.140625
+    reduced = reduced - turns * 9.67653589793e-4
     square = reduced * reduced
-    sine = (-1.9515295891e-4 * square + 8.3321608736e-3) * square - 1.6666654611e-1
+    sine = square * -2.5052108385e-8 + 2.7557319224e-6
+    sine = sine * square - 1.9841269841e-4
+    sine = sine * square + 8.3333333333e-3
+    sine = sine * square - 1.6666666667e-1
     sine = sine * square * reduced + reduced
-    cosine = (2.443315711809948e-5 * square - 1.388731625493765e-3) * square
-    cosine = (cosine + 4.166664568298827e-2) * square * square - 0.5 * square + 1.0
-    quarter = turns.astype(jnp.int32)
-    odd = (quarter & 1) == 1
-    first = jnp.where(odd, sine, cosine)
-    second = jnp.where(odd, cosine, sine)
-    first = jnp.where(((quarter + 1) & 2) == 2, -first, first)
-    second = jnp.where((quarter & 2) == 2, -second, second)
-    return first, second
+    cosine = square * 2.0876756988e-9 - 2.7557319224e-7
+    cosine = cosine * square + 2.4801587302e-5
+    cosine = cosine * square - 1.3888888889e-3
+    cosine = cosine * square + 4.1666666667e-2
+    cosine = cosine * square - 0.5
+    cosine = cosine * square + 1.0
+    twice = sine + sine
+    return 1.0 - twice * sine, twice * cosine
 
 
 def pack_kernel(

time: 88.5 us -> 87.6 us (0.990)
  Pallas kernels: 58.7 us -> 57.1 us
    pallas_call x1, Pallas kernels: 36.4 us -> 34.9 us  [whole_part(): pl.pallas_call(functools.partial(map_kernel, shape), out_shape=jax.ShapeD...]
where the time goes in v9:
time: 87.6 us; the launch traced here: 87.3 us
  Pallas kernels  57.1 us (65%)
  starting transfers between devices  13.3 us (15%)
  waiting for transfers between devices  12.2 us (14%)
  blocking collectives  2.14 us (2%)
  other arithmetic  1.8 us (2%)
    pallas_call x1, Pallas kernels, whole_part(): pl.pallas_call(functools.partial(map_kernel, shape), out_shape=jax.ShapeD...  34.9 us
    pallas_call x1, Pallas kernels, whole_part(): pl.pallas_call(write_kernel, out_shape=[jax.ShapeDtypeStruct((height, own...  13.3 us
    ppermute x6, starting transfers between devices, along_det(): lax.ppermute(block, 'det', [(i, (i + shift) % dets) for i in range(dets)])  8.69 us
    pallas_call x1, Pallas kernels, whole_part(): pl.pallas_call(functools.partial(list_kernel, shape), out_shape=[jax.Shap...  7.25 us
    ppermute x6, waiting for transfers between devices, along_det(): lax.ppermute(block, 'det', [(i, (i + shift) % dets) for i in range(dets)])  6.42 us
    ppermute x3, starting transfers between devices, other_wafer(): return lax.ppermute(here, 'wafer', swap)  4.01 us
    ppermute x3, waiting for transfers between devices, other_wafer(): return lax.ppermute(here, 'wafer', swap)  3.71 us
    all_gather x1, blocking collectives, whole_part(): tables = lax.all_gather(tables, 'rep', axis=0, tiled=False)  2.14 us
  transfers between devices with their start and end apart: 11, of which 6 were waited for; matrix products, arithmetic and copies ran while one was open for 1% of the time, Pallas kernels for 8%

profile of v9, /device:TPU:0, one launch (start us, length us, event | category | flops | bytes accessed | tf_op | source)
XLA Modules:
  0.0 87.3 jit_solution(16107490781645037354)
XLA Ops:
  0.6 1.7 %pack.1 = (f32[2,8,128]{2,1,0:T(8,128)}, f32[8,16,128]{2,1,0:T(8,128)}, f32[8,16,128]{2,1,0:T(8,128)}) custom-call(f32[8,2048]{1,0:T(8,128)} %bitcast.52, f32[8,2048]{1,0:T(8,128)} %bitcast.53, s32[8,16]{1,0:T(8,128)} %bitcast.63, s32[8,32]{1,0:T(8,128)} %bitcast.64, s32[1,8]{1,0:T(1,128)} %group_ref.1, f32[1,8]{1,0:T(1,128)} %base_ref.1, f32[4,8]{1,0:T(4,128)} %bitcast.65, ...), custom_call_target="tpu_custom_call" | custom-call | tf_op jit(solution)/shard_map/pack/pallas_call | solution.py:986
  2.3 2.1 %all-gather = f32[4,8,128]{2,1,0:T(8,128)S(1)} all-gather(f32[2,8,128]{2,1,0:T(8,128)} %get-tuple-element.40), channel_id=2, replica_groups=mesh['groups'=2,'det'=4,'wafer'=2,'rep'=2] {'rep'}, dimensions={0}, use_global_device_ids=true | all-gather | bytes 24576 | tf_op jit(solution)/shard_map/all_gather | solution.py:1005
  4.5 0.8 pad_maximum_fusion.5
  5.3 2.8 %collective-permute-start = (f32[16,8,128]{2,1,0:T(8,128)}, f32[16,8,128]{2,1,0:T(8,128)S(1)}, u32[]{:S(2)}, u32[]{:S(2)}) collective-permute-start(f32[16,8,128]{2,1,0:T(8,128)} %bitcast.59), channel_id=1, source_target_pairs={{0,2},{2,0},{1,3},{3,1},{4,6},{6,4},{5,7},{7,5},{8,10},{10,8},{9,1... | collective-permute-start | bytes 196616 | tf_op jit(solution)/shard_map/ppermute | solution.py:981
  8.1 3.6 %collective-permute-start.3 = (f32[20,8,128]{2,1,0:T(8,128)S(1)}, f32[20,8,128]{2,1,0:T(8,128)S(1)}, u32[]{:S(2)}, u32[]{:S(2)}) collective-permute-start(f32[20,8,128]{2,1,0:T(8,128)S(1)} %pad_maximum_fusion.5), channel_id=1, source_target_pairs={{0,12},{4,0},{8,4},{12,8},{1,13},{5,1},{9,5},{13,9},{2,14},{6,2},{... | collective-permute-start | bytes 245768 | tf_op jit(solution)/shard_map/ppermute | solution.py:975
  11.7 1.0 %collective-permute-start.1 = (f32[20,8,128]{2,1,0:T(8,128)S(1)}, f32[20,8,128]{2,1,0:T(8,128)S(1)}, u32[]{:S(2)}, u32[]{:S(2)}) collective-permute-start(f32[20,8,128]{2,1,0:T(8,128)S(1)} %pad_maximum_fusion.5), channel_id=1, source_target_pairs={{0,4},{4,8},{8,12},{12,0},{1,5},{5,9},{9,13},{13,1},{2,6},{6,10},{... | collective-permute-start | bytes 245768 | tf_op jit(solution)/shard_map/ppermute | solution.py:975
  12.7 0.0 collective-permute-done
  12.7 0.8 pad_maximum_fusion.3
  13.6 1.0 %collective-permute-done.3 = f32[20,8,128]{2,1,0:T(8,128)S(1)} collective-permute-done((f32[20,8,128]{2,1,0:T(8,128)S(1)}, f32[20,8,128]{2,1,0:T(8,128)S(1)}, u32[]{:S(2)}, u32[]{:S(2)}) %collective-permute-start.3) | collective-permute-done | bytes 81952 | tf_op jit(solution)/shard_map/ppermute | solution.py:975
  14.6 4.8 %collective-permute-done.2 = f32[20,8,128]{2,1,0:T(8,128)S(1)} collective-permute-done((f32[20,8,128]{2,1,0:T(8,128)S(1)}, f32[20,8,128]{2,1,0:T(8,128)S(1)}, u32[]{:S(2)}, u32[]{:S(2)}) %collective-permute-start.2) | collective-permute-done | bytes 81952 | tf_op jit(solution)/shard_map/ppermute | solution.py:975
  19.4 0.0 collective-permute-done.1
  19.4 0.6 collective-permute-start.4
  20.1 3.7 %collective-permute-done.4 = f32[4,4,8,128]{3,2,1,0:T(8,128)S(1)} collective-permute-done((f32[4,4,8,128]{3,2,1,0:T(8,128)S(1)}, f32[4,4,8,128]{3,2,1,0:T(8,128)S(1)}, u32[]{:S(2)}, u32[]{:S(2)}) %collective-permute-start.4) | collective-permute-done | bytes 65568 | tf_op jit(solution)/shard_map/ppermute | solution.py:981
  23.8 0.6 collective-permute-start.5
  24.4 2.5 %collective-permute-start.8 = (f32[2,16,8,128]{3,2,1,0:T(8,128)S(1)}, f32[2,16,8,128]{3,2,1,0:T(8,128)S(1)}, u32[]{:S(2)}, u32[]{:S(2)}) collective-permute-start(f32[2,16,8,128]{3,2,1,0:T(8,128)S(1)} %pad_maximum_fusion.3), channel_id=1, source_target_pairs={{0,12},{4,0},{8,4},{12,8},{1,13},{5,1},{9,5},{13,9},{2,14},{6,2},{... | collective-permute-start | bytes 393224 | tf_op jit(solution)/shard_map/ppermute | solution.py:975
  26.9 1.6 %collective-permute-start.6 = (f32[2,16,8,128]{3,2,1,0:T(8,128)S(1)}, f32[2,16,8,128]{3,2,1,0:T(8,128)S(1)}, u32[]{:S(2)}, u32[]{:S(2)}) collective-permute-start(f32[2,16,8,128]{3,2,1,0:T(8,128)S(1)} %pad_maximum_fusion.3), channel_id=1, source_target_pairs={{0,4},{4,8},{8,12},{12,0},{1,5},{5,9},{9,13},{13,1},{2,6},{6,10},{... | collective-permute-start | bytes 393224 | tf_op jit(solution)/shard_map/ppermute | solution.py:975
  28.5 7.2 %lists.1 = (f32[16,128]{1,0:T(8,128)S(1)}, s32[16,128]{1,0:T(8,128)S(1)}, s32[256,128]{1,0:T(8,128)S(1)}, s32[8,256]{1,0:T(8,128)S(1)}, s32[16,128]{1,0:T(8,128)...) custom-call(s32[1]{0:T(128)} %bitcast.25.wafer_ref, s32[1]{0:T(128)} %bitcast.26.det_ref, ...), custom_call_target="tpu_custom_call" | custom-call | flops 1000000000 | bytes 50000000 | tf_op jit(solution)/shard_map/lists/pallas_call | solution.py:1018
  35.7 0.7 collective-permute-done.7
  36.4 0.1 collective-permute-start.9
  36.5 0.6 collective-permute-start.10
  37.1 1.3 %collective-permute-done.9.angle_other_ref = f32[2,4,16,8,128]{4,3,2,1,0:T(8,128)S(1)} collective-permute-done((f32[2,4,16,8,128]{4,3,2,1,0:T(8,128)S(1)}, f32[2,4,16,8,128]{4,3,2,1,0:T(8,128)S(1)}, u32[]{:S(2)}, u32[]{:S(2)}) %collective-permute-start.9) | collective-permute-done | bytes 524320 | tf_op jit(solution)/shard_map/ppermute | solution.py:984
  38.4 0.7 collective-permute-done.10.tod_other_ref
  39.2 34.9 %map_maker.1.column_ref = bf16[5,384,256]{2,1,0:T(8,128)(2,1)S(1)} custom-call(s32[1]{0:T(128)} %bitcast.25.wafer_ref, s32[1]{0:T(128)} %bitcast.26.det_ref, s32[1]{0:T(128)} %bitcast.27.rep_ref, s32[2]{0:T(128)S(1)} %get-tuple-element.59.size_ref, s32[2048]{0:T(1024)S(1)} %get-tuple-element.60.pair_ref, s32[2048]{0:T(1024)S(1)} %get-tuple-element.61.group_ref, ...), custom_call_target="tpu_custom_call" | custom-call | tf_op jit(solution)/shard_map/map_maker/pallas_call | solution.py:1056
  74.0 13.3 %write.1 = (f32[192,24576]{1,0:T(8,128)}, f32[192,24576]{1,0:T(8,128)}) custom-call(s32[8,256]{1,0:T(8,128)S(1)} %get-tuple-element.58.start_ref, bf16[5,384,256]{2,1,0:T(8,128)(2,1)S(1)} %map_maker.1.column_ref, s32[256,128]{1,0:T(8,128)S(1)} %get-tuple-element.71.place_ref), custom_call_target="tpu_custom_call" | custom-call | tf_op jit(solution)/shard_map/write/pallas_call | solution.py:1079
  (14 shorter events, 0.2 us)
Async XLA Ops:
  5.3 7.4 %collective-permute-start = (f32[16,8,128]{2,1,0:T(8,128)}, f32[16,8,128]{2,1,0:T(8,128)S(1)}, u32[]{:S(2)}, u32[]{:S(2)}) collective-permute-start(f32[16,8,128]{2,1,0:T(8,128)} %bitcast.59), channel_id=1, source_target_pairs={{0,2},{2,0},{1,3},{3,1},{4,6},{6,4},{5,7},{7,5},{8,10},{10,8},{9,1... | collective-permute-start | bytes 196616 | tf_op jit(solution)/shard_map/ppermute | solution.py:981
  8.1 6.4 %collective-permute-start.3 = (f32[20,8,128]{2,1,0:T(8,128)S(1)}, f32[20,8,128]{2,1,0:T(8,128)S(1)}, u32[]{:S(2)}, u32[]{:S(2)}) collective-permute-start(f32[20,8,128]{2,1,0:T(8,128)S(1)} %pad_maximum_fusion.5), channel_id=1, source_target_pairs={{0,12},{4,0},{8,4},{12,8},{1,13},{5,1},{9,5},{13,9},{2,14},{6,2},{... | collective-permute-start | bytes 245768 | tf_op jit(solution)/shard_map/ppermute | solution.py:975
  11.7 7.6 %collective-permute-start.2 = (f32[20,8,128]{2,1,0:T(8,128)S(1)}, f32[20,8,128]{2,1,0:T(8,128)S(1)}, u32[]{:S(2)}, u32[]{:S(2)}) collective-permute-start(f32[20,8,128]{2,1,0:T(8,128)S(1)} %pad_maximum_fusion.5), channel_id=1, source_target_pairs={{0,8},{4,12},{8,0},{12,4},{1,9},{5,13},{9,1},{13,5},{2,10},{6,14},... | collective-permute-start | bytes 245768 | tf_op jit(solution)/shard_map/ppermute | solution.py:975
  11.7 7.6 %collective-permute-start.1 = (f32[20,8,128]{2,1,0:T(8,128)S(1)}, f32[20,8,128]{2,1,0:T(8,128)S(1)}, u32[]{:S(2)}, u32[]{:S(2)}) collective-permute-start(f32[20,8,128]{2,1,0:T(8,128)S(1)} %pad_maximum_fusion.5), channel_id=1, source_target_pairs={{0,4},{4,8},{8,12},{12,0},{1,5},{5,9},{9,13},{13,1},{2,6},{6,10},{... | collective-permute-start | bytes 245768 | tf_op jit(solution)/shard_map/ppermute | solution.py:975
  19.4 4.3 %collective-permute-start.4 = (f32[4,4,8,128]{3,2,1,0:T(8,128)S(1)}, f32[4,4,8,128]{3,2,1,0:T(8,128)S(1)}, u32[]{:S(2)}, u32[]{:S(2)}) collective-permute-start(f32[4,4,8,128]{3,2,1,0:T(8,128)S(1)} %pad_maximum_fusion.6), channel_id=1, source_target_pairs={{0,2},{2,0},{1,3},{3,1},{4,6},{6,4},{5,7},{7,5},{8,10},{10,8},{9,1... | collective-permute-start | bytes 196616 | tf_op jit(solution)/shard_map/ppermute | solution.py:981
  23.8 12.6 %collective-permute-start.5 = (f32[4,16,8,128]{3,2,1,0:T(8,128)S(1)}, f32[4,16,8,128]{3,2,1,0:T(8,128)S(1)}, u32[]{:S(2)}, u32[]{:S(2)}) collective-permute-start(f32[4,16,8,128]{3,2,1,0:T(8,128)S(1)} %pad_maximum_fusion.2.angle_here_ref), channel_id=1, source_target_pairs={{0,2},{2,0},{1,3},{3,1},{4,6},{6,4},{5,7},{7,5},{8,10},{10,8},{9,1... | collective-permute-start | bytes 786440 | tf_op jit(solution)/shard_map/ppermute | solution.py:981
  24.4 11.3 %collective-permute-start.8 = (f32[2,16,8,128]{3,2,1,0:T(8,128)S(1)}, f32[2,16,8,128]{3,2,1,0:T(8,128)S(1)}, u32[]{:S(2)}, u32[]{:S(2)}) collective-permute-start(f32[2,16,8,128]{3,2,1,0:T(8,128)S(1)} %pad_maximum_fusion.3), channel_id=1, source_target_pairs={{0,12},{4,0},{8,4},{12,8},{1,13},{5,1},{9,5},{13,9},{2,14},{6,2},{... | collective-permute-start | bytes 393224 | tf_op jit(solution)/shard_map/ppermute | solution.py:975
  26.9 9.5 %collective-permute-start.7 = (f32[2,16,8,128]{3,2,1,0:T(8,128)S(1)}, f32[2,16,8,128]{3,2,1,0:T(8,128)S(1)}, u32[]{:S(2)}, u32[]{:S(2)}) collective-permute-start(f32[2,16,8,128]{3,2,1,0:T(8,128)S(1)} %pad_maximum_fusion.3), channel_id=1, source_target_pairs={{0,8},{4,12},{8,0},{12,4},{1,9},{5,13},{9,1},{13,5},{2,10},{6,14},... | collective-permute-start | bytes 393224 | tf_op jit(solution)/shard_map/ppermute | solution.py:975
  26.9 9.5 %collective-permute-start.6 = (f32[2,16,8,128]{3,2,1,0:T(8,128)S(1)}, f32[2,16,8,128]{3,2,1,0:T(8,128)S(1)}, u32[]{:S(2)}, u32[]{:S(2)}) collective-permute-start(f32[2,16,8,128]{3,2,1,0:T(8,128)S(1)} %pad_maximum_fusion.3), channel_id=1, source_target_pairs={{0,4},{4,8},{8,12},{12,0},{1,5},{5,9},{9,13},{13,1},{2,6},{6,10},{... | collective-permute-start | bytes 393224 | tf_op jit(solution)/shard_map/ppermute | solution.py:975
  36.4 2.0 %collective-permute-start.9 = (f32[2,4,16,8,128]{4,3,2,1,0:T(8,128)S(1)}, f32[2,4,16,8,128]{4,3,2,1,0:T(8,128)S(1)}, u32[]{:S(2)}, u32[]{:S(2)}) collective-permute-start(f32[2,4,16,8,128]{4,3,2,1,0:T(8,128)S(1)} %pad_maximum_fusion), channel_id=1, source_target_pairs={{0,1},{1,0},{2,3},{3,2},{4,5},{5,4},{6,7},{7,6},{8,9},{9,8},{10,11... | collective-permute-start | bytes 1572872 | tf_op jit(solution)/shard_map/ppermute | solution.py:984
  36.5 2.6 %collective-permute-start.10 = (f32[4,2,16,8,128]{4,3,2,1,0:T(8,128)S(1)}, f32[4,2,16,8,128]{4,3,2,1,0:T(8,128)S(1)}, u32[]{:S(2)}, u32[]{:S(2)}) collective-permute-start(f32[4,2,16,8,128]{4,3,2,1,0:T(8,128)S(1)} %pad_maximum_fusion.1.tod_here_ref), channel_id=1, source_target_pairs={{0,1},{1,0},{2,3},{3,2},{4,5},{5,4},{6,7},{7,6},{8,9},{9,8},{10,11... | collective-permute-start | bytes 1572872 | tf_op jit(solution)/shard_map/ppermute | solution.py:1052
